TPU v7x, 32 devices: a whole 2x2x4 slice. The times are simulated.
32 devices in a mesh: img: 8 (over z, x), rows: 4 (over y, core).
Axes of the slice: x: 2, y: 2, z: 4, core: 2. Of those that a mesh axis runs over, the one named last changes fastest.
Arguments:
- small_images: bfloat16 [32, 224, 768], P('img', 'rows'), may hold values from -6 to 6
- large_images: bfloat16 [64, 576, 768], P('img', 'rows'), may hold values from -6 to 6
- w_qkv: float32 [768, 2304], P(('img', 'rows')), may hold values from -0.21875 to 0.21875
- w_out: float32 [768, 768], P(('img', 'rows')), may hold values from -0.875 to 0.875
- w_up: float32 [768, 3072], P(('img', 'rows')), may hold values from -0.21875 to 0.21875
- w_down: float32 [3072, 768], P(('img', 'rows')), may hold values from -0.109375 to 0.109375
- gains: float32 [768, 4], P(('img', 'rows')), may hold values from 0.5 to 1.5
- biases: float32 [768, 6], P(('img', 'rows')), may hold values from -3 to 3
- up_bias: float32 [3072], P(('img', 'rows')), may hold values from -3 to 3
- small_table: float32 [12, 729], replicated, may hold values from -6 to 6
- large_table: float32 [12, 2209], replicated, may hold values from -6 to 6
- small_cotangent: bfloat16 [32, 224, 768], P('img', 'rows'), may hold values from -6 to 6
- large_cotangent: bfloat16 [64, 576, 768], P('img', 'rows'), may hold values from -6 to 6
Outputs:
- small_out: bfloat16 [32, 224, 768], P('img', 'rows')
- large_out: bfloat16 [64, 576, 768], P('img', 'rows')
- small_grad: bfloat16 [32, 224, 768], P('img', 'rows')
- large_grad: bfloat16 [64, 576, 768], P('img', 'rows')
- grad_w_qkv: float32 [768, 2304], P(('img', 'rows'))
- grad_w_out: float32 [768, 768], P(('img', 'rows'))
- grad_w_up: float32 [768, 3072], P(('img', 'rows'))
- grad_w_down: float32 [3072, 768], P(('img', 'rows'))
- grad_gains: float32 [768, 4], P(('img', 'rows'))
- grad_biases: float32 [768, 6], P(('img', 'rows'))
- grad_up_bias: float32 [3072], P(('img', 'rows'))
- grad_small_table: float32 [12, 729], replicated
- grad_large_table: float32 [12, 2209], replicated
All inputs are finite; a program needn't handle non-finite values.
Results may differ from a plain program's by a relative error of at most 0.015.
The roundings to bfloat16 on the way count: a program that leaves them out, or rounds other values in their place, can miss the bound.
Values may be sent and summed in bfloat16 or wider, within the bound.
A program may use at most 256 MiB of HBM per device.

v0:
```python
import jax
import jax.numpy as jnp
from jax import lax
from jax.sharding import PartitionSpec as P

H = 12
SIDE_S = 14
SIDE_L = 24


HIGH = lax.Precision.HIGHEST


def layer_norm(values, gain, shift):
    average = jnp.mean(values, -1, keepdims=True)
    centered = values - average
    variance = jnp.mean(centered * centered, -1, keepdims=True)
    return centered * lax.rsqrt(variance + 1e-06) * gain + shift


def offset_tables(query_pos, key_pos, side):
    span = 2 * side - 1
    query_rows = query_pos.reshape(-1, side)[:, 0] // side
    key_rows = key_pos.reshape(-1, side)[:, 0] // side
    row_gap = jnp.clip(query_rows[:, None] - key_rows[None, :], 1 - side, side - 1) + side - 1
    offsets = jnp.arange(span, dtype=jnp.int32)
    row_hot = (row_gap[None, :, :] == offsets[:, None, None]).astype(jnp.float32)
    columns = jnp.arange(side, dtype=jnp.int32)
    col_gap = columns[:, None] - columns[None, :] + side - 1
    col_hot = (col_gap[None, :, :] == offsets[:, None, None]).astype(jnp.float32)
    return (row_hot, col_hot)


def bias_block(table, hots, side):
    row_hot, col_hot = hots
    span = 2 * side - 1
    heads = table.shape[0]
    square = table.reshape(heads, span, span)
    inner = jnp.einsum(
        "hab,bij->haij", square, col_hot, precision=HIGH, preferred_element_type=jnp.float32
    )
    whole = jnp.einsum(
        "haij,axy->hxiyj", inner, row_hot, precision=HIGH, preferred_element_type=jnp.float32
    )
    return whole.reshape(heads, row_hot.shape[1] * side, row_hot.shape[2] * side)


def table_block_grad(per_pair, hots, side):
    row_hot, col_hot = hots
    span = 2 * side - 1
    heads = per_pair.shape[0]
    split = per_pair.reshape(heads, row_hot.shape[1], side, row_hot.shape[2], side)
    inner = jnp.einsum(
        "hxiyj,axy->haij", split, row_hot, precision=HIGH, preferred_element_type=jnp.float32
    )
    square = jnp.einsum(
        "haij,bij->hab", inner, col_hot, precision=HIGH, preferred_element_type=jnp.float32
    )
    return square.reshape(heads, span * span)


def score_block(queries, keys, table, side, query_pos, key_pos):
    hots = offset_tables(query_pos, key_pos, side)
    bias = bias_block(table, hots, side)
    raw = (
        jnp.einsum("nqhd,nkhd->nhqk", queries, keys, preferred_element_type=jnp.float32) * 0.125
        + bias[None]
    )
    keep = key_pos // side < side
    return (jnp.where(keep[None, None, None, :], raw, -1e30), hots)


def attend(queries, keys, values, table, side, query_pos):
    key_pos = jnp.arange(keys.shape[1], dtype=jnp.int32)
    scores, hots = score_block(queries, keys, table, side, query_pos, key_pos)
    top = jnp.max(scores, -1, keepdims=True)
    expo = jnp.exp(scores - top)
    total = jnp.sum(expo, -1, keepdims=True)
    probs = (expo / total).astype(jnp.bfloat16)
    attended = jnp.einsum("nhqk,nkhd->nqhd", probs, values, preferred_element_type=jnp.float32)
    return (attended.astype(jnp.bfloat16), top + jnp.log(total))


def pair_terms(queries, keys, values, table, side, query_pos, key_pos, log_total, d_att, row_dot):
    scores, hots = score_block(queries, keys, table, side, query_pos, key_pos)
    probs = jnp.exp(scores - log_total)
    d_probs = jnp.einsum("nqhd,nkhd->nhqk", d_att, values, preferred_element_type=jnp.float32)
    d_probs = lax.optimization_barrier(d_probs.astype(jnp.bfloat16)).astype(jnp.float32)
    row_dot = jnp.sum(probs * d_probs, -1, keepdims=True)
    d_low = (probs * (d_probs - row_dot)).astype(jnp.bfloat16)
    return (probs, d_low, hots, row_dot)


def query_grads(d_low, keys, hots, side):
    d_queries = (
        jnp.einsum("nhqk,nkhd->nqhd", d_low, keys, preferred_element_type=jnp.float32) * 0.125
    )
    per_pair = jnp.sum(lax.optimization_barrier(d_low).astype(jnp.float32), 0)
    return (d_queries, table_block_grad(per_pair, hots, side))


def key_grads(probs, d_low, queries, d_att):
    d_values = jnp.einsum(
        "nhqk,nqhd->nkhd", probs.astype(jnp.bfloat16), d_att, preferred_element_type=jnp.float32
    )
    d_keys = (
        jnp.einsum("nhqk,nqhd->nkhd", d_low, queries, preferred_element_type=jnp.float32) * 0.125
    )
    return (d_keys, d_values)


def on_device(
    small_images,
    large_images,
    w_qkv,
    w_out,
    w_up,
    w_down,
    gains,
    biases,
    up_bias,
    small_table,
    large_table,
    small_cotangent,
    large_cotangent,
):
    full = (
        lax.all_gather(w_qkv.astype(jnp.bfloat16), ("img", "rows"), axis=0, tiled=True),
        lax.all_gather(w_out.astype(jnp.bfloat16), ("img", "rows"), axis=0, tiled=True),
        lax.all_gather(w_up.astype(jnp.bfloat16), ("img", "rows"), axis=0, tiled=True),
        lax.all_gather(w_down.astype(jnp.bfloat16), ("img", "rows"), axis=0, tiled=True),
        lax.all_gather(gains.astype(jnp.bfloat16), ("img", "rows"), axis=0, tiled=True),
        lax.all_gather(biases.astype(jnp.bfloat16), ("img", "rows"), axis=0, tiled=True),
        lax.all_gather(up_bias.astype(jnp.bfloat16), ("img", "rows"), axis=0, tiled=True),
    )
    qkv_low, out_low, up_low, down_low = (full[0], full[1], full[2], full[3])
    gain_vec = full[4].astype(jnp.float32)
    bias_vec = full[5].astype(jnp.float32)
    up_vec = full[6].astype(jnp.float32)
    small_x, small_ct, large_x, large_ct = (
        small_images,
        small_cotangent,
        large_images,
        large_cotangent,
    )
    block_index = lax.axis_index("rows")
    small_count, small_local, width = small_x.shape
    large_count, large_local = (large_x.shape[0], large_x.shape[1])
    split_at = small_count * small_local
    heads = H
    small_qpos = block_index * small_local + jnp.arange(small_local, dtype=jnp.int32)
    large_qpos = block_index * large_local + jnp.arange(large_local, dtype=jnp.int32)
    tokens = jnp.concatenate([small_x.reshape(-1, width), large_x.reshape(-1, width)], 0).astype(
        jnp.float32
    )
    normed = layer_norm(tokens, gain_vec[:, 0], bias_vec[:, 0]).astype(jnp.bfloat16)
    merged_bias = jnp.concatenate(
        [bias_vec[:, 2], jnp.zeros((width,), jnp.float32), bias_vec[:, 3]]
    )
    merged = (jnp.dot(normed, qkv_low, preferred_element_type=jnp.float32) + merged_bias).astype(
        jnp.bfloat16
    )
    small_merged = merged[:split_at].reshape(small_count, small_local, 3 * width)
    large_merged = merged[split_at:].reshape(large_count, large_local, 3 * width)
    own_parts = (
        small_merged[:, :, width : 2 * width],
        small_merged[:, :, 2 * width :],
        large_merged[:, :, width : 2 * width],
        large_merged[:, :, 2 * width :],
    )
    gathered = (
        lax.all_gather(own_parts[0], "rows", axis=1, tiled=True),
        lax.all_gather(own_parts[1], "rows", axis=1, tiled=True),
        lax.all_gather(own_parts[2], "rows", axis=1, tiled=True),
        lax.all_gather(own_parts[3], "rows", axis=1, tiled=True),
    )
    small_q = small_merged[:, :, :width].reshape(small_count, small_local, heads, -1)
    large_q = large_merged[:, :, :width].reshape(large_count, large_local, heads, -1)
    head_size = small_q.shape[3]
    small_k = gathered[0].reshape(small_count, -1, heads, head_size)
    small_v = gathered[1].reshape(small_count, -1, heads, head_size)
    large_k = gathered[2].reshape(large_count, -1, heads, head_size)
    large_v = gathered[3].reshape(large_count, -1, heads, head_size)
    small_att, small_lse = attend(small_q, small_k, small_v, small_table, SIDE_S, small_qpos)
    large_att, large_lse = attend(large_q, large_k, large_v, large_table, SIDE_L, large_qpos)
    attended = jnp.concatenate([small_att.reshape(-1, width), large_att.reshape(-1, width)], 0)
    branch = jnp.dot(attended, out_low, preferred_element_type=jnp.float32) + bias_vec[:, 4]
    middle = tokens + gain_vec[:, 2] * branch
    normed_mid = layer_norm(middle, gain_vec[:, 1], bias_vec[:, 1]).astype(jnp.bfloat16)
    hidden = jnp.dot(normed_mid, up_low, preferred_element_type=jnp.float32) + up_vec
    active = jax.nn.gelu(hidden, approximate=False).astype(jnp.bfloat16)
    mlp_out = jnp.dot(active, down_low, preferred_element_type=jnp.float32) + bias_vec[:, 5]
    result = (middle + gain_vec[:, 3] * mlp_out).astype(jnp.bfloat16)
    valid = (small_qpos // SIDE_S < SIDE_S).astype(jnp.float32)
    small_dy = small_ct.astype(jnp.float32) * valid[None, :, None]
    d_result = jnp.concatenate(
        [small_dy.reshape(-1, width), large_ct.astype(jnp.float32).reshape(-1, width)], 0
    )
    d_mlp = (gain_vec[:, 3] * d_result).astype(jnp.bfloat16)
    grad_scale_two = jnp.sum(mlp_out * d_result, 0)
    grad_down_bias = jnp.sum(d_mlp.astype(jnp.float32), 0)
    grad_w_down = jnp.einsum("rf,rd->fd", active, d_mlp, preferred_element_type=jnp.float32)
    d_active = jnp.einsum("rd,fd->rf", d_mlp, down_low, preferred_element_type=jnp.float32)
    gelu_value, gelu_pull = jax.vjp(lambda inner: jax.nn.gelu(inner, approximate=False), hidden)
    d_hidden = gelu_pull(d_active)[0].astype(jnp.bfloat16)
    grad_up_bias = jnp.sum(d_hidden.astype(jnp.float32), 0)
    grad_w_up = jnp.einsum("rd,rf->df", normed_mid, d_hidden, preferred_element_type=jnp.float32)
    d_normed_mid = jnp.einsum("rf,df->rd", d_hidden, up_low, preferred_element_type=jnp.float32)
    norm_value, norm_pull = jax.vjp(layer_norm, middle, gain_vec[:, 1], bias_vec[:, 1])
    d_middle_part, grad_gain_two, grad_shift_two = norm_pull(d_normed_mid)
    d_middle = d_result + d_middle_part
    d_branch = (gain_vec[:, 2] * d_middle).astype(jnp.bfloat16)
    grad_scale_one = jnp.sum(branch * d_middle, 0)
    grad_out_bias = jnp.sum(d_branch.astype(jnp.float32), 0)
    grad_w_out = jnp.einsum("re,rd->ed", attended, d_branch, preferred_element_type=jnp.float32)
    d_attended = jnp.einsum(
        "rd,ed->re", d_branch, out_low, preferred_element_type=jnp.float32
    ).astype(jnp.bfloat16)
    small_d_att = d_attended[:split_at].reshape(small_q.shape)
    large_d_att = d_attended[split_at:].reshape(large_q.shape)
    small_kpos = jnp.arange(small_k.shape[1], dtype=jnp.int32)
    large_kpos = jnp.arange(large_k.shape[1], dtype=jnp.int32)
    small_probs, small_dlow, small_hots, small_dot = pair_terms(
        small_q,
        small_k,
        small_v,
        small_table,
        SIDE_S,
        small_qpos,
        small_kpos,
        small_lse,
        small_d_att,
        None,
    )
    large_probs, large_dlow, large_hots, large_dot = pair_terms(
        large_q,
        large_k,
        large_v,
        large_table,
        SIDE_L,
        large_qpos,
        large_kpos,
        large_lse,
        large_d_att,
        None,
    )
    small_dq, small_table_grad = query_grads(small_dlow, small_k, small_hots, SIDE_S)
    large_dq, large_table_grad = query_grads(large_dlow, large_k, large_hots, SIDE_L)
    small_dk, small_dv = key_grads(small_probs, small_dlow, small_q, small_d_att)
    large_dk, large_dv = key_grads(large_probs, large_dlow, large_q, large_d_att)
    partial_kv = (
        small_dk.reshape(small_count, -1, width),
        small_dv.reshape(small_count, -1, width),
        large_dk.reshape(large_count, -1, width),
        large_dv.reshape(large_count, -1, width),
    )
    owned = (
        lax.psum_scatter(
            partial_kv[0].astype(jnp.bfloat16), "rows", scatter_dimension=1, tiled=True
        ).astype(jnp.float32),
        lax.psum_scatter(
            partial_kv[1].astype(jnp.bfloat16), "rows", scatter_dimension=1, tiled=True
        ).astype(jnp.float32),
        lax.psum_scatter(
            partial_kv[2].astype(jnp.bfloat16), "rows", scatter_dimension=1, tiled=True
        ).astype(jnp.float32),
        lax.psum_scatter(
            partial_kv[3].astype(jnp.bfloat16), "rows", scatter_dimension=1, tiled=True
        ).astype(jnp.float32),
    )
    d_merged = jnp.concatenate(
        [
            jnp.concatenate(
                [
                    small_dq.reshape(-1, width),
                    owned[0].reshape(-1, width),
                    owned[1].reshape(-1, width),
                ],
                1,
            ),
            jnp.concatenate(
                [
                    large_dq.reshape(-1, width),
                    owned[2].reshape(-1, width),
                    owned[3].reshape(-1, width),
                ],
                1,
            ),
        ],
        0,
    ).astype(jnp.bfloat16)
    merged_sums = jnp.sum(d_merged.astype(jnp.float32), 0)
    grad_w_qkv = jnp.einsum("rd,re->de", normed, d_merged, preferred_element_type=jnp.float32)
    d_normed = jnp.einsum("re,de->rd", d_merged, qkv_low, preferred_element_type=jnp.float32)
    first_value, first_pull = jax.vjp(layer_norm, tokens, gain_vec[:, 0], bias_vec[:, 0])
    d_tokens_part, grad_gain_one, grad_shift_one = first_pull(d_normed)
    d_tokens = (d_middle + d_tokens_part).astype(jnp.bfloat16)
    small_out = result[:split_at].reshape(small_x.shape)
    large_out = result[split_at:].reshape(large_x.shape)
    small_grad = d_tokens[:split_at].reshape(small_x.shape)
    large_grad = d_tokens[split_at:].reshape(large_x.shape)
    grad_gains = jnp.stack([grad_gain_one, grad_gain_two, grad_scale_one, grad_scale_two], 1)
    grad_biases = jnp.stack(
        [
            grad_shift_one,
            grad_shift_two,
            merged_sums[:width],
            merged_sums[2 * width :],
            grad_out_bias,
            grad_down_bias,
        ],
        1,
    )
    table_sums = lax.psum((small_table_grad, large_table_grad), ("img", "rows"))
    shards = (
        lax.psum_scatter(grad_w_qkv, ("img", "rows"), scatter_dimension=0, tiled=True),
        lax.psum_scatter(grad_w_out, ("img", "rows"), scatter_dimension=0, tiled=True),
        lax.psum_scatter(grad_w_up, ("img", "rows"), scatter_dimension=0, tiled=True),
        lax.psum_scatter(grad_w_down, ("img", "rows"), scatter_dimension=0, tiled=True),
        lax.psum_scatter(grad_gains, ("img", "rows"), scatter_dimension=0, tiled=True),
        lax.psum_scatter(grad_biases, ("img", "rows"), scatter_dimension=0, tiled=True),
        lax.psum_scatter(grad_up_bias, ("img", "rows"), scatter_dimension=0, tiled=True),
    )
    return (
        small_out,
        large_out,
        small_grad,
        large_grad,
        shards[0],
        shards[1],
        shards[2],
        shards[3],
        shards[4],
        shards[5],
        shards[6],
        table_sums[0],
        table_sums[1],
    )


def solution(mesh):
    in_specs = (
        P("img", "rows", None),
        P("img", "rows", None),
        P(("img", "rows"), None),
        P(("img", "rows"), None),
        P(("img", "rows"), None),
        P(("img", "rows"), None),
        P(("img", "rows"), None),
        P(("img", "rows"), None),
        P(("img", "rows")),
        P(),
        P(),
        P("img", "rows", None),
        P("img", "rows", None),
    )
    out_specs = (
        P("img", "rows", None),
        P("img", "rows", None),
        P("img", "rows", None),
        P("img", "rows", None),
        P(("img", "rows"), None),
        P(("img", "rows"), None),
        P(("img", "rows"), None),
        P(("img", "rows"), None),
        P(("img", "rows"), None),
        P(("img", "rows"), None),
        P(("img", "rows")),
        P(),
        P(),
    )
    return jax.shard_map(
        on_device, mesh=mesh, in_specs=in_specs, out_specs=out_specs, check_vma=False
    )
```

profile of v0, /device:TPU:0, one launch (start us, length us, event | category | flops | bytes accessed | tf_op | source)
XLA Modules:
  0.0 1548.1 jit_solution(2514422830215124428)
XLA Ops:
  9.7 43.3 %all-gather = bf16[32,24,4]{1,2,0:T(4,128)(2,1)S(1)} all-gather(bf16[1,24,4]{1,2,0:T(4,128)(2,1)S(1)} %convert_bitcast_fusion.2), channel_id=1, replica_groups=mesh['img'=8,'rows'=4] {'img','rows'}, dimensions={0}, use_global_device_ids=true | all-gather | bytes 6336 | tf_op jit(solution)/shard_map/all_gather | solution.py:132
  54.0 36.9 %all-gather.1 = bf16[32,24,6]{1,2,0:T(8,128)(2,1)S(1)} all-gather(bf16[1,24,6]{1,2,0:T(8,128)(2,1)S(1)} %convert_bitcast_fusion.1), channel_id=1, replica_groups=mesh['img'=8,'rows'=4] {'img','rows'}, dimensions={0}, use_global_device_ids=true | all-gather | bytes 9504 | tf_op jit(solution)/shard_map/all_gather | solution.py:133
  95.6 8.2 fusion.15
  116.5 37.5 %all-reduce = bf16[3072]{0:T(1024)(128)(2,1)S(1)} all-reduce(bf16[3072]{0:T(1024)(128)(2,1)S(1)} %dynamic-update-slice), channel_id=1, replica_groups=mesh['img'=8,'rows'=4] {'img','rows'}, use_global_device_ids=true, to_apply=%add | all-reduce | flops 3072 | bytes 12288
  155.0 3.9 bitcast_convert_fusion
  159.7 6.1 convolution_bitcast_fusion.1
  165.9 2.7 copy.132
  168.6 6.0 add.263
  176.3 9.0 convolution_bitcast_fusion
  185.3 7.6 copy.137
  192.9 15.1 add.268
  210.5 2.7 copy.135
  222.5 3.2 fusion.46
  230.3 10.3 copy.136
  240.6 19.5 %fusion.107 = (f32[8,12,144]{2,1,0:T(8,128)}, f32[8,12,144,576]{3,2,1,0:T(8,128)}) fusion(f32[12,144,576]{2,1,0:T(8,128)} %add.268, bf16[8,144,12,64]{1,3,2,0:T(8,128)(2,1)S(1)} %bitcast.213, bf16[8,576,12,64]{1,3,2,0:T(8,128)(2,1)} %bitcast.199, pred[576]{0:T(1024)(128)(4,1)S(1)} %fusion.83), kind=kOutput, calls=%fused_computation.212 | convolution fusion | flops 1051052544 | bytes 44735040 | tf_op jit(solution)/shard_map/nqhd,nkhd->nhqk/dot_general | solution.py:66
  260.1 15.2 fusion.3
  275.4 10.2 copy.134
  285.6 18.4 %convert_bitcast_fusion = bf16[8,144,12,64]{1,3,2,0:T(8,128)(2,1)} fusion(bf16[8,576,12,64]{1,3,2,0:T(8,128)(2,1)} %bitcast.202, f32[8,12,144,576]{3,2,1,0:T(8,128)} %get-tuple-element.62, f32[8,12,144]{2,1,0:T(8,128)S(1)} %fusion.3, f32[8,12,144]{2,1,0:T(8,128)S(1)} %copy-done.24), kind=kOutput, calls=%fused_computation.80 | convolution fusion | flops 1043988480 | bytes 40808448 | tf_op jit(solution)/shard_map/nhqk,nkhd->nqhd/dot_general | solution.py:80
  304.1 5.8 copy.138
  309.9 5.9 reshape.464
  315.8 6.5 fusion.103
  325.5 49.0 %all-gather.23.cloned.1.call-done = bf16[768,3072]{1,0:T(8,128)(2,1)} async-done(((bf16[24,3072]{1,0:T(8,128)(2,1)}), bf16[768,3072]{1,0:T(8,128)(2,1)}) %all-gather.23.cloned.1.call-update) | async-done | bytes 4718608 | tf_op jit(solution)/shard_map/all_gather | solution.py:130
  374.5 48.9 %multiply_convert_fusion = (bf16[1376,3072]{1,0:T(8,128)(2,1)}, f32[1376,3072]{1,0:T(8,128)}, f32[1376,3072]{1,0:T(8,128)}) fusion(f32[3072]{0:T(1024)} %convert_element_type.201, bf16[768,3072]{1,0:T(8,128)(2,1)} %all-gather.23.cloned.1.call-done, f32[1376,768]{1,0:T(8,128)} %copy-done.10, f32[768]{0:T(1024)} %get-tuple-element.21, ...), kind=kOutput, calls=%fused_computation.19 | convolution fusion | flops 6777053184 | bytes 51245824 | tf_op jit(solution)/shard_map/dot_general | solution.py:190
  423.4 17.0 %all-gather.25.cloned.1.call-done = bf16[3072,768]{1,0:T(8,128)(2,1)} async-done(((bf16[96,768]{1,0:T(8,128)(2,1)}), bf16[3072,768]{1,0:T(8,128)(2,1)}) %all-gather.25.cloned.1.call-update) | async-done | bytes 4718608 | tf_op jit(solution)/shard_map/all_gather | solution.py:131
  440.4 13.9 multiply_reduce_fusion
  454.3 22.5 %convert_reduce_fusion.1 = (f32[3072]{0:T(1024)}, bf16[1376,3072]{1,0:T(8,128)(2,1)}) fusion(f32[1376,3072]{1,0:T(8,128)} %get-tuple-element.44, bf16[1376,768]{1,0:T(8,128)(2,1)} %get-tuple-element.53, bf16[3072,768]{1,0:T(8,128)(2,1)} %all-gather.25.cloned.1.call-done, f32[1376,3072]{1,0:T(8,128)} %get-tuple-element.66, f32[3072]{0:T(1024)} %convert_element_type.201), kind=kOutput, calls=%fused_computation.17 | convolution fusion | flops 6564639744 | bytes 49127424 | tf_op jit(solution)/shard_map/rd,fd->rf/dot_general | solution.py:203
  476.8 15.0 multiply_reduce_fusion.2
  493.5 2.7 convert_reduce_fusion.5
  500.9 3.2 convolution_convert_fusion.2
  504.1 3.7 copy.174
  520.0 4.6 reshape.517
  524.6 6.4 copy.149
  531.1 16.9 %fusion.16 = bf16[8,12,64,576]{3,2,1,0:T(8,128)(2,1)} fusion(bf16[8,144,12,64]{1,3,2,0:T(8,128)(2,1)S(1)} %copy.149, f32[8,12,144,576]{3,2,1,0:T(8,128)} %get-tuple-element.62, f32[8,12,144]{2,1,0:T(8,128)S(1)} %log_add_fusion), kind=kOutput, calls=%fused_computation.39 | convolution fusion | flops 1038680064 | bytes 40753152 | tf_op jit(solution)/shard_map/nhqk,nqhd->nkhd/dot_general | solution.py:103
  548.0 10.2 copy.153
  558.2 10.8 convolution_convert_fusion
  569.0 22.2 %fusion = f32[8,12,144]{2,1,0:T(8,128)S(1)} fusion(bf16[8,12,144,576]{3,2,1,0:T(8,128)(2,1)} %convolution_convert_fusion, f32[8,12,144,576]{3,2,1,0:T(8,128)} %get-tuple-element.62, f32[8,12,144]{2,1,0:T(8,128)S(1)} %log_add_fusion), kind=kLoop, calls=%fused_computation.2 | loop fusion | flops 31836672 | bytes 47886336 | tf_op jit(solution)/shard_map/reduce_sum | solution.py:89
  591.2 25.0 %fusion.2 = bf16[8,12,144,576]{3,2,1,0:T(8,128)(2,1)} fusion(bf16[8,12,144,576]{3,2,1,0:T(8,128)(2,1)} %convolution_convert_fusion, f32[8,12,144,576]{3,2,1,0:T(8,128)} %get-tuple-element.62, f32[8,12,144]{2,1,0:T(8,128)S(1)} %fusion, f32[8,12,144]{2,1,0:T(8,128)S(1)} %log_add_fusion), kind=kLoop, calls=%fused_computation.4 | loop fusion | flops 39813120 | bytes 63811584 | tf_op jit(solution)/shard_map/convert_element_type | solution.py:90
  616.2 9.5 multiply_convert_fusion.1
  625.7 10.3 copy.151
  644.3 4.8 reshape.480
  649.1 6.7 convolution_bitcast_fusion.2
  657.8 12.6 fusion.33
  670.5 3.7 copy.150
  674.2 4.9 reshape.475
  679.1 9.5 convert_reduce_fusion
  688.7 14.2 reshape.482
  702.9 23.6 %fusion.68 = f32[47,12,24,24,1]{0,3,2,4,1:T(8,128)} fusion(f32[12,6,24,24,24]{4,3,2,1,0:T(8,128)} %reshape.482, s32[6,24]{1,0:T(8,128)S(1)} %copy-done.34), kind=kOutput, calls=%fused_computation.128 | convolution fusion | flops 561371776 | bytes 5281344 | tf_op jit(solution)/shard_map/hxiyj,axy->haij/dot_general | solution.py:53
  731.0 3.9 copy.155
  734.8 3.9 copy.154
  738.7 18.1 %convert_reduce_fusion.2 = (f32[2304]{0:T(1024)S(1)}, bf16[1376,2304]{0,1:T(8,128)(2,1)S(1)}) fusion(bf16[1152,768]{0,1:T(8,128)(2,1)} %copy.155, bf16[1152,768]{0,1:T(8,128)(2,1)} %copy.154, bf16[1152,768]{0,1:T(8,128)(2,1)S(1)} %reshape.475, bf16[224,768]{0,1:T(8,128)(2,1)} %copy.147, bf16[224,768]{0,1:T(8,128)(2,1)} %copy.146, bf16[224,768]{0,1:T(8,128)(2,1)} %reshape.471), kind=kLoop, calls=%fused_computation.35 | loop fusion | flops 44381952 | bytes 12690432 | tf_op jit(solution)/shard_map/reduce_sum | solution.py:292
  758.5 6.3 fusion.100
  767.7 3.6 multiply_reduce_fusion.1
  773.4 5.7 fusion.48
  781.2 5.2 fusion.39
  786.5 14.3 fusion.98
  800.9 12.8 fusion.109
  814.7 11.7 fusion.94
  828.3 2.8 slice.147
  833.2 62.5 %all-reduce.10.cloned.1.call-done = (f32[768,4]{0,1:T(4,128)}, f32[768,6]{0,1:T(8,128)}, f32[3072]{0:T(1024)}, f32[12,729]{1,0:T(8,128)}) async-done(((f32[768,4]{0,1:T(4,128)}, f32[768,6]{0,1:T(8,128)}, f32[3072]{0:T(1024)}, f32[12,729]{1,0:T(8,128)}), (f32[768,4]{0,1:T(4,128)}, f32[768,6]{0,1:T(8,128)}, f32[3072]{0:T(1024)}, f32[12,729]{1,0:T(8,128)})) %all-reduce.10.cloned.1.call-update) | async-done | bytes 78016
  899.7 123.6 %all-reduce.8.cloned.1.call-done = f32[12,2209]{1,0:T(8,128)} async-done(((f32[12,2209]{1,0:T(8,128)}), f32[12,2209]{1,0:T(8,128)}) %all-reduce.8.cloned.1.call-update) | async-done | bytes 106048 | tf_op jit(solution)/shard_map/psum | solution.py:314
  1023.3 106.7 %reduce-scatter.21.cloned.1.call-done = f32[24,768]{1,0:T(8,128)} async-done(((f32[768,768]{1,0:T(8,128)}), f32[24,768]{1,0:T(8,128)}) %reduce-scatter.21.cloned.1.call-update) | async-done | bytes 73744 | tf_op jit(solution)/shard_map/reduce_scatter | solution.py:317
  1130.0 142.0 %reduce-scatter.23.cloned.1.call-done = f32[24,3072]{1,0:T(8,128)} async-done(((f32[768,3072]{1,0:T(8,128)}), f32[24,3072]{1,0:T(8,128)}) %reduce-scatter.23.cloned.1.call-update) | async-done | bytes 294928 | tf_op jit(solution)/shard_map/reduce_scatter | solution.py:318
  1271.9 140.7 %reduce-scatter.25.cloned.1.call-done = f32[96,768]{1,0:T(8,128)} async-done(((f32[3072,768]{1,0:T(8,128)}), f32[96,768]{1,0:T(8,128)}) %reduce-scatter.25.cloned.1.call-update) | async-done | bytes 294928 | tf_op jit(solution)/shard_map/reduce_scatter | solution.py:319
  1412.6 125.3 %reduce-scatter.19.cloned.1.call-done = f32[24,2304]{1,0:T(8,128)} async-done(((f32[768,2304]{1,0:T(8,128)}), f32[24,2304]{1,0:T(8,128)}) %reduce-scatter.19.cloned.1.call-update) | async-done | bytes 221200 | tf_op jit(solution)/shard_map/reduce_scatter | solution.py:316
  (308 shorter events, 97.4 us)
Async XLA Ops:
  7.2 86.6 %copy-start.2 = (bf16[8,144,768]{2,1,0:T(8,128)(2,1)S(1)}, bf16[8,144,768]{2,1,0:T(8,128)(2,1)}, u32[]{:S(2)}) copy-start(bf16[8,144,768]{2,1,0:T(8,128)(2,1)} %param.14) | copy-start | bytes 5308420
  7.2 88.4 %copy-start.18 = (bf16[4,56,768]{2,1,0:T(8,128)(2,1)S(1)}, bf16[4,56,768]{2,1,0:T(8,128)(2,1)}, u32[]{:S(2)}) copy-start(bf16[4,56,768]{2,1,0:T(8,128)(2,1)} %param.13) | copy-start | bytes 1032196
  7.2 88.4 %all-gather.11.cloned.1.call-start = ((), (), s32[]{:S(2)}) async-start(), calls=%async_computation.8 | async-start | bytes 3649536 | tf_op jit(solution)/shard_map/all_gather | solution.py:128
  9.0 204.2 %all-gather.15.cloned.1.call-start = ((), (), s32[]{:S(2)}) async-start(), calls=%async_computation.10 | async-start | bytes 1720320 | tf_op jit(solution)/shard_map/all_gather | solution.py:172
  93.7 10.1 copy-start.50
  93.7 10.1 copy-start.63
  93.7 222.0 %copy-start.57 = (f32[768]{0:T(1024)}, f32[768]{0:T(1024)S(1)}, u32[]{:S(2)}) copy-start(f32[768]{0:T(1024)S(1)} %get-tuple-element.22) | copy-start | bytes 9220
  93.8 222.0 %copy-start.59 = (f32[768]{0:T(1024)}, f32[768]{0:T(1024)S(1)}, u32[]{:S(2)}) copy-start(f32[768]{0:T(1024)S(1)} %get-tuple-element.71) | copy-start | bytes 9220
  93.8 10.1 copy-start.36
  95.5 8.3 copy-start.43
  95.6 8.3 copy-start.39
  107.6 112.4 %all-gather.13.cloned.1.call-start = ((), (), s32[]{:S(2)}) async-start(), calls=%async_computation.9 | async-start | bytes 1720320 | tf_op jit(solution)/shard_map/all_gather | solution.py:173
  108.3 122.0 %all-gather.19.cloned.1.call-start = ((), (), s32[]{:S(2)}) async-start(), calls=%async_computation.12 | async-start | bytes 8847360 | tf_op jit(solution)/shard_map/all_gather | solution.py:174
  113.1 41.5 %copy-start.49 = (f32[12,729]{1,0:T(8,128)S(1)}, f32[12,729]{1,0:T(8,128)}, u32[]{:S(2)}) copy-start(f32[12,729]{1,0:T(8,128)} %param.22) | copy-start | bytes 104980
  113.1 41.7 %copy-start.35 = (f32[12,2209]{1,0:T(8,128)S(1)}, f32[12,2209]{1,0:T(8,128)}, u32[]{:S(2)}) copy-start(f32[12,2209]{1,0:T(8,128)} %param.23) | copy-start | bytes 318100
  113.1 162.2 %all-gather.17.cloned.1.call-start = ((), (), s32[]{:S(2)}) async-start(), calls=%async_computation.11 | async-start | bytes 8847360 | tf_op jit(solution)/shard_map/all_gather | solution.py:175
  113.7 202.0 %all-gather.21.cloned.1.call-start = ((), (), s32[]{:S(2)}) async-start(), calls=%async_computation.13 | async-start | bytes 1216512 | tf_op jit(solution)/shard_map/all_gather | solution.py:129
  114.4 260.1 %all-gather.23.cloned.1.call-start = ((), (), s32[]{:S(2)}) async-start(), calls=%async_computation.14 | async-start | bytes 4866048 | tf_op jit(solution)/shard_map/all_gather | solution.py:130
  115.2 325.2 %all-gather.25.cloned.1.call-start = ((), (), s32[]{:S(2)}) async-start(), calls=%async_computation.15 | async-start | bytes 4866048 | tf_op jit(solution)/shard_map/all_gather | solution.py:131
  115.9 610.6 %reduce-scatter.29.cloned.1.call-start = ((), (), s32[]{:S(2)}) async-start(), calls=%async_computation.24 | async-start | bytes 1720320
  116.1 49.7 %copy-start.41 = (s32[14,14]{1,0:T(8,128)}, s32[14,14]{1,0:T(8,128)S(1)}, u32[]{:S(2)}) copy-start(s32[14,14]{1,0:T(8,128)S(1)} %subtract_add_fusion.1) | copy-start | bytes 2356
  116.2 58.5 %copy-start.38 = (s32[24,24]{1,0:T(8,128)}, s32[24,24]{1,0:T(8,128)S(1)}, u32[]{:S(2)}) copy-start(s32[24,24]{1,0:T(8,128)S(1)} %subtract_add_fusion) | copy-start | bytes 6916
  158.9 6.9 copy-start.54
  174.7 10.6 copy-start.33
  192.9 15.1 copy-start.30
  218.5 7.3 copy-start
  230.3 10.3 copy-start.5
  275.3 10.3 copy-start.27
  275.3 10.3 copy-start.24
  304.0 11.7 copy-start.3
  304.1 11.7 copy-start.29
  322.2 169.6 %copy-start.48 = (f32[1376]{0:T(1024)}, f32[1376]{0:T(1024)S(1)}, u32[]{:S(2)}) copy-start(f32[1376]{0:T(1024)S(1)} %broadcast_multiply_fusion) | copy-start | bytes 16516
  325.5 166.3 %copy-start.53 = (f32[1376]{0:T(1024)}, f32[1376]{0:T(1024)S(1)}, u32[]{:S(2)}) copy-start(f32[1376]{0:T(1024)S(1)} %fusion.82) | copy-start | bytes 16516
  374.5 65.9 %copy-start.12 = (f32[1152,768]{1,0:T(8,128)S(1)}, f32[1152,768]{1,0:T(8,128)}, u32[]{:S(2)}) copy-start(f32[1152,768]{1,0:T(8,128)} %bitcast_convert_fusion) | copy-start | bytes 10616836
  476.8 15.0 copy-start.46
  476.8 15.0 copy-start.11
  476.8 15.0 copy-start.56
  510.5 218.3 %reduce-scatter.27.cloned.1.call-start = ((), (), s32[]{:S(2)}) async-start(), calls=%async_computation.23 | async-start | bytes 1720320
  519.4 211.6 %reduce-scatter.17.cloned.1.call-start = ((), (), s32[]{:S(2)}) async-start(), calls=%async_computation.17 | async-start | bytes 8847360 | tf_op jit(solution)/shard_map/reduce_scatter | solution.py:267
  524.6 6.4 copy-start.25
  524.6 6.4 copy-start.28
  558.2 176.6 %reduce-scatter.15.cloned.1.call-start = ((), (), s32[]{:S(2)}) async-start(), calls=%async_computation.16 | async-start | bytes 8847360 | tf_op jit(solution)/shard_map/reduce_scatter | solution.py:264
  591.2 25.0 %copy-start.6 = (bf16[8,144,768]{1,2,0:T(8,128)(2,1)S(1)}, bf16[8,144,768]{1,2,0:T(8,128)(2,1)}, u32[]{:S(2)}) copy-start(bf16[8,144,768]{1,2,0:T(8,128)(2,1)} %copy.135) | copy-start | bytes 5308420
  636.1 259.6 %all-reduce.10.cloned.1.call-start = ((), (), s32[]{:S(2)}) async-start(), calls=%async_computation.25 | async-start | bytes 196608
  649.1 6.7 copy-start.42
  688.7 14.2 copy-start.34
  738.7 19.8 %copy-start.4 = (bf16[8,144,768]{2,1,0:T(8,128)(2,1)S(1)}, bf16[8,144,768]{2,1,0:T(8,128)(2,1)}, u32[]{:S(2)}) copy-start(bf16[8,144,768]{2,1,0:T(8,128)(2,1)} %param.14) | copy-start | bytes 5308420
  738.7 19.8 %copy-start.19 = (bf16[4,56,768]{2,1,0:T(8,128)(2,1)S(1)}, bf16[4,56,768]{2,1,0:T(8,128)(2,1)}, u32[]{:S(2)}) copy-start(bf16[4,56,768]{2,1,0:T(8,128)(2,1)} %param.13) | copy-start | bytes 1032196
  738.7 19.8 %copy-start.37 = (f32[1376]{0:T(1024)S(1)}, f32[1376]{0:T(1024)}, u32[]{:S(2)}) copy-start(f32[1376]{0:T(1024)} %copy-done.36) | copy-start | bytes 16516
  738.7 19.8 %copy-start.51 = (f32[768]{0:T(1024)S(1)}, f32[768]{0:T(1024)}, u32[]{:S(2)}) copy-start(f32[768]{0:T(1024)} %copy-done.50) | copy-start | bytes 9220
  738.7 19.8 %copy-start.69 = (bf16[768,2304]{1,0:T(8,128)(2,1)S(1)}, bf16[768,2304]{1,0:T(8,128)(2,1)}, u32[]{:S(2)}) copy-start(bf16[768,2304]{1,0:T(8,128)(2,1)} %all-gather.11.cloned.1.call-done) | copy-start | bytes 10616836
  756.8 8.1 copy-start.16
  758.5 9.2 slice-start.1
  758.5 9.2 slice-start.4
  758.5 7.0 copy-start.44
  758.5 7.0 copy-start.40
  758.5 9.1 slice-start.2
  758.5 9.1 slice-start.5
  771.3 9.9 copy-start.23
  773.3 249.9 %all-reduce.8.cloned.1.call-start = ((), (), s32[]{:S(2)}) async-start(), calls=%async_computation.22 | async-start | bytes 294912 | tf_op jit(solution)/shard_map/psum | solution.py:314
  780.9 349.1 %reduce-scatter.21.cloned.1.call-start = ((), (), s32[]{:S(2)}) async-start(), calls=%async_computation.19 | async-start | bytes 2433024 | tf_op jit(solution)/shard_map/reduce_scatter | solution.py:317
  786.5 485.5 %reduce-scatter.23.cloned.1.call-start = ((), (), s32[]{:S(2)}) async-start(), calls=%async_computation.20 | async-start | bytes 9732096 | tf_op jit(solution)/shard_map/reduce_scatter | solution.py:318
  800.9 611.8 %reduce-scatter.25.cloned.1.call-start = ((), (), s32[]{:S(2)}) async-start(), calls=%async_computation.21 | async-start | bytes 9732096 | tf_op jit(solution)/shard_map/reduce_scatter | solution.py:319
  813.8 724.2 %reduce-scatter.19.cloned.1.call-start = ((), (), s32[]{:S(2)}) async-start(), calls=%async_computation.18 | async-start | bytes 7299072 | tf_op jit(solution)/shard_map/reduce_scatter | solution.py:316
  (32 other events, 82.0 us)
Sparse Core Ops, SparseCore 0:
  11.5 62.9 all-gather.10
  107.7 16.3 all-gather.14
  126.2 18.9 all-gather.12
  147.3 50.8 all-gather.18
  200.1 50.8 all-gather.16
  254.3 54.0 all-gather.20
  311.9 62.5 all-gather.22
  378.0 62.3 all-gather.24
  510.6 25.7 reduce-scatter.28
  539.0 26.9 reduce-scatter.26
  568.5 63.6 reduce-scatter.16
  636.2 63.4 reduce-scatter.14
  773.5 122.2 all-reduce.9
  901.7 121.5 all-reduce.7
  1029.0 100.9 reduce-scatter.20
  1137.3 134.5 reduce-scatter.22
  1278.3 134.3 reduce-scatter.24
  1419.7 118.2 reduce-scatter.18
where the time goes:
time: 1560 us; the launch traced here: 1550 us
  waiting for transfers between devices  768 us (49%)
  matrix products  323 us (21%)
  local copies, waits for them, and re-layouts  202 us (13%)
  other arithmetic  120 us (8%)
  blocking collectives  118 us (8%)
  between operations  15.7 us (1%)
    reduce_scatter x1, waiting for transfers between devices, on_device(): lax.psum_scatter(grad_w_up, ('img', 'rows'), scatter_dimension=0, tiled=T...  142 us
    reduce_scatter x1, waiting for transfers between devices, on_device(): lax.psum_scatter(grad_w_down, ('img', 'rows'), scatter_dimension=0, tiled...  141 us
    reduce_scatter x1, waiting for transfers between devices, on_device(): lax.psum_scatter(grad_w_qkv, ('img', 'rows'), scatter_dimension=0, tiled=...  125 us
    psum x1, waiting for transfers between devices, on_device(): table_sums = lax.psum((small_table_grad, large_table_grad), ('img', 'rows'))  124 us
    reduce_scatter x1, waiting for transfers between devices, on_device(): lax.psum_scatter(grad_w_out, ('img', 'rows'), scatter_dimension=0, tiled=...  107 us
    unnamed x21, waiting for transfers between devices  64 us
    all_gather x1, waiting for transfers between devices, on_device(): lax.all_gather(w_up.astype(jnp.bfloat16), ('img', 'rows'), axis=0, tiled=...  49 us
    dot_general x1, matrix products, on_device(): jnp.dot(normed_mid, up_low, preferred_element_type=jnp.float32) + up_vec  48.9 us
  transfers between devices with their start and end apart: 18, of which 8 were waited for; matrix products, arithmetic and copies ran while one was open for 33% of the time, Pallas kernels for 0%

commit v1 on v0

v1 whole, which is shorter than its diff:
```python
import functools

import jax
import jax.numpy as jnp
from jax import lax
from jax.experimental import pallas as pl
from jax.experimental.pallas import tpu as pltpu
from jax.sharding import PartitionSpec as P

H = 12
SIDE_S = 14
SIDE_L = 24
LEN_S = 224
LEN_L = 576
WIDE_L = 1152
WIDE_S = 512

F32 = jnp.float32
BF = jnp.bfloat16
NN = (((1,), (0,)), ((), ()))
NT = (((1,), (1,)), ((), ()))
TN = (((0,), (0,)), ((), ()))
MESH = pl.DeviceIdType.MESH
ANY = pl.BlockSpec(memory_space=pl.ANY)
MIB = 1 << 20


def dot(left, right, dims):
    return lax.dot_general(left, right, dims, preferred_element_type=F32)


class Place:
    def __init__(self, img_size):
        self.img = lax.axis_index("img")
        self.row = lax.axis_index("rows")
        self.zs = img_size // 2
        self.z, self.x = self.img // 2, self.img % 2
        self.y, self.c = self.row // 2, self.row % 2

    def at(self, z=None, x=None, y=None, c=None):
        z = self.z if z is None else z
        x = self.x if x is None else x
        y = self.y if y is None else y
        c = self.c if c is None else c
        return (z * 2 + x, y * 2 + c)

    def z_other(self, step):
        return lax.rem(self.z + step, self.zs)

    def row_other(self, step):
        return lax.rem(self.row + step, 4)

    def partners(self):
        along_z = [self.at(z=self.z_other(s)) for s in range(1, self.zs)]
        in_rows = [(self.img, self.row_other(s)) for s in range(1, 4)]
        return along_z + in_rows + [self.at(x=1 - self.x)]


def greet(partners):
    barrier = pltpu.get_barrier_semaphore()
    for p in partners:
        pl.semaphore_signal(barrier, inc=1, device_id=p, device_id_type=MESH)
    pl.semaphore_wait(barrier, len(partners))


class Copies:
    def __init__(self, send, recv, local):
        self.send, self.recv, self.local = send, recv, local
        self.remotes, self.locals = 0, 0

    def remote(self, src, dst, device):
        i = self.remotes
        self.remotes += 1
        copy = pltpu.make_async_remote_copy(
            src_ref=src, dst_ref=dst, send_sem=self.send.at[i], recv_sem=self.recv.at[i],
            device_id=device, device_id_type=MESH,
        )
        copy.start()
        return copy

    def here(self, src, dst):
        i = self.locals
        self.locals += 1
        copy = pltpu.make_async_copy(src, dst, self.local.at[i])
        copy.start()
        return copy


def pipelined(units):
    depth = max(len(u) for u in units)
    for t in range(len(units) + depth - 1):
        for f in reversed(range(depth)):
            u = t - f
            if 0 <= u < len(units) and f < len(units[u]):
                units[u][f]()


def columns(start, size):
    return pl.ds(pl.multiple_of(start, 128), size)


class Gather:
    def __init__(self, place, copies, shard, full, both, low, chunks):
        self.p, self.copies = place, copies
        self.shard, self.full, self.both, self.low = shard, full, both, low
        self.k, self.cols = shard.shape
        self.half = self.cols // 2
        self.wide = self.half // chunks
        self.chunks = chunks
        self.state = [None] * chunks

    def exchange(self):
        p = self.p
        mine = pl.ds(pl.multiple_of(p.c * self.k, 8), self.k)
        self.kept = self.copies.here(self.shard.at[:, columns(p.c * self.half, self.half)], self.both.at[mine])
        self.swapped = self.copies.remote(
            self.shard.at[:, columns((1 - p.c) * self.half, self.half)], self.both.at[mine], p.at(c=1 - p.c)
        )

    def convert(self):
        self.kept.wait()
        self.swapped.wait_recv()
        self.low[...] = self.both[...].astype(BF)

    def along_z(self, u):
        if u == 0:
            self.convert()
        p = self.p
        src = self.low.at[:, pl.ds(u * self.wide, self.wide)]
        dst = self.full.at[p.z, p.x, p.y, :, self.part(u)]
        own = self.copies.here(src, dst)
        sent = [self.copies.remote(src, dst, p.at(z=p.z_other(s))) for s in range(1, p.zs)]
        self.state[u] = (own, sent, [])

    def part(self, u):
        return columns(self.p.c * self.half + u * self.wide, self.wide)

    def send(self, u, part, device):
        self.state[u][2].append(self.copies.remote(part, part, device))

    def along_y(self, u):
        p = self.p
        own, sent, _ = self.state[u]
        own.wait()
        for copy in sent:
            copy.wait_recv()
        self.send(u, self.full.at[:, p.x, p.y, :, self.part(u)], p.at(y=1 - p.y))

    def along_x(self, u):
        p = self.p
        self.state[u][2][-1].wait_recv()
        self.send(u, self.full.at[:, p.x, :, :, self.part(u)], p.at(x=1 - p.x))

    def along_c(self, u):
        p = self.p
        self.state[u][2][-1].wait_recv()
        self.send(u, self.full.at[:, :, :, :, self.part(u)], p.at(c=1 - p.c))

    def finish(self, u):
        own, sent, later = self.state[u]
        later[-1].wait_recv()
        for copy in sent + later:
            copy.wait_send()
        if u == 0:
            self.swapped.wait_send()

    def units(self):
        steps = (self.along_z, self.along_y, self.along_x, self.along_c, self.finish)
        return [[functools.partial(step, u) for step in steps] for u in range(self.chunks)]

    @staticmethod
    def scratch(shape):
        k, cols = shape
        return [pltpu.VMEM((2 * k, cols // 2), F32), pltpu.VMEM((2 * k, cols // 2), BF)]


class Spread:
    def __init__(self, place, copies, block, full):
        self.p, self.copies, self.block, self.full = place, copies, block, full
        self.sent = []

    def along_z(self):
        p = self.p
        dst = self.full.at[p.z, p.x, p.y, p.c]
        self.own = self.copies.here(self.block, dst)
        self.sent += [self.copies.remote(self.block, dst, p.at(z=p.z_other(s))) for s in range(1, p.zs)]

    def along_y(self):
        self.own.wait()
        for copy in self.sent:
            copy.wait_recv()
        p = self.p
        part = self.full.at[:, p.x, p.y, p.c]
        self.sent.append(self.copies.remote(part, part, p.at(y=1 - p.y)))

    def along_x(self):
        self.sent[-1].wait_recv()
        p = self.p
        part = self.full.at[:, p.x, :, p.c]
        self.sent.append(self.copies.remote(part, part, p.at(x=1 - p.x)))

    def along_c(self):
        self.sent[-1].wait_recv()
        p = self.p
        part = self.full.at[:, :, :, p.c]
        self.sent.append(self.copies.remote(part, part, p.at(c=1 - p.c)))

    def finish(self):
        self.sent[-1].wait_recv()
        for copy in self.sent:
            copy.wait_send()

    def units(self):
        return [[self.along_z, self.along_y, self.along_x, self.along_c, self.finish]]


class ToImages:
    def __init__(self, place, copies, blocks, whole):
        self.p, self.copies, self.blocks, self.whole = place, copies, blocks, whole
        self.n = blocks.shape[0] // 4

    def start(self):
        p, n = self.p, self.n
        dst = self.whole.at[:, p.row]
        self.sent = [
            self.copies.remote(self.blocks.at[pl.ds(p.row_other(s) * n, n)], dst, (p.img, p.row_other(s)))
            for s in (2, 3, 1)
        ]
        self.own = self.copies.here(self.blocks.at[pl.ds(p.row * n, n)], dst)

    def finish(self):
        self.own.wait()
        for copy in self.sent:
            copy.wait()


class ToBlocks(ToImages):
    def __init__(self, place, copies, whole, blocks):
        super().__init__(place, copies, blocks, whole)

    def start(self):
        p, n = self.p, self.n
        dst = self.blocks.at[pl.ds(p.row * n, n)]
        self.sent = [
            self.copies.remote(self.whole.at[:, p.row_other(s)], dst, (p.img, p.row_other(s))) for s in (2, 3, 1)
        ]
        self.own = self.copies.here(self.whole.at[:, p.row], dst)


class Scatter:
    def __init__(self, place, copies, grad, shard, own, from_c, from_x, from_y, from_z, summed, chunks):
        self.p, self.copies, self.grad, self.shard = place, copies, grad, shard
        self.own, self.from_c, self.from_x, self.from_y, self.from_z = own, from_c, from_x, from_y, from_z
        self.summed = summed
        self.k, self.cols = shard.shape
        self.half = self.cols // 2
        self.wide = self.half // chunks
        self.chunks = chunks
        self.sent = [[] for _ in range(chunks)]
        self.kept = [None] * chunks

    def send(self, u, src, dst, device):
        self.sent[u].append(self.copies.remote(src, dst, device))

    def along_c(self, u):
        p = self.p
        self.send(u, self.grad.at[:, :, :, :, columns((1 - p.c) * self.half + u * self.wide, self.wide)],
                  self.from_c.at[u], p.at(c=1 - p.c))
        self.kept[u] = self.copies.here(
            self.grad.at[:, :, :, :, columns(p.c * self.half + u * self.wide, self.wide)], self.own.at[u])

    def add(self, into, other):
        into[...] = (into[...].astype(F32) + other[...].astype(F32)).astype(BF)

    def along_x(self, u):
        p = self.p
        self.kept[u].wait()
        self.sent[u][-1].wait_recv()
        own, got = self.own.at[u], self.from_c.at[u]
        for z in range(p.zs):
            self.add(own.at[z, 1 - p.x], got.at[z, 1 - p.x])
        self.send(u, own.at[:, 1 - p.x], self.from_x.at[u], p.at(x=1 - p.x))
        for z in range(p.zs):
            self.add(own.at[z, p.x], got.at[z, p.x])

    def along_y(self, u):
        p = self.p
        self.sent[u][-1].wait_recv()
        own, got = self.own.at[u], self.from_x.at[u]
        for z in range(p.zs):
            self.add(own.at[z, p.x, 1 - p.y], got.at[z, 1 - p.y])
        self.send(u, own.at[:, p.x, 1 - p.y], self.from_y.at[u], p.at(y=1 - p.y))
        for z in range(p.zs):
            self.add(own.at[z, p.x, p.y], got.at[z, p.y])

    def along_z(self, u):
        p = self.p
        self.sent[u][-1].wait_recv()
        own, got = self.own.at[u], self.from_y.at[u]
        for z in range(p.zs):
            self.add(own.at[z, p.x, p.y], got.at[z])
        for s in range(1, p.zs):
            self.send(u, own.at[p.z_other(s), p.x, p.y], self.from_z.at[u, s - 1], p.at(z=p.z_other(s)))

    def finish(self, u):
        p = self.p
        for copy in self.sent[u][-(p.zs - 1):]:
            copy.wait_recv()
        total = self.own[u, p.z, p.x, p.y].astype(F32)
        for s in range(p.zs - 1):
            total += self.from_z[u, s].astype(F32)
        self.summed[:, pl.ds(u * self.wide, self.wide)] = total
        for copy in self.sent[u]:
            copy.wait_send()
        if u == self.chunks - 1:
            cols = columns(p.c * self.half, self.half)
            mine = pl.ds(pl.multiple_of(p.c * self.k, 8), self.k)
            theirs = pl.ds(pl.multiple_of((1 - p.c) * self.k, 8), self.k)
            self.last = [
                self.copies.remote(self.summed.at[theirs], self.shard.at[:, cols], p.at(c=1 - p.c)),
                self.copies.here(self.summed.at[mine], self.shard.at[:, cols]),
            ]

    def end(self):
        for copy in self.last:
            copy.wait()

    def units(self):
        steps = (self.along_c, self.along_x, self.along_y, self.along_z, self.finish)
        return [[functools.partial(step, u) for step in steps] for u in range(self.chunks)]

    @staticmethod
    def scratch(zs, k, cols, n):
        w = cols // 2 // n
        return [
            pltpu.VMEM((n, zs, 2, 2, 2 * k, w), BF),
            pltpu.VMEM((n, zs, 2, 2, 2 * k, w), BF),
            pltpu.VMEM((n, zs, 2, 2 * k, w), BF),
            pltpu.VMEM((n, zs, 2 * k, w), BF),
            pltpu.VMEM((n, zs - 1, 2 * k, w), BF),
            pltpu.VMEM((2 * k, cols // 2), F32),
        ]


class SmallSum:
    def __init__(self, place, copies, grad, shard, own, from_c, from_x, from_y, from_z):
        self.p, self.copies, self.grad, self.shard = place, copies, grad, shard
        self.own, self.from_c, self.from_x, self.from_y, self.from_z = own, from_c, from_x, from_y, from_z
        self.sent = []

    def along_c(self):
        p = self.p
        self.kept = self.copies.here(self.grad.at[:, :, :, p.c], self.own)
        self.sent.append(self.copies.remote(self.grad.at[:, :, :, 1 - p.c], self.from_c, p.at(c=1 - p.c)))

    def along_x(self):
        p = self.p
        self.kept.wait()
        self.sent[-1].wait_recv()
        self.own[...] = self.own[...] + self.from_c[...]
        self.sent.append(self.copies.remote(self.own.at[:, 1 - p.x], self.from_x, p.at(x=1 - p.x)))

    def along_y(self):
        p = self.p
        self.sent[-1].wait_recv()
        self.own[:, p.x] = self.own[:, p.x] + self.from_x[...]
        self.sent.append(self.copies.remote(self.own.at[:, p.x, 1 - p.y], self.from_y, p.at(y=1 - p.y)))

    def along_z(self):
        p = self.p
        self.sent[-1].wait_recv()
        self.own[:, p.x, p.y] = self.own[:, p.x, p.y] + self.from_y[...]
        self.sent += [
            self.copies.remote(self.own.at[p.z_other(s), p.x, p.y], self.from_z.at[s - 1], p.at(z=p.z_other(s)))
            for s in range(1, p.zs)
        ]

    def finish(self):
        p = self.p
        for copy in self.sent[-(p.zs - 1):]:
            copy.wait_recv()
        for copy in self.sent:
            copy.wait_send()
        total = self.own[p.z, p.x, p.y]
        for s in range(p.zs - 1):
            total += self.from_z[s]
        self.shard[...] = total

    def units(self):
        return [[self.along_c, self.along_x, self.along_y, self.along_z, self.finish]]

    @staticmethod
    def scratch(zs):
        return [
            pltpu.VMEM((zs, 2, 2, 8, 128), F32),
            pltpu.VMEM((zs, 2, 2, 8, 128), F32),
            pltpu.VMEM((zs, 2, 8, 128), F32),
            pltpu.VMEM((zs, 8, 128), F32),
            pltpu.VMEM((zs - 1, 8, 128), F32),
        ]


class TableSum:
    def __init__(self, place, copies, grad, result, got, work, from_z):
        self.p, self.copies, self.grad, self.result = place, copies, grad, result
        self.got, self.work, self.from_z = got, work, from_z
        self.sent = []

    def along_c(self):
        p = self.p
        self.kept = self.copies.here(self.grad.at[p.c], self.work)
        self.sent.append(self.copies.remote(self.grad.at[1 - p.c], self.got.at[0], p.at(c=1 - p.c)))

    def along_x(self):
        p = self.p
        self.kept.wait()
        self.sent[-1].wait_recv()
        self.work[...] = self.work[...] + self.got[0]
        self.sent.append(self.copies.remote(self.work, self.got.at[1], p.at(x=1 - p.x)))

    def along_y(self):
        p = self.p
        self.sent[-1].wait()
        self.work[...] = self.work[...] + self.got[1]
        self.sent.append(self.copies.remote(self.work, self.got.at[2], p.at(y=1 - p.y)))

    def along_z(self):
        p = self.p
        self.sent[-1].wait()
        self.from_z[p.z] = self.work[...] + self.got[2]
        mine = self.from_z.at[p.z]
        self.over_z = [self.copies.remote(mine, mine, p.at(z=p.z_other(s))) for s in range(1, p.zs)]

    def finish(self):
        p = self.p
        self.sent[0].wait_send()
        for copy in self.over_z:
            copy.wait()
        total = self.from_z[0]
        for z in range(1, p.zs):
            total += self.from_z[z]
        self.work[...] = total
        self.last = [
            self.copies.remote(self.work, self.result.at[p.c], p.at(c=1 - p.c)),
            self.copies.here(self.work, self.result.at[p.c]),
        ]

    def end(self):
        for copy in self.last:
            copy.wait()

    def units(self):
        return [[self.along_c, self.along_x, self.along_y, self.along_z, self.finish]]

    @staticmethod
    def scratch(zs, rows):
        return [pltpu.VMEM((3, rows, 128), F32), pltpu.VMEM((rows, 128), F32), pltpu.VMEM((zs, rows, 128), F32)]


def semaphores(remotes, locals_):
    return [
        pltpu.SemaphoreType.DMA((remotes,)),
        pltpu.SemaphoreType.DMA((remotes,)),
        pltpu.SemaphoreType.DMA((locals_,)),
    ]


def split_refs(refs, *sizes):
    parts, at = [], 0
    for size in sizes:
        parts.append(refs[at:at + size])
        at += size
    return parts + [refs[at:]]


def full_shape(img_size, shard):
    k, cols = shard.shape
    return (img_size // 2, 2, 2, 2 * k, cols)


def front(img_size, arrays, block, shards, chunks):
    na, nw = len(arrays), len(shards)
    zs = img_size // 2
    outs = [jax.ShapeDtypeStruct((a.shape[0] // 4, 4) + a.shape[1:], a.dtype) for a in arrays]
    outs += [jax.ShapeDtypeStruct((zs, 2, 2, 2, 8, 128), F32)]
    outs += [jax.ShapeDtypeStruct(full_shape(img_size, s), BF) for s in shards]

    def kernel(*refs):
        ins, blk, sh, whole, small, full, scr = split_refs(refs, na, 1, nw, na, 1, nw)
        p = Place(img_size)
        greet(p.partners())
        copies = Copies(*scr[-3:])
        gathers = [Gather(p, copies, sh[i], full[i], scr[2 * i], scr[2 * i + 1], chunks[i]) for i in range(nw)]
        moves = [ToImages(p, copies, a, b) for a, b in zip(ins, whole)]
        for g in gathers:
            g.exchange()
        for m in moves[:2]:
            m.start()
        units = Spread(p, copies, blk[0], small[0]).units()
        for i, g in enumerate(gathers):
            units += g.units()
        for m in moves[2:]:
            m.start()
        pipelined(units)
        for m in moves:
            m.finish()

    remotes = 3 * na + (zs + 2) + sum(1 + n * (zs + 2) for n in chunks)
    locals_ = na + 1 + sum(1 + n for n in chunks)
    return pl.pallas_call(
        kernel,
        out_shape=outs,
        in_specs=[ANY] * (na + 1 + nw),
        out_specs=[ANY] * len(outs),
        scratch_shapes=[s for w in shards for s in Gather.scratch(w.shape)] + semaphores(remotes, locals_),
        compiler_params=pltpu.CompilerParams(collective_id=0, has_side_effects=True, vmem_limit_bytes=40 * MIB),
        name="front",
    )(*arrays, block, *shards)


def finish(img_size, wholes, small, tables, grads, chunks):
    na, nw = len(wholes), len(grads)
    zs = img_size // 2
    outs = [jax.ShapeDtypeStruct((a.shape[0] * 4,) + a.shape[2:], a.dtype) for a in wholes]
    outs += [jax.ShapeDtypeStruct((8, 128), F32), jax.ShapeDtypeStruct(tables.shape, F32)]
    outs += [jax.ShapeDtypeStruct((g.shape[3] // 2, g.shape[4]), F32) for g in grads]

    def kernel(*refs):
        ins, sm, tb, gr, blocks, small_out, table_out, shard, scr = split_refs(refs, na, 1, 1, nw, na, 1, 1, nw)
        p = Place(img_size)
        greet(p.partners())
        copies = Copies(*scr[-3:])
        moves = [ToBlocks(p, copies, a, b) for a, b in zip(ins, blocks)]
        scatters = [Scatter(p, copies, gr[i], shard[i], *scr[6 * i:6 * i + 6], chunks[i]) for i in range(nw)]
        at = 6 * nw
        table = TableSum(p, copies, tb[0], table_out[0], *scr[at:at + 3])
        own = SmallSum(p, copies, sm[0], small_out[0], *scr[at + 3:at + 8])
        for m in moves:
            m.start()
        units = table.units() + own.units()
        for s in scatters:
            units += s.units()
        pipelined(units)
        for s in scatters:
            s.end()
        table.end()
        for m in moves:
            m.finish()

    remotes = 3 * na + (zs + 2) + (zs + 3) + sum(1 + n * (zs + 2) for n in chunks)
    locals_ = na + 1 + 2 + sum(1 + n for n in chunks)
    scratch = []
    for g, n in zip(grads, chunks):
        scratch += Scatter.scratch(zs, g.shape[3] // 2, g.shape[4], n)
    scratch += TableSum.scratch(zs, tables.shape[1]) + SmallSum.scratch(zs)
    vmem = pl.BlockSpec(memory_space=pltpu.VMEM)
    return pl.pallas_call(
        kernel,
        out_shape=outs,
        in_specs=[ANY] * (na + 2 + nw),
        out_specs=[ANY] * na + [vmem] + [ANY] * (1 + nw),
        scratch_shapes=scratch + semaphores(remotes, locals_),
        compiler_params=pltpu.CompilerParams(collective_id=1, has_side_effects=True, vmem_limit_bytes=56 * MIB),
        name="finish",
    )(*wholes, small, tables, *grads)


def table_rows(table, side, blocks, wide):
    span = 2 * side - 1
    square = table.reshape(H, span, span)
    square = jnp.concatenate([square] + [square[:, -1:]] * (blocks - span), 1)
    rows = []
    for turned in (square, square[:, ::-1, ::-1]):
        for part, pads in ((turned[:, :, :side], (0, 1)), (turned[:, :, side:], (1, 0))):
            part = jnp.pad(part, ((0, 0), pads, (0, side - part.shape[2])))
            flat = part.reshape(H, 1, (blocks + 1) * side)
            rows.append(jnp.roll(jnp.pad(flat, ((0, 0), (0, 0), (0, wide - flat.shape[2]))), 1 - side, 2))
    return jnp.concatenate(rows + [jnp.zeros((H, 4, wide), F32)], 1)


def table_sums(rows, side, blocks):
    span = 2 * side - 1
    rows = jnp.roll(rows, side - -(-side // 8) * 8, 2)
    parts = rows[:, :, :(blocks + 1) * side].reshape(H, 2, blocks + 1, side)
    square = jnp.concatenate([parts[:, 0, :blocks], parts[:, 1, 1:, :side - 1]], 2)
    square = jnp.concatenate([square[:, :span - 1], jnp.sum(square[:, span - 1:], 1, keepdims=True)], 1)
    return square.reshape(H, span * span)


def lower_offsets(side, rows, wide):
    lane = lax.rem(lax.broadcasted_iota(jnp.int32, (rows, wide), 1), side)
    return lane <= lax.broadcasted_iota(jnp.int32, (rows, wide), 0)


def spread_rows(rows_ref, h, first, side, rows, wide, lower):
    low = jnp.broadcast_to(rows_ref[h, first:first + 1, :], (rows, wide))
    high = jnp.broadcast_to(rows_ref[h, first + 1:first + 2, :], (rows, wide))
    return jnp.where(
        lower, pltpu.roll(low, 0, 1, stride=1, stride_axis=0), pltpu.roll(high, 0, 1, stride=1, stride_axis=0)
    )


def fill_bias(bias, h, spread, side, rows, first_offset):
    size = bias.shape[2]
    wide = spread.shape[1]
    window = -(-size // 128) * 128 + 128
    for r in range(rows):
        offset = (first_offset - r) * side
        base, rest = offset // 128 * 128, offset % 128
        part = spread[:, base:min(base + window, wide)]
        if part.shape[1] < window:
            part = jnp.concatenate([part, jnp.zeros((spread.shape[0], window - part.shape[1]), F32)], 1)
        if rest:
            part = pltpu.roll(part, window - rest, 1)
        bias[h, r * side:(r + 1) * side, :] = part[:side, :size]


def fold_bias(total, h, acc, side, rows, first_offset, lower, out_ref):
    size = total.shape[2]
    window = -(-size // 128) * 128 + 128
    height, wide = lower.shape
    acc[...] = jnp.zeros_like(acc)
    for r in range(rows):
        offset = (first_offset - r) * side
        base, rest = offset // 128 * 128, offset % 128
        part = total[h, r * side:(r + 1) * side, :]
        part = jnp.concatenate([part, jnp.zeros((side, window - size), F32)], 1)
        if rest:
            part = pltpu.roll(part, rest, 1)
        acc[:side, base:base + window] += part
    whole = acc[:, :wide]
    zero = jnp.zeros_like(whole)
    for at, part in enumerate((jnp.where(lower, whole, zero), jnp.where(lower, zero, whole))):
        turned = jnp.concatenate([part[j:j + 1] for j in reversed(range(height))], 0)
        out_ref[h, at:at + 1, :] = jnp.sum(pltpu.roll(turned, 0, 1, stride=1, stride_axis=0), 0, keepdims=True)


def head_part(full, mask, h):
    keep = mask if h == 0 else jnp.logical_not(mask)
    return jnp.where(keep, full, jnp.zeros_like(full))


def attend_kernel(large, small, q_ref, k_ref, v_ref, rows_l, rows_s, o_ref, bias_l, bias_s):
    mask = lax.broadcasted_iota(jnp.int32, (1, 128), 1) < 64
    lower_l = lower_offsets(SIDE_L, SIDE_L, WIDE_L)
    lower_s = lower_offsets(SIDE_S, 16, WIDE_S)
    for h in range(2):
        fill_bias(bias_l, h, spread_rows(rows_l, h, 2, SIDE_L, SIDE_L, WIDE_L, lower_l), SIDE_L, 24, 23)
        fill_bias(bias_s, h, spread_rows(rows_s, h, 2, SIDE_S, 16, WIDE_S, lower_s), SIDE_S, 16, 15)
    keep = lax.broadcasted_iota(jnp.int32, (1, LEN_S), 1) < SIDE_S * SIDE_S
    images = [(n * LEN_L, LEN_L, bias_l) for n in range(large)]
    images += [(large * LEN_L + n * LEN_S, LEN_S, bias_s) for n in range(small)]
    for at, size, bias in images:
        q, k, v = (ref[at:at + size, :] for ref in (q_ref, k_ref, v_ref))
        outs = []
        for h in range(2):
            s = dot(head_part(q, mask, h) * BF(0.125), k, NT) + bias[h]
            if size == LEN_S:
                s = jnp.where(keep, s, -1e30)
            e = jnp.exp(s - jnp.max(s, 1, keepdims=True))
            p = (e * (1.0 / jnp.sum(e, 1, keepdims=True))).astype(BF)
            outs.append(dot(p, v, NN))
        o_ref[at:at + size, :] = jnp.where(mask, outs[0], outs[1]).astype(BF)


def attend_back_kernel(large, small, q_ref, k_ref, v_ref, do_ref, rows_l, rows_s,
                       dq_ref, dk_ref, dv_ref, grad_l, grad_s, bias_l, bias_s, total_l, total_s, acc_l, acc_s):
    mask = lax.broadcasted_iota(jnp.int32, (1, 128), 1) < 64
    lower_l = lower_offsets(SIDE_L, SIDE_L, WIDE_L)
    lower_s = lower_offsets(SIDE_S, 16, WIDE_S)
    for h in range(2):
        fill_bias(bias_l, h, spread_rows(rows_l, h, 0, SIDE_L, SIDE_L, WIDE_L, lower_l), SIDE_L, 24, 23)
        fill_bias(bias_s, h, spread_rows(rows_s, h, 0, SIDE_S, 16, WIDE_S, lower_s), SIDE_S, 14, 13)
    keep = lax.broadcasted_iota(jnp.int32, (LEN_S, 1), 0) < SIDE_S * SIDE_S
    images = [(n * LEN_L, LEN_L, bias_l, total_l, n == 0) for n in range(large)]
    images += [(large * LEN_L + n * LEN_S, LEN_S, bias_s, total_s, n == 0) for n in range(small)]
    for at, size, bias, total, first in images:
        q, k, v, do = (ref[at:at + size, :] for ref in (q_ref, k_ref, v_ref, do_ref))
        got = []
        for h in range(2):
            s = dot(head_part(k, mask, h) * BF(0.125), q, NT) + bias[h]
            if size == LEN_S:
                s = jnp.where(keep, s, -1e30)
            e = jnp.exp(s - jnp.max(s, 0, keepdims=True))
            p = e * (1.0 / jnp.sum(e, 0, keepdims=True))
            dp = dot(head_part(v, mask, h), do, NT).astype(BF).astype(F32)
            pd = p * dp
            low = (pd - p * jnp.sum(pd, 0, keepdims=True)).astype(BF)
            got.append((dot(low, k, TN), dot(low, q, NN), dot(p.astype(BF), do, NN)))
            total[h] = low.astype(F32) if first else total[h] + low.astype(F32)
        for ref, a, b, scale in zip((dq_ref, dk_ref, dv_ref), got[0], got[1], (0.125, 0.125, 1.0)):
            ref[at:at + size, :] = (jnp.where(mask, a, b) * scale).astype(BF)
    for h in range(2):
        fold_bias(total_l, h, acc_l, SIDE_L, 24, 23, lower_l, grad_l)
        fold_bias(total_s, h, acc_s, SIDE_S, 14, 13, lower_s, grad_s)


def head_columns(rows, at):
    return pl.BlockSpec((rows, 128), lambda g: (0, g + at))


ROWS_L = pl.BlockSpec((2, 8, WIDE_L), lambda g: (g, 0, 0))
ROWS_S = pl.BlockSpec((2, 8, WIDE_S), lambda g: (g, 0, 0))


def attend(qkv, rows_l, rows_s, large, small):
    rows = qkv.shape[0]
    return pl.pallas_call(
        functools.partial(attend_kernel, large, small),
        grid=(H // 2,),
        out_shape=jax.ShapeDtypeStruct((rows, 64 * H), BF),
        in_specs=[head_columns(rows, H // 2 * i) for i in range(3)] + [ROWS_L, ROWS_S],
        out_specs=head_columns(rows, 0),
        scratch_shapes=[pltpu.VMEM((2, LEN_L, LEN_L), F32), pltpu.VMEM((2, LEN_S, LEN_S), F32)],
        compiler_params=pltpu.CompilerParams(vmem_limit_bytes=56 * MIB),
        name="attend",
    )(qkv, qkv, qkv, rows_l, rows_s)


def attend_back(qkv, d_att, rows_l, rows_s, large, small):
    rows = qkv.shape[0]
    flat = jax.ShapeDtypeStruct((rows, 64 * H), BF)
    return pl.pallas_call(
        functools.partial(attend_back_kernel, large, small),
        grid=(H // 2,),
        out_shape=[flat] * 3 + [jax.ShapeDtypeStruct((H, 8, WIDE_L), F32), jax.ShapeDtypeStruct((H, 8, WIDE_S), F32)],
        in_specs=[head_columns(rows, H // 2 * i) for i in range(3)] + [head_columns(rows, 0), ROWS_L, ROWS_S],
        out_specs=[head_columns(rows, 0)] * 3 + [ROWS_L, ROWS_S],
        scratch_shapes=[pltpu.VMEM((2, LEN_L, LEN_L), F32), pltpu.VMEM((2, LEN_S, LEN_S), F32)] * 2
        + [pltpu.VMEM((SIDE_L, WIDE_L + 128), F32), pltpu.VMEM((16, WIDE_S + 128), F32)],
        compiler_params=pltpu.CompilerParams(vmem_limit_bytes=56 * MIB),
        name="attend_back",
    )(qkv, qkv, qkv, d_att, rows_l, rows_s)


def layer_norm(values, gain, shift):
    average = jnp.mean(values, -1, keepdims=True)
    centered = values - average
    variance = jnp.mean(centered * centered, -1, keepdims=True)
    return centered * lax.rsqrt(variance + 1e-06) * gain + shift


def to_images(blocks):
    n = blocks.shape[0] // 4
    got = lax.all_to_all(blocks.reshape((4, n) + blocks.shape[1:]), "rows", 0, 0)
    return jnp.swapaxes(got, 0, 1)


def to_blocks(whole):
    got = lax.all_to_all(jnp.swapaxes(whole, 0, 1), "rows", 0, 0)
    return got.reshape((-1,) + got.shape[2:])


def front_plain(arrays, block, shards):
    axes = ("img", "rows")
    wholes = [to_images(a) for a in arrays]
    small = lax.all_gather(block, axes, axis=0)
    return wholes + [small] + [lax.all_gather(s.astype(BF), axes, axis=0, tiled=True) for s in shards]


def finish_plain(wholes, small, tables, grads):
    axes = ("img", "rows")
    blocks = [to_blocks(a) for a in wholes]
    own = lax.psum_scatter(small, axes, scatter_dimension=0, tiled=False)
    shards = [lax.psum_scatter(g.astype(F32), axes, scatter_dimension=0, tiled=True) for g in grads]
    return blocks + [own, lax.psum(tables, axes)] + shards


def on_device(img_size, small_images, large_images, w_qkv, w_out, w_up, w_down, gains, biases, up_bias,
              small_table, large_table, small_cotangent, large_cotangent):
    width = small_images.shape[2]
    shards = [w_qkv, w_out, w_up, w_down]
    own = gains.shape[0]
    own_up = up_bias.shape[0]
    own_len = 10 * own + own_up
    block = jnp.concatenate([gains.T.reshape(-1), biases.T.reshape(-1), up_bias])
    block = jnp.pad(block, (0, 1024 - own_len)).reshape(8, 128)
    arrays = [large_images, small_images, large_cotangent, small_cotangent]
    direct = own % 8 == 0
    if direct:
        got = front(img_size, arrays, block, shards, [3, 1, 3, 3])
    else:
        got = front_plain(arrays, block, shards)
    large_x, small_x, large_ct, small_ct = got[:4]
    vectors = got[4].reshape(-1, 1024).astype(BF).astype(F32)
    columns_ = jnp.swapaxes(vectors[:, :10 * own].reshape(-1, 10, own), 0, 1).reshape(10, width)
    up_vec = vectors[:, 10 * own:own_len].reshape(-1)
    gain_one, gain_two, scale_one, scale_two = (columns_[i] for i in range(4))
    shift_one, shift_two, q_bias, v_bias, out_bias, down_bias = (columns_[4 + i] for i in range(6))
    qkv_low, out_low, up_low, down_low = (g.reshape(-1, g.shape[-1]) for g in got[5:])

    large, small = large_x.shape[0], small_x.shape[0]
    split_at = large * LEN_L
    rows_l = table_rows(large_table, SIDE_L, 47, WIDE_L)
    rows_s = table_rows(small_table, SIDE_S, 29, WIDE_S)

    tokens = jnp.concatenate([large_x.reshape(-1, width), small_x.reshape(-1, width)], 0).astype(F32)
    normed = layer_norm(tokens, gain_one, shift_one).astype(BF)
    merged_bias = jnp.concatenate([q_bias, jnp.zeros((width,), F32), v_bias])
    merged = (jnp.dot(normed, qkv_low, preferred_element_type=F32) + merged_bias).astype(BF)
    attended = attend(merged, rows_l, rows_s, large, small)

    branch = jnp.dot(attended, out_low, preferred_element_type=F32) + out_bias
    middle = tokens + scale_one * branch
    normed_mid = layer_norm(middle, gain_two, shift_two).astype(BF)
    hidden = jnp.dot(normed_mid, up_low, preferred_element_type=F32) + up_vec
    active = jax.nn.gelu(hidden, approximate=False).astype(BF)
    mlp_out = jnp.dot(active, down_low, preferred_element_type=F32) + down_bias
    result = (middle + scale_two * mlp_out).astype(BF)

    valid = (jnp.arange(LEN_S) < SIDE_S * SIDE_S).astype(F32)
    small_dy = small_ct.reshape(small, LEN_S, width).astype(F32) * valid[None, :, None]
    d_result = jnp.concatenate([large_ct.reshape(-1, width).astype(F32), small_dy.reshape(-1, width)], 0)
    d_mlp = (scale_two * d_result).astype(BF)
    grad_scale_two = jnp.sum(mlp_out * d_result, 0)
    grad_down_bias = jnp.sum(d_mlp.astype(F32), 0)
    grad_w_down = jnp.einsum("rf,rd->fd", active, d_mlp, preferred_element_type=F32).astype(BF)
    d_active = jnp.einsum("rd,fd->rf", d_mlp, down_low, preferred_element_type=F32)
    _, gelu_pull = jax.vjp(lambda inner: jax.nn.gelu(inner, approximate=False), hidden)
    d_hidden = gelu_pull(d_active)[0].astype(BF)
    grad_up_bias = jnp.sum(d_hidden.astype(F32), 0)
    grad_w_up = jnp.einsum("rd,rf->df", normed_mid, d_hidden, preferred_element_type=F32).astype(BF)
    d_normed_mid = jnp.einsum("rf,df->rd", d_hidden, up_low, preferred_element_type=F32)
    _, norm_pull = jax.vjp(layer_norm, middle, gain_two, shift_two)
    d_middle_part, grad_gain_two, grad_shift_two = norm_pull(d_normed_mid)
    d_middle = d_result + d_middle_part
    d_branch = (scale_one * d_middle).astype(BF)
    grad_scale_one = jnp.sum(branch * d_middle, 0)
    grad_out_bias = jnp.sum(d_branch.astype(F32), 0)
    grad_w_out = jnp.einsum("re,rd->ed", attended, d_branch, preferred_element_type=F32).astype(BF)
    d_attended = jnp.einsum("rd,ed->re", d_branch, out_low, preferred_element_type=F32).astype(BF)

    dq, dk, dv, large_sums, small_sums = attend_back(merged, d_attended, rows_l, rows_s, large, small)
    d_merged = jnp.concatenate([dq, dk, dv], 1)
    grad_q_bias = jnp.sum(dq.astype(F32), 0)
    grad_v_bias = jnp.sum(dv.astype(F32), 0)
    grad_w_qkv = jnp.einsum("rd,re->de", normed, d_merged, preferred_element_type=F32).astype(BF)
    d_normed = jnp.einsum("re,de->rd", d_merged, qkv_low, preferred_element_type=F32)
    _, first_pull = jax.vjp(layer_norm, tokens, gain_one, shift_one)
    d_tokens_part, grad_gain_one, grad_shift_one = first_pull(d_normed)
    d_tokens = (d_middle + d_tokens_part).astype(BF)

    def whole(flat):
        return [flat[:split_at].reshape(large_x.shape), flat[split_at:].reshape(small_x.shape)]

    grad_columns = jnp.stack([
        grad_gain_one, grad_gain_two, grad_scale_one, grad_scale_two,
        grad_shift_one, grad_shift_two, grad_q_bias, grad_v_bias, grad_out_bias, grad_down_bias,
    ])
    devices = width // own
    packed = jnp.concatenate([
        jnp.swapaxes(grad_columns.reshape(10, devices, own), 0, 1).reshape(devices, 10 * own),
        grad_up_bias.reshape(devices, own_up),
        jnp.zeros((devices, 1024 - own_len), F32),
    ], 1)
    tables = jnp.concatenate([large_sums[:, :2].reshape(-1, 128), small_sums[:, :2].reshape(-1, 128)], 0)
    tables = jnp.pad(tables, ((0, 320 - tables.shape[0]), (0, 0))).reshape(2, 160, 128)
    wholes = whole(result) + whole(d_tokens)
    grads = [grad_w_qkv, grad_w_out, grad_w_up, grad_w_down]
    if direct:
        grads = [g.reshape(img_size // 2, 2, 2, 2 * s.shape[0], s.shape[1]) for g, s in zip(grads, shards)]
        done = finish(img_size, wholes, packed.reshape(img_size // 2, 2, 2, 2, 8, 128), tables, grads, [3, 1, 3, 3])
    else:
        done = finish_plain(wholes, packed, tables, grads)
    large_out, small_out, large_grad, small_grad, own_sums, table_total = done[:6]
    own_sums = own_sums.reshape(-1)
    own_columns = own_sums[:10 * own].reshape(10, own).T
    table_total = table_total.reshape(320, 128)
    count_l = H * 2 * WIDE_L // 128
    count_s = H * 2 * WIDE_S // 128
    grad_large_table = table_sums(table_total[:count_l].reshape(H, 2, WIDE_L), SIDE_L, 47)
    grad_small_table = table_sums(table_total[count_l:count_l + count_s].reshape(H, 2, WIDE_S), SIDE_S, 29)
    return (
        small_out, large_out, small_grad, large_grad, *done[6:],
        own_columns[:, :4], own_columns[:, 4:], own_sums[10 * own:own_len],
        grad_small_table, grad_large_table,
    )


def solution(mesh):
    images = P("img", "rows", None)
    matrix = P(("img", "rows"), None)
    vector = P(("img", "rows"))
    in_specs = (images, images) + (matrix,) * 6 + (vector, P(), P(), images, images)
    out_specs = (images,) * 4 + (matrix,) * 6 + (vector, P(), P())
    return jax.shard_map(
        functools.partial(on_device, mesh.shape["img"]),
        mesh=mesh, in_specs=in_specs, out_specs=out_specs, check_vma=False,
    )
```

time: 1560 us -> 637 us (0.41)
  waiting for transfers between devices: 768 us -> 0 us
  Pallas kernels: 0 us -> 372 us
  matrix products: 323 us -> 163 us
  local copies, waits for them, and re-layouts: 202 us -> 67.1 us
  blocking collectives: 118 us -> 0 us
  other arithmetic: 120 us -> 24.9 us
    reduce_scatter x6 -> x0, waiting for transfers between devices: 515 us -> none  [the longest x1 142 us: on_device(): lax.psum_scatter(grad_w_up, ('img', 'rows'), scatter_dimension=0, tiled=T...]
    pallas_call x0 -> x4, Pallas kernels: none -> 372 us  [the longest x1 145 us: finish(): pl.pallas_call(kernel, out_shape=outs, in_specs=[ANY] * (na + 2 + nw), ou...]
    dot_general x32 -> x12, matrix products: 323 us -> 163 us  [the longest x1 48.5 us: on_device(): hidden = jnp.dot(normed_mid, up_low, preferred_element_type=F32) + up_vec]
    psum x1 -> x0, waiting for transfers between devices: 124 us -> none  [on_device(): table_sums = lax.psum((small_table_grad, large_table_grad), ('img', 'rows'))]
    all_gather x2 -> x0, blocking collectives: 80.2 us -> none  [the longest x1 43.3 us: on_device(): lax.all_gather(gains.astype(jnp.bfloat16), ('img', 'rows'), axis=0, tiled...]
    all_gather x8 -> x0, waiting for transfers between devices: 66 us -> none  [the longest x1 49 us: on_device(): lax.all_gather(w_up.astype(jnp.bfloat16), ('img', 'rows'), axis=0, tiled=...]
    unnamed x21 -> x0, waiting for transfers between devices: 64 us -> none
    reduce_sum x8 -> x4, other arithmetic: 69.7 us -> 7.15 us  [the longest x1 2.93 us: on_device(): grad_out_bias = jnp.sum(d_branch.astype(F32), 0)]
  transfers between devices with their start and end apart: 18 -> 0, of which waited for: 8 -> 0; matrix products, arithmetic and copies ran while one was open for 33% -> 0% of each run, Pallas kernels for 0% -> 0%
where the time goes in v1:
time: 637 us; the launch traced here: 628 us
  Pallas kernels  372 us (58%)
  matrix products  163 us (26%)
  local copies, waits for them, and re-layouts  67.1 us (11%)
  other arithmetic  24.9 us (4%)
    pallas_call x1, Pallas kernels, finish(): pl.pallas_call(kernel, out_shape=outs, in_specs=[ANY] * (na + 2 + nw), ou...  145 us
    pallas_call x1, Pallas kernels, front(): pl.pallas_call(kernel, out_shape=outs, in_specs=[ANY] * (na + 1 + nw), ou...  144 us
    pallas_call x1, Pallas kernels, attend_back(): pl.pallas_call(functools.partial(attend_back_kernel, large, small), grid=...  51.3 us
    dot_general x1, matrix products, on_device(): hidden = jnp.dot(normed_mid, up_low, preferred_element_type=F32) + up_vec  48.5 us
    pallas_call x1, Pallas kernels, attend(): pl.pallas_call(functools.partial(attend_kernel, large, small), grid=(H //...  30.6 us
    unnamed x146, local copies, waits for them, and re-layouts  28.9 us
    dot_general x1, matrix products, on_device(): jnp.einsum('rd,fd->rf', d_mlp, down_low, preferred_element_type=F32)  24.1 us
    dot_general x1, matrix products, on_device(): mlp_out = jnp.dot(active, down_low, preferred_element_type=F32) + down_bias  14.7 us

profile of v1, /device:TPU:0, one launch (start us, length us, event | category | flops | bytes accessed | tf_op | source)
XLA Modules:
  0.0 628.3 jit_solution(8605043919522997090)
XLA Ops:
  0.6 0.8 reshape.290
  1.4 0.8 reshape.289
  2.9 1.5 copy-done.4
  4.4 1.5 copy-done.5
  5.9 1.0 copy-done.8
  6.8 1.0 copy-done.9
  7.8 1.0 copy-done.10
  8.8 1.0 copy-done.11
  9.7 0.9 copy-done.12
  10.7 0.9 copy-done.13
  11.6 144.2 %front.1 = (bf16[2,4,144,768]{3,2,1,0:T(8,128)(2,1)S(1)}, bf16[1,4,56,768]{3,2,1,0:T(8,128)(2,1)S(1)}, bf16[2,4,144,768]{3,2,1,0:T(8,128)(2,1)S(1)}, bf16[1,4,56...) custom-call(bf16[8,144,768]{2,1,0:T(8,128)(2,1)S(1)} %copy-done.4, ...), custom_call_target="tpu_custom_call" | custom-call | tf_op jit(solution)/shard_map/front/pallas_call | solution.py:510
  155.8 1.2 copy-done.6
  157.0 1.8 copy-done.14
  159.1 0.8 fusion.16
  161.9 10.1 %fusion.6.q_ref.k_ref.v_ref = bf16[1376,2304]{1,0:T(8,128)(2,1)} fusion(bf16[768,2304]{1,0:T(8,128)(2,1)} %bitcast.86, f32[2304]{0:T(1024)S(1)} %pad_maximum_fusion.14, f32[768]{0:T(1024)S(1)} %add.121, f32[768]{0:T(1024)S(1)} %mul.206, f32[1376]{0:T(1024)S(1)} %fusion.19, f32[1376]{0:T(1024)S(1)} %broadcast_multiply_fusion.1, ...), kind=kOutput, calls=%fused_computation.19 | convolution fusion | flops 4885438464 | bytes 12019456 | tf_op jit(solution)/shard_map/dot_general | solution.py:800
  174.8 0.9 concatenate.82.rows_s
  175.7 1.1 reshape.296
  176.8 0.8 fusion.31
  178.1 0.8 slice.280
  179.8 0.9 pad_maximum_fusion.7
  180.8 1.0 pad.50
  182.8 1.1 concatenate.76.rows_l
  184.0 30.6 %attend.1 = bf16[1376,768]{1,0:T(8,128)(2,1)} custom-call(bf16[1376,2304]{1,0:T(8,128)(2,1)} %fusion.6.q_ref.k_ref.v_ref, bf16[1376,2304]{1,0:T(8,128)(2,1)} %fusion.6.q_ref.k_ref.v_ref, bf16[1376,2304]{1,0:T(8,128)(2,1)} %fusion.6.q_ref.k_ref.v_ref, f32[12,8,1152]{2,1,0:T(8,128)} %concatenate.76.rows_l, f32[12,8,512]{2,1,0:T(8,128)} %concatenate.82.rows_s), custom_call_target="tpu_custom_call" | custom-call | tf_op jit(solution)/shard_map/attend/pallas_call | solution.py:708
  214.9 6.0 fusion.29
  220.9 2.0 copy-done.17
  224.1 48.5 %multiply_convert_fusion = (bf16[1376,3072]{1,0:T(8,128)(2,1)}, f32[1376,3072]{1,0:T(8,128)}, f32[1376,3072]{1,0:T(8,128)}) fusion(f32[3072]{0:T(1024)S(1)} %add.134, bf16[768,3072]{1,0:T(8,128)(2,1)} %bitcast.116, f32[1376,768]{1,0:T(8,128)} %copy-done.17, f32[768]{0:T(1024)S(1)} %add.131, f32[768]{0:T(1024)S(1)} %mul.215, f32[1376]{0:T(1024)S(1)} %fusion.20, ...), kind=kOutput, calls=%fused_computation.4 | convolution fusion | flops 6777053184 | bytes 51245824 | tf_op jit(solution)/shard_map/dot_general | solution.py:806
  273.5 14.7 %multiply_reduce_fusion = (f32[768]{0:T(1024)S(1)}, bf16[1376,768]{1,0:T(8,128)(2,1)}, f32[768]{0:T(1024)S(1)}, bf16[1376,768]{1,0:T(8,128)(2,1)S(1)}) fusion(f32[224,768]{1,0:T(8,128)S(1)} %convert_multiply_fusion, f32[1152,768]{1,0:T(8,128)S(1)} %bitcast_convert_fusion, f32[768]{0:T(1024)S(1)} %add.137, f32[1376,768]{1,0:T(8,128)} %copy-done.17, ...), kind=kOutput, calls=%fused_computation.44 | convolution fusion | flops 6504404992 | bytes 25866240 | tf_op jit(solution)/shard_map/dot_general | solution.py:808
  288.2 9.5 %convolution_convert_fusion = bf16[3072,768]{1,0:T(8,128)(2,1)} fusion(bf16[1376,3072]{1,0:T(8,128)(2,1)S(1)} %bitcast.121, bf16[1376,768]{1,0:T(8,128)(2,1)S(1)} %get-tuple-element.82), kind=kOutput, calls=%fused_computation.29 | convolution fusion | flops 6495141888 | bytes 15286272 | tf_op jit(solution)/shard_map/rf,rd->fd/dot_general | solution.py:817
  297.7 24.1 %convert_reduce_fusion = (f32[3072]{0:T(1024)S(1)}, bf16[1376,3072]{1,0:T(8,128)(2,1)}) fusion(f32[1376,3072]{1,0:T(8,128)} %get-tuple-element.76, bf16[1376,768]{1,0:T(8,128)(2,1)} %copy-done.56, bf16[3072,768]{1,0:T(8,128)(2,1)} %bitcast.119, f32[1376,3072]{1,0:T(8,128)} %get-tuple-element.104, f32[3072]{0:T(1024)S(1)} %add.134), kind=kOutput, calls=%fused_computation.2 | convolution fusion | flops 6564639744 | bytes 49127424 | tf_op jit(solution)/shard_map/rd,fd->rf/dot_general | solution.py:818
  321.8 14.3 %convolution_convert_fusion.2 = bf16[768,3072]{1,0:T(8,128)(2,1)} fusion(bf16[1376,3072]{1,0:T(8,128)(2,1)} %get-tuple-element.108, f32[1376,768]{1,0:T(8,128)} %copy-done.17, f32[768]{0:T(1024)S(1)} %add.131, f32[768]{0:T(1024)S(1)} %mul.215, f32[1376]{0:T(1024)S(1)} %fusion.20, f32[1376]{0:T(1024)S(1)} %broadcast_multiply_fusion), kind=kOutput, calls=%fused_computation.31 | convolution fusion | flops 6500425728 | bytes 17416960 | tf_op jit(solution)/shard_map/rd,rf->df/dot_general | solution.py:822
  336.0 11.6 %multiply_reduce_fusion.2 = (f32[768]{0:T(1024)S(1)}, f32[1376]{0:T(1024)S(1)}, f32[768]{0:T(1024)S(1)}, f32[1376,768]{1,0:T(8,128)S(1)}) fusion(f32[1376,768]{1,0:T(8,128)} %copy-done.17, f32[1376]{0:T(1024)S(1)} %fusion.20, f32[1376]{0:T(1024)S(1)} %broadcast_multiply_fusion, f32[768]{0:T(1024)S(1)} %mul.215, bf16[1376,3072]{1,0:T(8,128)(2,1)S(1)} %copy-done.55, ...), kind=kOutput, calls=%fused_computation.46 | convolution fusion | flops 6501233664 | bytes 21652608 | tf_op jit(solution)/shard_map/rf,df->rd/dot_general | solution.py:823
  347.7 1.5 fusion.27
  349.7 2.9 convert_reduce_fusion.3
  352.7 3.2 convolution_convert_fusion.3.do_ref
  355.9 51.3 %attend_back.1 = (bf16[1376,768]{1,0:T(8,128)(2,1)}, bf16[1376,768]{1,0:T(8,128)(2,1)}, bf16[1376,768]{1,0:T(8,128)(2,1)}, f32[12,8,1152]{2,1,0:T(8,128)}, f32[12,8,512]{2,1,0:T(8,128)}) custom-call(bf16[1376,2304]{1,0:T(8,128)(2,1)} %fusion.6.q_ref.k_ref.v_ref, bf16[1376,2304]{1,0:T(8,128)(2,1)} %fusion.6.q_ref.k_ref.v_ref, ...), custom_call_target="tpu_custom_call" | custom-call | tf_op jit(solution)/shard_map/attend_back/pallas_call | solution.py:723
  407.2 1.9 constant_dynamic-update-slice_fusion.2
  410.2 0.9 copy-done.1
  411.1 7.9 %convolution_convert_fusion.1 = bf16[768,2304]{1,0:T(8,128)(2,1)} fusion(bf16[1376,2304]{1,0:T(8,128)(2,1)S(1)} %constant_dynamic-update-slice_fusion, f32[768]{0:T(1024)S(1)} %copy-done.54, f32[768]{0:T(1024)S(1)} %copy-done.48, f32[1376]{0:T(1024)S(1)} %copy-done.36, f32[1376]{0:T(1024)S(1)} %copy-done.34, bf16[224,768]{1,0:T(8,128)(2,1)S(1)} %bitcast.82, ...), kind=kOutput, calls=%fused_computation.30 | convolution fusion | flops 4880867328 | bytes 12010240 | tf_op jit(solution)/shard_map/rd,re->de/dot_general | solution.py:837
  419.0 3.1 convolution_convert_fusion.4
  422.1 1.0 slice.252
  423.2 0.9 slice.253
  424.9 9.7 %fusion.26 = (f32[768]{0:T(1024)S(1)}, f32[1376]{0:T(1024)S(1)}, f32[1376,768]{1,0:T(8,128)S(1)}) fusion(f32[768]{0:T(1024)S(1)} %copy-done.48, f32[1376]{0:T(1024)S(1)} %copy-done.34, bf16[224,768]{1,0:T(8,128)(2,1)S(1)} %bitcast.83, bf16[1152,768]{1,0:T(8,128)(2,1)S(1)} %bitcast.75, bf16[1376,2304]{1,0:T(8,128)(2,1)} %copy-done.28, ...), kind=kOutput, calls=%fused_computation.118 | convolution fusion | flops 4879095296 | bytes 16237312 | tf_op jit(solution)/shard_map/re,de->rd/dot_general | solution.py:838
  434.6 1.9 copy-done.18
  436.5 2.1 fusion.15
  438.9 7.3 %multiply_reduce_fusion.1 = (f32[768]{0:T(1024)S(1)}, bf16[1376,768]{1,0:T(8,128)(2,1)}) fusion(f32[1376,768]{1,0:T(8,128)} %get-tuple-element.72, f32[1376,768]{1,0:T(8,128)} %get-tuple-element.103, f32[768]{0:T(1024)S(1)} %copy-done.50, f32[1376]{0:T(1024)S(1)} %negate_multiply_fusion.1, f32[1376]{0:T(1024)S(1)} %multiply_multiply_fusion.5, ...), kind=kLoop, calls=%fused_computation.45 | loop fusion | flops 16907520 | bytes 16939520 | tf_op jit(solution)/shard_map/reduce_sum | solution.py:828
  446.6 2.2 convert_reduce_fusion.5
  448.8 2.0 convert_reduce_fusion.4
  452.2 1.3 slice.302
  454.3 1.3 slice.300
  456.4 145.5 %finish.1 = (bf16[8,144,768]{2,1,0:T(8,128)(2,1)}, bf16[4,56,768]{2,1,0:T(8,128)(2,1)}, bf16[8,144,768]{2,1,0:T(8,128)(2,1)}, bf16[4,56,768]{2,1,0:T(8,128)(2,1)...) custom-call(bf16[2,4,144,768]{3,2,1,0:T(8,128)(2,1)} %bitcast.93, ...), custom_call_target="tpu_custom_call" | custom-call | tf_op jit(solution)/shard_map/finish/pallas_call | solution.py:557
  601.8 1.0 slice.312
  603.3 0.9 pad_maximum_fusion.2
  604.2 1.9 reshape.330
  606.1 1.4 slice.306
  607.5 1.4 reshape.326
  608.9 1.5 slice.307
  610.5 2.0 reshape.327
  612.5 0.9 slice_bitcast_fusion.2
  613.4 0.9 slice_bitcast_fusion.3
  615.3 1.7 reshape.328
  618.9 1.3 slice.257
  620.2 1.8 copy.82
  622.0 1.2 copy.83
  623.9 1.2 copy.85
  (251 shorter events, 23.0 us)
Async XLA Ops:
  2.9 1.5 copy-start.4
  4.4 1.5 copy-start.5
  5.9 1.0 copy-start.8
  6.8 1.0 copy-start.9
  7.8 1.0 copy-start.10
  8.8 1.0 copy-start.11
  9.7 0.9 copy-start.12
  10.7 0.9 copy-start.13
  155.8 1.2 copy-start.6
  157.0 1.8 copy-start.14
  158.7 1.2 copy-start.15
  158.7 56.2 %copy-start = (bf16[2,4,144,768]{3,2,1,0:T(8,128)(2,1)}, bf16[2,4,144,768]{3,2,1,0:T(8,128)(2,1)S(1)}, u32[]{:S(2)}) copy-start(bf16[2,4,144,768]{3,2,1,0:T(8,128)(2,1)S(1)} %get-tuple-element.37) | copy-start | bytes 5308420
  158.7 56.2 %copy-start.2 = (bf16[1,4,56,768]{3,2,1,0:T(8,128)(2,1)}, bf16[1,4,56,768]{3,2,1,0:T(8,128)(2,1)S(1)}, u32[]{:S(2)}) copy-start(bf16[1,4,56,768]{3,2,1,0:T(8,128)(2,1)S(1)} %get-tuple-element.38) | copy-start | bytes 1032196
  159.1 12.9 %copy-start.33 = (f32[1376]{0:T(1024)}, f32[1376]{0:T(1024)S(1)}, u32[]{:S(2)}) copy-start(f32[1376]{0:T(1024)S(1)} %broadcast_multiply_fusion.1) | copy-start | bytes 16516
  159.9 0.6 copy-start.37
  159.9 12.2 %copy-start.35 = (f32[1376]{0:T(1024)}, f32[1376]{0:T(1024)S(1)}, u32[]{:S(2)}) copy-start(f32[1376]{0:T(1024)S(1)} %fusion.19) | copy-start | bytes 16516
  161.7 10.3 %copy-start.47 = (f32[768]{0:T(1024)}, f32[768]{0:T(1024)S(1)}, u32[]{:S(2)}) copy-start(f32[768]{0:T(1024)S(1)} %mul.206) | copy-start | bytes 9220
  161.9 10.2 %copy-start.53 = (f32[768]{0:T(1024)}, f32[768]{0:T(1024)S(1)}, u32[]{:S(2)}) copy-start(f32[768]{0:T(1024)S(1)} %add.121) | copy-start | bytes 9220
  161.9 10.2 %copy-start.42 = (f32[12,729]{1,0:T(8,128)S(1)}, f32[12,729]{1,0:T(8,128)}, u32[]{:S(2)}) copy-start(f32[12,729]{1,0:T(8,128)} %param.22) | copy-start | bytes 104980
  184.0 30.6 %copy-start.46 = (f32[1,32,24]{1,2,0:T(8,128)S(1)}, f32[1,32,24]{1,2,0:T(8,128)}, u32[]{:S(2)}) copy-start(f32[1,32,24]{1,2,0:T(8,128)} %get-tuple-element.97) | copy-start | bytes 9220
  184.0 30.8 %copy-start.45 = (f32[1,32,24]{1,2,0:T(8,128)S(1)}, f32[1,32,24]{1,2,0:T(8,128)}, u32[]{:S(2)}) copy-start(f32[1,32,24]{1,2,0:T(8,128)} %get-tuple-element.102) | copy-start | bytes 9220
  214.7 6.2 copy-start.49
  214.9 6.0 copy-start.51
  220.9 2.0 copy-start.17
  223.5 0.6 copy-start.39
  224.1 48.5 %copy-start.44 = (f32[1,32,24]{1,2,0:T(8,128)S(1)}, f32[1,32,24]{1,2,0:T(8,128)}, u32[]{:S(2)}) copy-start(f32[1,32,24]{1,2,0:T(8,128)} %get-tuple-element.94) | copy-start | bytes 9220
  224.1 48.6 %copy-start.43 = (f32[1,32,24]{1,2,0:T(8,128)S(1)}, f32[1,32,24]{1,2,0:T(8,128)}, u32[]{:S(2)}) copy-start(f32[1,32,24]{1,2,0:T(8,128)} %get-tuple-element.93) | copy-start | bytes 9220
  224.1 48.8 %copy-start.7 = (bf16[2,4,144,768]{3,2,1,0:T(8,128)(2,1)S(1)}, bf16[2,4,144,768]{3,2,1,0:T(8,128)(2,1)}, u32[]{:S(2)}) copy-start(bf16[2,4,144,768]{3,2,1,0:T(8,128)(2,1)} %copy-done.6) | copy-start | bytes 5308420
  273.3 14.9 %copy-start.19 = (f32[1152,768]{1,0:T(8,128)}, f32[1152,768]{1,0:T(8,128)S(1)}, u32[]{:S(2)}) copy-start(f32[1152,768]{1,0:T(8,128)S(1)} %bitcast_convert_fusion) | copy-start | bytes 10616836
  273.3 14.9 %slice-start.2 = ((s8[8454144]{0:T(1024)(128)(4,1)}), s8[4194304]{0:T(1024)(128)(4,1)S(1)}, s32[]{:S(2)}) async-start(s8[8454144]{0:T(1024)(128)(4,1)} %bitcast.120), calls=%async_computation.2 | async-start | bytes 8388608
  273.5 14.7 %slice-start.3 = ((s8[8454144]{0:T(1024)(128)(4,1)}), s8[4194304]{0:T(1024)(128)(4,1)S(1)}, s32[]{:S(2)}) async-start(s8[8454144]{0:T(1024)(128)(4,1)} %bitcast.120), calls=%async_computation.3 | async-start | bytes 8388608
  273.5 14.7 %slice-start.4 = ((s8[8454144]{0:T(1024)(128)(4,1)}), s8[65536]{0:T(1024)(128)(4,1)S(1)}, s32[]{:S(2)}) async-start(s8[8454144]{0:T(1024)(128)(4,1)} %bitcast.120), calls=%async_computation.4 | async-start | bytes 131072
  288.2 9.5 %copy-start.56 = (bf16[1376,768]{1,0:T(8,128)(2,1)}, bf16[1376,768]{1,0:T(8,128)(2,1)S(1)}, u32[]{:S(2)}) copy-start(bf16[1376,768]{1,0:T(8,128)(2,1)S(1)} %get-tuple-element.82) | copy-start | bytes 6340612
  321.8 14.3 %copy-start.55 = (bf16[1376,3072]{1,0:T(8,128)(2,1)S(1)}, bf16[1376,3072]{1,0:T(8,128)(2,1)}, u32[]{:S(2)}) copy-start(bf16[1376,3072]{1,0:T(8,128)(2,1)} %get-tuple-element.108) | copy-start | bytes 25362436
  321.8 25.9 %slice-start = ((s8[4227072]{0:T(1024)(128)(4,1)}), s8[4194304]{0:T(1024)(128)(4,1)S(1)}, s32[]{:S(2)}) async-start(s8[4227072]{0:T(1024)(128)(4,1)} %bitcast.90), calls=%async_computation | async-start | bytes 8388608
  336.0 11.6 %copy-start.40 = (f32[1376]{0:T(1024)S(1)}, f32[1376]{0:T(1024)}, u32[]{:S(2)}) copy-start(f32[1376]{0:T(1024)} %copy-done.39) | copy-start | bytes 16516
  336.0 11.7 %slice-start.1 = ((s8[4227072]{0:T(1024)(128)(4,1)}), s8[32768]{0:T(1024)(128)(4,1)S(1)}, s32[]{:S(2)}) async-start(s8[4227072]{0:T(1024)(128)(4,1)} %bitcast.90), calls=%async_computation.1 | async-start | bytes 65536
  347.7 2.0 copy-start.20
  347.7 2.0 copy-start.52
  349.7 2.9 copy-start.16
  407.1 2.2 copy-start.25
  407.2 2.9 copy-start.22
  409.4 1.6 copy-start.1
  409.4 1.7 copy-start.3
  409.4 1.7 copy-start.34
  409.4 1.7 copy-start.36
  409.4 1.7 copy-start.48
  409.4 1.7 copy-start.54
  411.1 7.9 %copy-start.28 = (bf16[1376,2304]{1,0:T(8,128)(2,1)}, bf16[1376,2304]{1,0:T(8,128)(2,1)S(1)}, u32[]{:S(2)}) copy-start(bf16[1376,2304]{1,0:T(8,128)(2,1)S(1)} %constant_dynamic-update-slice_fusion) | copy-start | bytes 19021828
  411.1 7.9 %copy-start.23 = (bf16[1376,768]{1,0:T(8,128)(2,1)S(1)}, bf16[1376,768]{1,0:T(8,128)(2,1)}, u32[]{:S(2)}) copy-start(bf16[1376,768]{1,0:T(8,128)(2,1)} %attend.1) | copy-start | bytes 6340612
  424.9 9.7 %copy-start.38 = (f32[1376]{0:T(1024)S(1)}, f32[1376]{0:T(1024)}, u32[]{:S(2)}) copy-start(f32[1376]{0:T(1024)} %copy-done.37) | copy-start | bytes 16516
  434.6 2.0 copy-start.18
  434.6 4.3 copy-start.50
  446.2 6.0 copy-start.21
  451.3 2.9 copy-start.24
  601.8 20.1 %copy-start.27 = (bf16[8,144,768]{2,1,0:T(8,128)(2,1)S(1)}, bf16[8,144,768]{2,1,0:T(8,128)(2,1)}, u32[]{:S(2)}) copy-start(bf16[8,144,768]{2,1,0:T(8,128)(2,1)} %get-tuple-element.131) | copy-start | bytes 5308420
  604.1 19.8 %copy-start.26 = (bf16[8,144,768]{2,1,0:T(8,128)(2,1)S(1)}, bf16[8,144,768]{2,1,0:T(8,128)(2,1)}, u32[]{:S(2)}) copy-start(bf16[8,144,768]{2,1,0:T(8,128)(2,1)} %get-tuple-element.133) | copy-start | bytes 5308420
  617.7 5.4 copy-start.29
  620.2 4.9 copy-start.32
  622.0 3.9 copy-start.41
  622.0 4.5 copy-start.31
  622.0 5.2 copy-start.30

commit v2 on v1

v2 whole, which is shorter than its diff:
```python
import functools

import jax
import jax.numpy as jnp
from jax import lax
from jax.experimental import pallas as pl
from jax.experimental.pallas import tpu as pltpu
from jax.sharding import PartitionSpec as P

H = 12
SIDE_S = 14
SIDE_L = 24
LEN_S = 224
LEN_L = 576
WIDE_L = 1152
WIDE_S = 512

F32 = jnp.float32
BF = jnp.bfloat16
NN = (((1,), (0,)), ((), ()))
NT = (((1,), (1,)), ((), ()))
TN = (((0,), (0,)), ((), ()))
MESH = pl.DeviceIdType.MESH
ANY = pl.BlockSpec(memory_space=pl.ANY)
MIB = 1 << 20


def dot(left, right, dims):
    return lax.dot_general(left, right, dims, preferred_element_type=F32)


class Place:
    def __init__(self, img_size):
        self.img = lax.axis_index("img")
        self.row = lax.axis_index("rows")
        self.zs = img_size // 2
        self.z, self.x = self.img // 2, self.img % 2
        self.y, self.c = self.row // 2, self.row % 2

    def at(self, z=None, x=None, y=None, c=None):
        z = self.z if z is None else z
        x = self.x if x is None else x
        y = self.y if y is None else y
        c = self.c if c is None else c
        return (z * 2 + x, y * 2 + c)

    def z_other(self, step):
        return lax.rem(self.z + step, self.zs)

    def row_other(self, step):
        return lax.rem(self.row + step, 4)

    def partners(self):
        along_z = [self.at(z=self.z_other(s)) for s in range(1, self.zs)]
        in_rows = [(self.img, self.row_other(s)) for s in range(1, 4)]
        return along_z + in_rows + [self.at(x=1 - self.x)]


def greet(partners):
    barrier = pltpu.get_barrier_semaphore()
    for p in partners:
        pl.semaphore_signal(barrier, inc=1, device_id=p, device_id_type=MESH)
    pl.semaphore_wait(barrier, len(partners))


class Remote:
    def __init__(self, copies, build):
        self.copies, self.build, self.at = copies, build, copies.remotes
        copies.remotes += 1

    def made(self):
        src, dst, device = self.build()
        return pltpu.make_async_remote_copy(
            src_ref=src, dst_ref=dst, send_sem=self.copies.send.at[self.at], recv_sem=self.copies.recv.at[self.at],
            device_id=device, device_id_type=MESH,
        )

    def start(self):
        self.made().start()
        return self

    def wait_send(self):
        self.made().wait_send()

    def wait_recv(self):
        self.made().wait_recv()


class Local:
    def __init__(self, copies, build):
        self.copies, self.build, self.at = copies, build, copies.locals
        copies.locals += 1

    def made(self):
        return pltpu.make_async_copy(*self.build(), self.copies.local.at[self.at])

    def start(self):
        self.made().start()
        return self

    def wait(self):
        self.made().wait()


class Copies:
    def __init__(self, send, recv, local):
        self.send, self.recv, self.local = send, recv, local
        self.remotes, self.locals = 0, 0

    def remote(self, build):
        return Remote(self, build)

    def here(self, build):
        return Local(self, build)


def pipelined(units):
    depth = max(len(u) for u in units)

    def step(t):
        for f in range(depth):
            u = t - f
            if 0 <= u < len(units) and f < len(units[u]):
                units[u][f]()

    return [functools.partial(step, t) for t in range(len(units) + depth - 1)]


def columns(start, size):
    return pl.ds(pl.multiple_of(start, 128), size)


class Gather:
    def __init__(self, place, copies, shard, full, both, low, pieces):
        self.p, self.copies = place, copies
        self.full, self.both, self.low = full, both, low
        self.k, self.cols = shard.shape
        self.half = self.cols // 2
        self.panels, self.wide = full.shape[0], full.shape[-1]
        self.tall = 2 * self.k // pieces
        self.pieces = pieces
        p = place

        def mine():
            return both.at[pl.ds(pl.multiple_of(p.c * self.k, 8), self.k)]

        self.kept = copies.here(lambda: (shard.at[:, columns(p.c * self.half, self.half)], mine()))
        self.swapped = copies.remote(
            lambda: (shard.at[:, columns((1 - p.c) * self.half, self.half)], mine(), p.at(c=1 - p.c)))

    def exchange(self):
        self.kept.start()
        self.swapped.start()

    def convert(self):
        self.kept.wait()
        self.swapped.wait_recv()
        self.low[...] = self.both[...].astype(BF)

    def unit(self, u, r):
        p, full = self.p, self.full
        rows = pl.ds(r * self.tall, self.tall)
        src = self.low.at[rows, pl.ds(u * self.wide, self.wide)]

        def dst():
            return full.at[u, p.c, p.z, p.x, p.y, rows]

        def twice(part, device):
            return self.copies.remote(lambda: (part(), part(), device()))

        own = self.copies.here(lambda: (src, dst()))
        over_z = [
            self.copies.remote(lambda s=s: (src, dst(), p.at(z=p.z_other(s)))) for s in range(1, p.zs)
        ]
        over_y = twice(lambda: full.at[u, p.c, :, p.x, p.y, rows], lambda: p.at(y=1 - p.y))
        over_x = twice(lambda: full.at[u, p.c, :, p.x, :, rows], lambda: p.at(x=1 - p.x))
        over_c = twice(lambda: full.at[u, p.c, :, :, :, rows], lambda: p.at(c=1 - p.c))

        def along_z():
            if u == 0 and r == 0:
                self.convert()
            for copy in [own] + over_z:
                copy.start()

        def along_y():
            own.wait()
            for copy in over_z:
                copy.wait_recv()
            over_y.start()

        def along_x():
            over_y.wait_recv()
            over_x.start()

        def along_c():
            over_x.wait_recv()
            over_c.start()

        def finish():
            over_c.wait_recv()
            for copy in over_z + [over_y, over_x, over_c]:
                copy.wait_send()
            if u == 0 and r == 0:
                self.swapped.wait_send()

        return [along_z, along_y, along_x, along_c, finish]

    def units(self):
        return [self.unit(u, r) for u in range(self.panels) for r in range(self.pieces)]

    @staticmethod
    def scratch(shape):
        k, cols = shape
        return [pltpu.VMEM((2 * k, cols // 2), F32), pltpu.VMEM((2 * k, cols // 2), BF)]


class Spread:
    def __init__(self, place, copies, block, full):
        p = place

        def dst():
            return full.at[p.z, p.x, p.y, p.c]

        def twice(part, device):
            return copies.remote(lambda: (part(), part(), device()))

        self.own = copies.here(lambda: (block, dst()))
        self.over_z = [copies.remote(lambda s=s: (block, dst(), p.at(z=p.z_other(s)))) for s in range(1, p.zs)]
        self.over_y = twice(lambda: full.at[:, p.x, p.y, p.c], lambda: p.at(y=1 - p.y))
        self.over_x = twice(lambda: full.at[:, p.x, :, p.c], lambda: p.at(x=1 - p.x))
        self.over_c = twice(lambda: full.at[:, :, :, p.c], lambda: p.at(c=1 - p.c))

    def along_z(self):
        for copy in [self.own] + self.over_z:
            copy.start()

    def along_y(self):
        self.own.wait()
        for copy in self.over_z:
            copy.wait_recv()
        self.over_y.start()

    def along_x(self):
        self.over_y.wait_recv()
        self.over_x.start()

    def along_c(self):
        self.over_x.wait_recv()
        self.over_c.start()

    def finish(self):
        self.over_c.wait_recv()
        for copy in self.over_z + [self.over_y, self.over_x, self.over_c]:
            copy.wait_send()

    def units(self):
        return [[self.along_z, self.along_y, self.along_x, self.along_c, self.finish]]


class Move:
    def __init__(self, place, copies, src, dst, to_images):
        p = place
        n = (src if to_images else dst).shape[0] // 4

        def part(row):
            if to_images:
                return src.at[pl.ds(row * n, n)], dst.at[:, p.row]
            return src.at[:, row], dst.at[pl.ds(p.row * n, n)]

        self.own = copies.here(lambda: part(p.row))
        self.sent = [
            copies.remote(lambda s=s: part(p.row_other(s)) + ((p.img, p.row_other(s)),)) for s in (2, 3, 1)
        ]

    def start(self):
        for copy in self.sent + [self.own]:
            copy.start()

    def finish(self):
        self.own.wait()
        for copy in self.sent:
            copy.wait_recv()
        for copy in self.sent:
            copy.wait_send()


class Scatter:
    def __init__(self, place, copies, grad, shard, scratch, pieces):
        self.p, self.copies, self.grad, self.shard = place, copies, grad, shard
        self.own, self.from_c, self.from_x, self.from_y, self.from_z, self.summed = scratch[:6]
        self.stage = scratch[6] if grad is None else None
        self.k, self.cols = shard.shape
        self.half = self.cols // 2
        self.pieces = pieces
        self.panels = self.own.shape[0] // pieces
        self.wide, self.tall = self.own.shape[-1], self.own.shape[-2]
        p = place

        def cols():
            return columns(p.c * self.half, self.half)

        def rows(c):
            return pl.ds(pl.multiple_of(c * self.k, 8), self.k)

        self.last = copies.remote(
            lambda: (self.summed.at[rows(1 - p.c)], shard.at[:, cols()], p.at(c=1 - p.c)))
        self.kept = copies.here(lambda: (self.summed.at[rows(p.c)], shard.at[:, cols()]))

    def unit(self, u, r):
        p, copies, grad = self.p, self.copies, self.grad
        at = u * self.pieces + r
        own, from_c, from_x = self.own.at[at], self.from_c.at[at], self.from_x.at[at]
        from_y, from_z = self.from_y.at[at], self.from_z.at[at]
        rows = pl.ds(r * self.tall, self.tall)
        if grad is None:
            over_c = copies.remote(lambda: (self.stage.at[at], from_c, p.at(c=1 - p.c)))
            loaded = None
        else:
            over_c = copies.remote(lambda: (grad.at[u, 1 - p.c, :, :, :, rows], from_c, p.at(c=1 - p.c)))
            loaded = copies.here(lambda: (grad.at[u, p.c, :, :, :, rows], own))
        over_x = copies.remote(lambda: (own.at[:, 1 - p.x], from_x, p.at(x=1 - p.x)))
        over_y = copies.remote(lambda: (own.at[:, p.x, 1 - p.y], from_y, p.at(y=1 - p.y)))
        over_z = [
            copies.remote(lambda s=s: (own.at[p.z_other(s), p.x, p.y], from_z.at[s - 1], p.at(z=p.z_other(s))))
            for s in range(1, p.zs)
        ]

        def add(into, other):
            into[...] = (into[...].astype(F32) + other[...].astype(F32)).astype(BF)

        def along_c():
            over_c.start()
            if loaded is not None:
                loaded.start()

        def along_x():
            if loaded is not None:
                loaded.wait()
            over_c.wait_recv()
            for z in range(p.zs):
                add(own.at[z, 1 - p.x], from_c.at[z, 1 - p.x])
            over_x.start()
            for z in range(p.zs):
                add(own.at[z, p.x], from_c.at[z, p.x])

        def along_y():
            over_x.wait_recv()
            for z in range(p.zs):
                add(own.at[z, p.x, 1 - p.y], from_x.at[z, 1 - p.y])
            over_y.start()
            for z in range(p.zs):
                add(own.at[z, p.x, p.y], from_x.at[z, p.y])

        def along_z():
            over_y.wait_recv()
            for z in range(p.zs):
                add(own.at[z, p.x, p.y], from_y.at[z])
            for copy in over_z:
                copy.start()

        def finish():
            for copy in over_z:
                copy.wait_recv()
            total = own[p.z, p.x, p.y].astype(F32)
            for s in range(p.zs - 1):
                total += from_z[s].astype(F32)
            self.summed[rows, pl.ds(u * self.wide, self.wide)] = total
            for copy in [over_c, over_x, over_y] + over_z:
                copy.wait_send()
            if at == self.panels * self.pieces - 1:
                self.last.start()
                self.kept.start()

        return [along_c, along_x, along_y, along_z, finish]

    def end(self):
        self.kept.wait()
        self.last.wait_recv()
        self.last.wait_send()

    def units(self):
        return [self.unit(u, r) for u in range(self.panels) for r in range(self.pieces)]

    @staticmethod
    def scratch(zs, k, cols, panels, pieces, staged=False):
        n, tall, w = panels * pieces, 2 * k // pieces, cols // 2 // panels
        shapes = [(n, zs, 2, 2, tall, w), (n, zs, 2, 2, tall, w), (n, zs, 2, tall, w), (n, zs, tall, w),
                  (n, zs - 1, tall, w)]
        return [pltpu.VMEM(s, BF) for s in shapes] + [pltpu.VMEM((2 * k, cols // 2), F32)] + (
            [pltpu.VMEM(shapes[0], BF)] if staged else [])

    @staticmethod
    def remotes(zs, panels, pieces):
        return 1 + panels * pieces * (zs + 2)


class Total:
    def __init__(self, place, copies, grad, result, got, work, from_z):
        self.p, self.grad, self.got, self.work, self.from_z = place, grad, got, work, from_z
        p = place
        self.kept = copies.here(lambda: (grad.at[p.c], work))
        self.over_c = copies.remote(lambda: (grad.at[1 - p.c], got.at[0], p.at(c=1 - p.c)))
        self.over_x = copies.remote(lambda: (work, got.at[1], p.at(x=1 - p.x)))
        self.over_y = copies.remote(lambda: (work, got.at[2], p.at(y=1 - p.y)))
        self.over_z = [
            copies.remote(lambda s=s: (from_z.at[p.z], from_z.at[p.z], p.at(z=p.z_other(s)))) for s in range(1, p.zs)
        ]
        self.last = [
            copies.remote(lambda: (work, result.at[p.c], p.at(c=1 - p.c))),
            copies.here(lambda: (work, result.at[p.c])),
        ]

    def along_c(self):
        self.kept.start()
        self.over_c.start()

    def along_x(self):
        self.kept.wait()
        self.over_c.wait_recv()
        self.work[...] = self.work[...] + self.got[0]
        self.over_x.start()

    def along_y(self):
        self.over_x.wait_recv()
        self.over_x.wait_send()
        self.work[...] = self.work[...] + self.got[1]
        self.over_y.start()

    def along_z(self):
        self.over_y.wait_recv()
        self.over_y.wait_send()
        self.from_z[self.p.z] = self.work[...] + self.got[2]
        for copy in self.over_z:
            copy.start()

    def finish(self):
        for copy in self.over_z:
            copy.wait_recv()
        for copy in [self.over_c] + self.over_z:
            copy.wait_send()
        total = self.from_z[0]
        for z in range(1, self.p.zs):
            total += self.from_z[z]
        self.work[...] = total
        for copy in self.last:
            copy.start()

    def end(self):
        self.last[1].wait()
        self.last[0].wait_recv()
        self.last[0].wait_send()

    def units(self):
        return [[self.along_c, self.along_x, self.along_y, self.along_z, self.finish]]

    @staticmethod
    def scratch(zs, rows, wide):
        return [pltpu.VMEM((3, rows, wide), F32), pltpu.VMEM((rows, wide), F32), pltpu.VMEM((zs, rows, wide), F32)]

    @staticmethod
    def remotes(zs):
        return zs + 3


def semaphores(remotes, locals_):
    return [
        pltpu.SemaphoreType.DMA((remotes,)),
        pltpu.SemaphoreType.DMA((remotes,)),
        pltpu.SemaphoreType.DMA((locals_,)),
    ]


def split_refs(refs, *sizes):
    parts, at = [], 0
    for size in sizes:
        parts.append(refs[at:at + size])
        at += size
    return parts + [refs[at:]]


def full_shape(img_size, shard, panels):
    k, cols = shard.shape
    return (panels, 2, img_size // 2, 2, 2, 2 * k, cols // 2 // panels)


def front(img_size, arrays, block, shards, cuts):
    na, nw = len(arrays), len(shards)
    zs = img_size // 2
    outs = [jax.ShapeDtypeStruct((a.shape[0] // 4, 4) + a.shape[1:], a.dtype) for a in arrays]
    outs += [jax.ShapeDtypeStruct((zs, 2, 2, 2, 8, 128), F32)]
    outs += [jax.ShapeDtypeStruct(full_shape(img_size, s, c[0]), BF) for s, c in zip(shards, cuts)]

    def kernel(*refs):
        ins, blk, sh, whole, small, full, scr = split_refs(refs, na, 1, nw, na, 1, nw)
        p = Place(img_size)
        greet(p.partners())
        copies = Copies(*scr[-3:])
        gathers = [Gather(p, copies, sh[i], full[i], scr[2 * i], scr[2 * i + 1], cuts[i][1]) for i in range(nw)]
        moves = [Move(p, copies, a, b, True) for a, b in zip(ins, whole)]
        for g in gathers:
            g.exchange()
        for m in moves:
            m.start()
        units = Spread(p, copies, blk[0], small[0]).units()
        for g in gathers:
            units += g.units()
        for step in pipelined(units):
            step()
        for m in moves:
            m.finish()

    count = sum(a * b for a, b in cuts)
    return pl.pallas_call(
        kernel,
        out_shape=outs,
        in_specs=[ANY] * (na + 1 + nw),
        out_specs=[ANY] * len(outs),
        scratch_shapes=[s for w in shards for s in Gather.scratch(w.shape)]
        + semaphores(3 * na + (zs + 2) * (1 + count) + nw, na + 1 + nw + count),
        compiler_params=pltpu.CompilerParams(collective_id=0, has_side_effects=True, vmem_limit_bytes=40 * MIB),
        name="front",
    )(*arrays, block, *shards)


def table_rows(table, side, blocks, wide):
    span = 2 * side - 1
    square = table.reshape(H, span, span)
    square = jnp.concatenate([square] + [square[:, -1:]] * (blocks - span), 1)
    rows = []
    for turned in (square, square[:, ::-1, ::-1]):
        for part, pads in ((turned[:, :, :side], (0, 1)), (turned[:, :, side:], (1, 0))):
            part = jnp.pad(part, ((0, 0), pads, (0, side - part.shape[2])))
            flat = part.reshape(H, 1, (blocks + 1) * side)
            rows.append(jnp.roll(jnp.pad(flat, ((0, 0), (0, 0), (0, wide - flat.shape[2]))), 1 - side, 2))
    return jnp.concatenate(rows + [jnp.zeros((H, 4, wide), F32)], 1)


def table_sums(rows, side, blocks):
    span = 2 * side - 1
    rows = jnp.roll(rows, side - -(-side // 8) * 8, 2)
    parts = rows[:, :, :(blocks + 1) * side].reshape(H, 2, blocks + 1, side)
    square = jnp.concatenate([parts[:, 0, :blocks], parts[:, 1, 1:, :side - 1]], 2)
    square = jnp.concatenate([square[:, :span - 1], jnp.sum(square[:, span - 1:], 1, keepdims=True)], 1)
    return square.reshape(H, span * span)


def lower_offsets(side, rows, wide):
    lane = lax.rem(lax.broadcasted_iota(jnp.int32, (rows, wide), 1), side)
    return lane <= lax.broadcasted_iota(jnp.int32, (rows, wide), 0)


def spread_rows(rows_ref, h, first, side, rows, wide, lower):
    low = jnp.broadcast_to(rows_ref[h, first:first + 1, :], (rows, wide))
    high = jnp.broadcast_to(rows_ref[h, first + 1:first + 2, :], (rows, wide))
    return jnp.where(
        lower, pltpu.roll(low, 0, 1, stride=1, stride_axis=0), pltpu.roll(high, 0, 1, stride=1, stride_axis=0)
    )


def fill_bias(bias, h, spread, side, rows, first_offset):
    size = bias.shape[2]
    wide = spread.shape[1]
    window = -(-size // 128) * 128 + 128
    for r in range(rows):
        offset = (first_offset - r) * side
        base, rest = offset // 128 * 128, offset % 128
        part = spread[:, base:min(base + window, wide)]
        if part.shape[1] < window:
            part = jnp.concatenate([part, jnp.zeros((spread.shape[0], window - part.shape[1]), F32)], 1)
        if rest:
            part = pltpu.roll(part, window - rest, 1)
        bias[h, r * side:(r + 1) * side, :] = part[:side, :size]


def fold_bias(total, h, acc, side, rows, first_offset, lower, out_ref, half, row):
    size = total.shape[2]
    window = -(-size // 128) * 128 + 128
    height, wide = lower.shape
    acc[...] = jnp.zeros_like(acc)
    for r in range(rows):
        offset = (first_offset - r) * side
        base, rest = offset // 128 * 128, offset % 128
        part = total[h, r * side:(r + 1) * side, :]
        part = jnp.concatenate([part, jnp.zeros((side, window - size), F32)], 1)
        if rest:
            part = pltpu.roll(part, rest, 1)
        acc[:side, base:base + window] += part
    whole = acc[:, :wide]
    zero = jnp.zeros_like(whole)
    for at, part in enumerate((jnp.where(lower, whole, zero), jnp.where(lower, zero, whole))):
        turned = jnp.concatenate([part[j:j + 1] for j in reversed(range(height))], 0)
        moved = pltpu.roll(turned, 0, 1, stride=1, stride_axis=0)
        out_ref[half, pl.ds(row + at, 1), :] = jnp.sum(moved, 0, keepdims=True)


def head_part(full, mask, h):
    keep = mask if h == 0 else jnp.logical_not(mask)
    return jnp.where(keep, full, jnp.zeros_like(full))


def attend_kernel(large, small, q_ref, k_ref, v_ref, rows_l, rows_s, o_ref, bias_l, bias_s):
    mask = lax.broadcasted_iota(jnp.int32, (1, 128), 1) < 64
    lower_l = lower_offsets(SIDE_L, SIDE_L, WIDE_L)
    lower_s = lower_offsets(SIDE_S, 16, WIDE_S)
    for h in range(2):
        fill_bias(bias_l, h, spread_rows(rows_l, h, 2, SIDE_L, SIDE_L, WIDE_L, lower_l), SIDE_L, 24, 23)
        fill_bias(bias_s, h, spread_rows(rows_s, h, 2, SIDE_S, 16, WIDE_S, lower_s), SIDE_S, 16, 15)
    keep = lax.broadcasted_iota(jnp.int32, (1, LEN_S), 1) < SIDE_S * SIDE_S
    images = [(n * LEN_L, LEN_L, bias_l) for n in range(large)]
    images += [(large * LEN_L + n * LEN_S, LEN_S, bias_s) for n in range(small)]
    for at, size, bias in images:
        q, k, v = (ref[at:at + size, :] for ref in (q_ref, k_ref, v_ref))
        outs = []
        for h in range(2):
            s = dot(head_part(q, mask, h) * BF(0.125), k, NT) + bias[h]
            if size == LEN_S:
                s = jnp.where(keep, s, -1e30)
            e = jnp.exp(s - jnp.max(s, 1, keepdims=True))
            p = (e * (1.0 / jnp.sum(e, 1, keepdims=True))).astype(BF)
            outs.append(dot(p, v, NN))
        o_ref[at:at + size, :] = jnp.where(mask, outs[0], outs[1]).astype(BF)


def loop_points(steps, every):
    return {t * every: step for t, step in enumerate(steps)}


def run_point(points, iteration, at, per, iterations):
    for i in range(iterations):
        step = points.get(i * per + at)
        if step is not None:
            pl.when(iteration == i)(step)


def run_rest(points, count):
    for at in sorted(points):
        if at >= count:
            points[at]()


def attend_back_pair(hp, qkv, do_ref, rows_l, rows_s, df, sums_l, sums_s, scratch, large, small, between):
    bias_l, bias_s, total_l, total_s, acc_l, acc_s = scratch
    mask = lax.broadcasted_iota(jnp.int32, (1, 128), 1) < 64
    lower_l = lower_offsets(SIDE_L, SIDE_L, WIDE_L)
    lower_s = lower_offsets(SIDE_S, 16, WIDE_S)
    for h in range(2):
        fill_bias(bias_l, h, spread_rows(rows_l, 2 * hp + h, 0, SIDE_L, SIDE_L, WIDE_L, lower_l), SIDE_L, 24, 23)
        fill_bias(bias_s, h, spread_rows(rows_s, 2 * hp + h, 0, SIDE_S, 16, WIDE_S, lower_s), SIDE_S, 14, 13)
    keep = lax.broadcasted_iota(jnp.int32, (LEN_S, 1), 0) < SIDE_S * SIDE_S
    images = [(n * LEN_L, LEN_L, bias_l, total_l, n == 0) for n in range(large)]
    images += [(large * LEN_L + n * LEN_S, LEN_S, bias_s, total_s, n == 0) for n in range(small)]
    cols = [columns(i * 64 * H + hp * 128, 128) for i in range(3)]
    for index, (at, size, bias, total, first) in enumerate(images):
        between(index)
        rows = slice(at, at + size)
        q, k, v = (qkv[rows, c] for c in cols)
        do = do_ref[rows, cols[0]]
        got = []
        for h in range(2):
            s = dot(head_part(k, mask, h) * BF(0.125), q, NT) + bias[h]
            if size == LEN_S:
                s = jnp.where(keep, s, -1e30)
            e = jnp.exp(s - jnp.max(s, 0, keepdims=True))
            p = e * (1.0 / jnp.sum(e, 0, keepdims=True))
            dp = dot(head_part(v, mask, h), do, NT).astype(BF).astype(F32)
            pd = p * dp
            low = (pd - p * jnp.sum(pd, 0, keepdims=True)).astype(BF)
            got.append((dot(low, k, TN), dot(low, q, NN), dot(p.astype(BF), do, NN)))
            total[h] = low.astype(F32) if first else total[h] + low.astype(F32)
        for c, a, b, scale in zip(cols, got[0], got[1], (0.125, 0.125, 1.0)):
            df[rows, c] = (jnp.where(mask, a, b) * scale).astype(BF)
    half, within = hp // 3, lax.rem(hp, 3)
    for h in range(2):
        fold_bias(total_l, h, acc_l, SIDE_L, 24, 23, lower_l, sums_l, half, 4 * within + 2 * h)
        fold_bias(total_s, h, acc_s, SIDE_S, 14, 13, lower_s, sums_s, half, 4 * within + 2 * h)


def back_scratch():
    return [pltpu.VMEM((2, LEN_L, LEN_L), F32), pltpu.VMEM((2, LEN_S, LEN_S), F32)] * 2 + [
        pltpu.VMEM((SIDE_L, WIDE_L + 128), F32), pltpu.VMEM((16, WIDE_S + 128), F32)]


VMEM = pl.BlockSpec(memory_space=pltpu.VMEM)


def attention_back(img_size, qkv, d_att, rows_l, rows_s, grads, cuts, wholes, large, small, every):
    zs = img_size // 2
    ng, nw = len(grads), len(wholes)
    rows = qkv.shape[0]
    shard_shapes = [(g.shape[5] // 2, g.shape[0] * 2 * g.shape[6]) for g in grads]

    def kernel(*refs):
        ins, gr, wh, outs, shards, blocks, scr = split_refs(refs, 4, ng, nw, 3, ng, nw)
        qkv_hbm, do_hbm, rl, rs = ins
        df_hbm, sums_l, sums_s = outs
        qkv_v, do_v, df_v = scr[:3]
        p = Place(img_size)
        copies = Copies(*scr[-3:])
        loads = [copies.here(lambda: (qkv_hbm, qkv_v)), copies.here(lambda: (do_hbm, do_v))]
        for copy in loads:
            copy.start()
        if ng + nw:
            greet(p.partners())
        at = 3 + 6
        scatters = []
        for i in range(ng):
            scatters.append(Scatter(p, copies, gr[i], shards[i], scr[at:at + 6], cuts[i]))
            at += 6
        moves = [Move(p, copies, a, b, False) for a, b in zip(wh, blocks)]
        units = [u for s in scatters for u in s.units()]
        points = loop_points(pipelined(units) if units else [], every)
        for m in moves:
            m.start()
        sums_l[...] = jnp.zeros_like(sums_l)
        sums_s[...] = jnp.zeros_like(sums_s)
        for copy in loads:
            copy.wait()

        def body(hp, carry):
            attend_back_pair(hp, qkv_v, do_v, rl, rs, df_v, sums_l, sums_s, scr[3:9], large, small,
                             lambda index: run_point(points, hp, index, large + small, H // 2))
            return carry

        lax.fori_loop(0, H // 2, body, 0)
        out = copies.here(lambda: (df_v, df_hbm))
        out.start()
        run_rest(points, (large + small) * (H // 2))
        for s in scatters:
            s.end()
        for m in moves:
            m.finish()
        out.wait()

    scratch = [pltpu.VMEM(qkv.shape, BF), pltpu.VMEM(d_att.shape, BF), pltpu.VMEM(qkv.shape, BF)] + back_scratch()
    for g, (k, cols), cut in zip(grads, shard_shapes, cuts):
        scratch += Scatter.scratch(zs, k, cols, g.shape[0], cut)
    remotes = 3 * nw + sum(Scatter.remotes(zs, g.shape[0], c) for g, c in zip(grads, cuts))
    locals_ = 3 + nw + sum(1 + g.shape[0] * c for g, c in zip(grads, cuts))
    remote = dict(collective_id=1, has_side_effects=True) if ng + nw else {}
    return pl.pallas_call(
        kernel,
        out_shape=[jax.ShapeDtypeStruct(qkv.shape, BF), jax.ShapeDtypeStruct((2, 16, WIDE_L), F32),
                   jax.ShapeDtypeStruct((2, 16, WIDE_S), F32)]
        + [jax.ShapeDtypeStruct(s, F32) for s in shard_shapes]
        + [jax.ShapeDtypeStruct((w.shape[0] * 4,) + w.shape[2:], w.dtype) for w in wholes],
        in_specs=[ANY, ANY, VMEM, VMEM] + [ANY] * (ng + nw),
        out_specs=[ANY, VMEM, VMEM] + [ANY] * (ng + nw),
        scratch_shapes=scratch + semaphores(max(remotes, 1), locals_),
        compiler_params=pltpu.CompilerParams(vmem_limit_bytes=60 * MIB, **remote),
        name="attention_back",
    )(qkv, d_att, rows_l, rows_s, *grads, *wholes)


def row_tiles(rows, tile, body):
    count = rows // tile

    def step(t, carry):
        body(pl.multiple_of(t * tile, 16), tile)
        return carry

    lax.fori_loop(0, count, step, 0)
    if rows % tile:
        body(count * tile, rows % tile)


def norm_parts(x):
    centered = x - jnp.mean(x, 1, keepdims=True)
    scale = lax.rsqrt(jnp.mean(centered * centered, 1, keepdims=True) + 1e-06)
    return centered * scale, scale


def norm_back(dn, hat, scale, gain):
    d_hat = dn * gain
    return scale * (d_hat - jnp.mean(d_hat, 1, keepdims=True) - hat * jnp.mean(d_hat * hat, 1, keepdims=True))


def fold8(values):
    return sum(values[i:i + 8] for i in range(0, values.shape[0], 8))


def place_small(ref, flat, at):
    for i in range(4):
        ref[at, i] = flat[i * 56:(i + 1) * 56].astype(ref.dtype)


def load_tokens(copies, large_hbm, small_hbm, flat, four):
    n, _, rows, _ = large_hbm.shape
    loads = [
        copies.here(lambda i=i, j=j: (large_hbm.at[i, j], flat.at[pl.ds((i * 4 + j) * rows, rows)]))
        for i in range(n) for j in range(4)
    ]
    return loads + [copies.here(lambda: (small_hbm, four))]


def join_small(flat, four, large):
    for n in range(four.shape[0]):
        rows = jnp.concatenate([four[n, i].astype(F32) for i in range(4)], 0)
        at = large * LEN_L + n * LEN_S
        flat[at:at + LEN_S, :] = rows.astype(flat.dtype)


def projection_back(img_size, df, dm, x_l, x_s, w_qkv, vectors, sums, tables, large, small):
    zs = img_size // 2
    rows, width = dm.shape
    panels, _, _, _, _, k2, wide = w_qkv.shape
    k, cols = k2 // 2, panels * 2 * wide
    nt = len(tables)

    def kernel(*refs):
        ins, tabs, outs, tab_outs, scr = split_refs(refs, 7, nt, 4, nt)
        df_hbm, dm_hbm, xl_hbm, xs_hbm, w_hbm, vec, sums_in = ins
        gl_out, gs_out, shard, sums_out = outs
        df_v, dm_v, flat, four, w_v, nt_v, dn, acc, own_sums, dl, ds = scr[:11]
        at = 11
        p = Place(img_size)
        copies = Copies(*scr[-3:])
        x_loads = load_tokens(copies, xl_hbm, xs_hbm, flat, four)
        df_load = copies.here(lambda: (df_hbm, df_v))
        later = [copies.here(lambda: (w_hbm, w_v)), copies.here(lambda: (dm_hbm, dm_v))]
        for copy in x_loads + [df_load] + later:
            copy.start()
        greet(p.partners())
        scatter = Scatter(p, copies, None, shard, scr[at:at + 7], 1)
        at += 7
        totals = []
        for a, b in zip(tabs, tab_outs):
            totals.append(Total(p, copies, a, b, *scr[at:at + 3]))
            at += 3
        last = Total(p, copies, own_sums, sums_out, *scr[at:at + 3])
        moves = [Move(p, copies, dl, gl_out, False), Move(p, copies, ds, gs_out, False)]
        for t in totals:
            t.along_c()
        for copy in x_loads:
            copy.wait()
        join_small(flat, four, large)
        gain, shift = vec[0:1, :], vec[4:5, :]

        def normed(start, size):
            hat, _ = norm_parts(flat[pl.ds(start, size), :].astype(F32))
            n1_v[pl.ds(start, size), :] = (hat * gain + shift).astype(BF)

        n1_v = scr[-4]
        row_tiles(rows, 96, normed)
        nt_v[...] = n1_v[...].T
        df_load.wait()
        units = scatter.units()
        for t in totals:
            t.along_x()
        for u in range(panels):
            def part(c):
                cols_ = columns(c * (cols // 2) + u * wide, wide)
                got = dot(nt_v[...], df_v[:, cols_], NN).astype(BF)
                return got.reshape(zs, 2, 2, k2, wide)
            scatter.stage[u] = part(1 - p.c)
            units[u][0]()
            scatter.own[u] = part(p.c)
            if u >= 1:
                units[u - 1][1]()
            if u >= 2:
                units[u - 2][2]()
            if u == 1:
                for t in totals:
                    t.along_y()
            if u == 2:
                for t in totals:
                    t.along_z()
        for copy in later:
            copy.wait()
        for u in range(panels):
            for c in range(2):
                cols_ = slice(c * (cols // 2) + u * wide, c * (cols // 2) + (u + 1) * wide)
                w = w_v[u, c].reshape(width, wide)
                got = dot(df_v[:, cols_], w, NT)
                dn[...] = got if u == 0 and c == 0 else dn[...] + got
            if u == 0:
                units[panels - 1][1]()
                units[panels - 2][2]()
        acc[...] = jnp.zeros_like(acc)

        def back(start, size):
            at_rows = pl.ds(start, size)
            hat, scale = norm_parts(flat[at_rows, :].astype(F32))
            d = dn[at_rows, :]
            acc[0] += fold8(d * hat)
            acc[1] += fold8(d)
            acc[2] += fold8(df_v[at_rows, :width].astype(F32))
            acc[3] += fold8(df_v[at_rows, 2 * width:].astype(F32))
            dm_v[at_rows, :] = dm_v[at_rows, :] + norm_back(d, hat, scale, gain)

        row_tiles(rows, 96, back)
        for i in range(large):
            for j in range(4):
                start = (i * 4 + j) * (LEN_L // 4)
                dl[i, j] = dm_v[start:start + LEN_L // 4, :].astype(BF)
        for n in range(small):
            start = large * LEN_L + n * LEN_S
            place_small(ds, dm_v[start:start + LEN_S, :], n)
        for m in moves:
            m.start()
        for i, row in ((0, 0), (1, 4), (2, 6), (3, 7)):
            own_sums[0, row:row + 1, :] = jnp.sum(acc[i], 0, keepdims=True)
        for row in (1, 2, 3, 5):
            own_sums[0, row:row + 1, :] = sums_in[0, row:row + 1, :]
        own_sums[1] = sums_in[1]
        last.along_c()
        units[panels - 1][2]()
        for f in (3, 4):
            for u in range(panels):
                units[u][f]()
            if f == 3:
                last.along_x()
                for t in totals:
                    t.finish()
        last.along_y()
        last.along_z()
        last.finish()
        scatter.end()
        for t in totals + [last]:
            t.end()
        for m in moves:
            m.finish()

    scratch = [
        pltpu.VMEM(df.shape, BF), pltpu.VMEM(dm.shape, F32), pltpu.VMEM((rows, width), BF),
        pltpu.VMEM(x_s.shape, BF), pltpu.VMEM(w_qkv.shape, BF), pltpu.VMEM((width, rows), BF),
        pltpu.VMEM((rows, width), F32), pltpu.VMEM((4, 8, width), F32), pltpu.VMEM((2, 8, width), F32),
        pltpu.VMEM(x_l.shape, BF), pltpu.VMEM(x_s.shape, BF),
    ] + Scatter.scratch(zs, k, cols, panels, 1, True)
    for t in list(tables) + [sums]:
        scratch += Total.scratch(zs, t.shape[1], t.shape[2])
    scratch += [pltpu.VMEM((rows, width), BF)]
    remotes = 6 + Scatter.remotes(zs, panels, 1) + Total.remotes(zs) * (nt + 1)
    locals_ = 4 * x_l.shape[0] + 1 + 3 + 2 + 1 + 2 * (nt + 1)
    f32 = lambda s: jax.ShapeDtypeStruct(s, F32)
    return pl.pallas_call(
        kernel,
        out_shape=[jax.ShapeDtypeStruct((4 * a.shape[0],) + a.shape[2:], BF) for a in (x_l, x_s)]
        + [f32((k, cols)), f32(sums.shape)] + [f32(t.shape) for t in tables],
        in_specs=[ANY] * 5 + [VMEM, VMEM] + [ANY] * nt,
        out_specs=[ANY] * (4 + nt),
        scratch_shapes=scratch + semaphores(remotes, locals_),
        compiler_params=pltpu.CompilerParams(collective_id=2, has_side_effects=True, vmem_limit_bytes=60 * MIB),
        name="projection_back",
    )(df, dm, x_l, x_s, w_qkv, vectors, sums, *tables)


def gelu_parts(u):
    bell = jnp.exp(-0.5 * (u * u))
    t = 1.0 / (1.0 + 0.2316418882663604 * jnp.abs(u))
    series = ((((1.061405429 * t - 1.453152027) * t + 1.421413741) * t - 0.284496736) * t + 0.254829592) * t
    tail = 0.5 * series * bell
    cdf = jnp.where(u >= 0.0, 1.0 - tail, tail)
    return u * cdf, cdf + 0.3989422804014327 * (u * bell)


def joined(w, *at):
    parts = [w[(at[0], c) + at[1:]] for c in range(2)]
    return jnp.concatenate([part.reshape(-1, part.shape[-1]) for part in parts], 1)


def image_rows(large, small):
    parts = [(n, j, (n * 4 + j) * (LEN_L // 4)) for n in range(large) for j in range(4)]
    return parts, [(n, large * LEN_L + n * LEN_S) for n in range(small)]


def forward_tail(att, x_l, x_s, ct_l, ct_s, w_out, w_up, w_down, vectors, up_vec):
    large, small = x_l.shape[0], x_s.shape[0]
    rows, width = att.shape
    chunks = up_vec.shape[0]
    half = rows // 2

    def kernel(att_hbm, xl_hbm, xs_hbm, cl_hbm, cs_hbm, wo_hbm, wu_hbm, wd_hbm, vec, upv,
               yl, ys, m_hbm, n2_hbm, e_hbm, g_hbm, dr_hbm, dy_hbm, sums,
               att_v, flat, four, ct_four, wo, wu, wd, m_v, n2_v, r_v, e_v, g_v, acc, local):
        copies = Copies(None, None, local)
        first = [copies.here(lambda: (att_hbm, att_v)), copies.here(lambda: (wo_hbm, wo))]
        first += load_tokens(copies, xl_hbm, xs_hbm, flat, four)
        second = [copies.here(lambda: (wu_hbm, wu))]
        third = [copies.here(lambda: (wd_hbm, wd))]
        for copy in first + second + third:
            copy.start()
        for copy in first:
            copy.wait()
        join_small(flat, four, large)
        g2, s1, s2, b2, bo, bd = (vec[i:i + 1, :] for i in (1, 2, 3, 5, 8, 9))

        def project(i, carry):
            at = pl.ds(pl.multiple_of(i * half, 16), half)
            m_v[at, :] = dot(att_v[at, :], joined(wo, 0), NN)
            return carry

        lax.fori_loop(0, 2, project, 0)

        def middle(start, size):
            at = pl.ds(start, size)
            m = flat[at, :].astype(F32) + s1 * (m_v[at, :] + bo)
            m_v[at, :] = m
            hat, _ = norm_parts(m)
            n2_v[at, :] = (hat * g2 + b2).astype(BF)

        row_tiles(rows, 96, middle)
        m_out = [copies.here(lambda: (m_v, m_hbm)), copies.here(lambda: (n2_v, n2_hbm))]
        for copy in m_out:
            copy.start()
        ct = load_tokens(copies, cl_hbm, cs_hbm, flat, ct_four)
        for copy in ct:
            copy.start()
        for copy in second + third:
            copy.wait()

        out_at = copies.locals
        copies.locals += 4

        def out(f, slot):
            return [
                pltpu.make_async_copy(v.at[slot], hbm.at[f], local.at[out_at + 2 * slot + i])
                for i, (v, hbm) in enumerate(((e_v, e_hbm), (g_v, g_hbm)))
            ]

        def chunk(f, carry):
            slot = lax.rem(f, 2)

            @pl.when(f >= 2)
            def _():
                for copy in out(f - 2, slot):
                    copy.wait()

            w1 = wu[lax.rem(f, 2), f // 2].reshape(width, width)
            w2 = jnp.concatenate([wd[0, c, f].reshape(width, width // 2) for c in range(2)], 1)
            for i in range(2):
                at = slice(i * half, (i + 1) * half)
                u = dot(n2_v[at, :], w1, NN) + upv[pl.ds(f, 1), :]
                e, g = gelu_parts(u)
                e = e.astype(BF)
                e_v[slot, at, :] = e
                g_v[slot, at, :] = g.astype(BF)
                r = dot(e, w2, NN)

                @pl.when(f == 0)
                def _():
                    r_v[at, :] = r

                @pl.when(f > 0)
                def _():
                    r_v[at, :] += r
            for copy in out(f, slot):
                copy.start()
            return carry

        lax.fori_loop(0, chunks, chunk, 0)
        for copy in ct:
            copy.wait()
        join_small(flat, ct_four, large)
        for n in range(small):
            at = large * LEN_L + n * LEN_S + SIDE_S * SIDE_S // 16 * 16
            keep = lax.broadcasted_iota(jnp.int32, (32, 1), 0) < SIDE_S * SIDE_S % 16
            flat[at:at + 32, :] = jnp.where(keep, flat[at:at + 32, :].astype(F32), 0.0).astype(BF)
        for copy in m_out:
            copy.wait()
        acc[...] = jnp.zeros_like(acc)

        def result(start, size):
            at = pl.ds(start, size)
            r = r_v[at, :] + bd
            dy = flat[at, :].astype(F32)
            dr = (s2 * dy).astype(BF)
            acc[0] += fold8(r * dy)
            acc[1] += fold8(dr.astype(F32))
            m_v[at, :] = m_v[at, :] + s2 * r
            n2_v[at, :] = dr

        row_tiles(rows, 96, result)
        last = [copies.here(lambda: (n2_v, dr_hbm)), copies.here(lambda: (flat, dy_hbm))]
        for copy in last:
            copy.start()
        for n, j, start in image_rows(large, small)[0]:
            yl[n, j] = m_v[start:start + LEN_L // 4, :].astype(BF)
        for n, start in image_rows(large, small)[1]:
            place_small(ys, m_v[start:start + LEN_S, :], n)
        for i in range(2):
            sums[i:i + 1, :] = jnp.sum(acc[i], 0, keepdims=True)
        for f in (chunks - 2, chunks - 1):
            for copy in out(f, f % 2):
                copy.wait()
        for copy in last:
            copy.wait()

    bf = lambda *s: jax.ShapeDtypeStruct(s, BF)
    return pl.pallas_call(
        kernel,
        out_shape=[bf(*x_l.shape), bf(*x_s.shape), jax.ShapeDtypeStruct((rows, width), F32), bf(rows, width),
                   bf(chunks, rows, width), bf(chunks, rows, width), bf(rows, width), bf(rows, width),
                   jax.ShapeDtypeStruct((8, width), F32)],
        in_specs=[ANY] * 8 + [VMEM, VMEM],
        out_specs=[VMEM, VMEM] + [ANY] * 6 + [VMEM],
        scratch_shapes=[
            pltpu.VMEM((rows, width), BF), pltpu.VMEM((rows, width), BF), pltpu.VMEM(x_s.shape, BF),
            pltpu.VMEM(x_s.shape, BF), pltpu.VMEM(w_out.shape, BF), pltpu.VMEM(w_up.shape, BF),
            pltpu.VMEM(w_down.shape, BF), pltpu.VMEM((rows, width), F32), pltpu.VMEM((rows, width), BF),
            pltpu.VMEM((rows, width), F32), pltpu.VMEM((2, rows, width), BF), pltpu.VMEM((2, rows, width), BF),
            pltpu.VMEM((2, 8, width), F32), pltpu.SemaphoreType.DMA((16 + 8 * large + 4,)),
        ],
        compiler_params=pltpu.CompilerParams(vmem_limit_bytes=60 * MIB),
        name="forward_tail",
    )(att, x_l, x_s, ct_l, ct_s, w_out, w_up, w_down, vectors, up_vec)


def backward_head(att, m, n2, e, g, dr, dy, w_out, w_up, w_down, vectors, sums_in):
    rows, width = att.shape
    chunks = e.shape[0]
    half = rows // 2

    def kernel(att_hbm, m_hbm, n2_hbm, e_hbm, g_hbm, dr_hbm, dy_hbm, wo_hbm, wu_hbm, wd_hbm, vec, s_in,
               go, gu, gd, dm_hbm, da_hbm, sums,
               att_v, m_v, n2_v, nt_v, e_v, g_v, dr_v, dy_v, wo, wu, wd, dn, du_v, gd_v, gu_v, go_v, acc, up_acc, local):
        copies = Copies(None, None, local)
        pairs = [(dr_hbm, dr_v), (n2_hbm, n2_v), (wd_hbm, wd), (wu_hbm, wu),
                 (m_hbm, m_v), (dy_hbm, dy_v), (att_hbm, att_v), (wo_hbm, wo)]
        loads = [copies.here(lambda a=a, b=b: (a, b)) for a, b in pairs]
        base = copies.locals
        copies.locals += 8

        def fetch(f, slot):
            return [pltpu.make_async_copy(h.at[f], v.at[slot], local.at[base + 2 * slot + i])
                    for i, (h, v) in enumerate(((e_hbm, e_v), (g_hbm, g_v)))]

        def put(f, slot):
            return [
                pltpu.make_async_copy(gd_v.at[slot], gd.at[0, :, f], local.at[base + 4 + 2 * slot]),
                pltpu.make_async_copy(gu_v.at[slot], gu.at[lax.rem(f, 2), f // 2], local.at[base + 5 + 2 * slot]),
            ]

        for copy in fetch(0, 0):
            copy.start()
        for copy in loads:
            copy.start()
        for copy in loads[:4]:
            copy.wait()
        nt_v[...] = n2_v[...].T
        g2, s1, b2, bo = (vec[i:i + 1, :] for i in (1, 2, 5, 8))

        def chunk(f, carry):
            slot = lax.rem(f, 2)
            for copy in fetch(f, slot):
                copy.wait()

            @pl.when(f + 1 < chunks)
            def _():
                for copy in fetch(f + 1, 1 - slot):
                    copy.start()

            @pl.when(f >= 2)
            def _():
                for copy in put(f - 2, slot):
                    copy.wait()

            w1 = wu[lax.rem(f, 2), f // 2].reshape(width, width)
            w2 = jnp.concatenate([wd[0, c, f].reshape(width, width // 2) for c in range(2)], 1)
            got = dot(e_v[slot], dr_v[...], TN).astype(BF)
            for c in range(2):
                part = got[:, c * (width // 2):(c + 1) * (width // 2)]
                gd_v[slot, c] = part.reshape(gd_v.shape[2:])
            total = jnp.zeros((8, width), F32)
            for i in range(2):
                at = slice(i * half, (i + 1) * half)
                de = dot(dr_v[at, :], w2, NT)
                du = (de * g_v[slot, at, :].astype(F32)).astype(BF)
                du_v[at, :] = du
                total += fold8(du.astype(F32))
                d = dot(du, w1, NT)

                @pl.when(f == 0)
                def _():
                    dn[at, :] = d

                @pl.when(f > 0)
                def _():
                    dn[at, :] += d
            up_acc[f] = total
            gu_v[slot] = dot(nt_v[...], du_v[...], NN).astype(BF).reshape(gu_v.shape[1:])
            for copy in put(f, slot):
                copy.start()
            return carry

        lax.fori_loop(0, chunks, chunk, 0)
        for copy in loads[4:]:
            copy.wait()
        acc[...] = jnp.zeros_like(acc)

        def norm(start, size):
            at = pl.ds(start, size)
            hat, scale = norm_parts(m_v[at, :])
            d = dn[at, :]
            acc[0] += fold8(d * hat)
            acc[1] += fold8(d)
            dm = dy_v[at, :].astype(F32) + norm_back(d, hat, scale, g2)
            da = (s1 * dm).astype(BF)
            acc[2] += fold8(da.astype(F32))
            m_v[at, :] = dm
            du_v[at, :] = da

        row_tiles(rows, 96, norm)
        out = [copies.here(lambda: (m_v, dm_hbm))]
        out[0].start()
        w = joined(wo, 0)
        got = dot(att_v[...], du_v[...], TN).astype(BF)
        for c in range(2):
            go_v[c] = got[:, c * (width // 2):(c + 1) * (width // 2)].reshape(go_v.shape[1:])
        out.append(copies.here(lambda: (go_v, go.at[0])))
        out[1].start()
        for i in range(2):
            at = slice(i * half, (i + 1) * half)
            n2_v[at, :] = dot(du_v[at, :], w, NT).astype(BF)
            a = dot(att_v[at, :], w, NN) + bo
            acc[3] += fold8(a * m_v[at, :])
        out.append(copies.here(lambda: (n2_v, da_hbm)))
        out[2].start()
        sums[...] = jnp.zeros_like(sums)
        for i, (part, row) in enumerate(((0, 1), (0, 5), (1, 0), (0, 2))):
            sums[part, row:row + 1, :] = jnp.sum(acc[i], 0, keepdims=True)
        sums[0, 3:4, :] = s_in[0:1, :]
        sums[1, 1:2, :] = s_in[1:2, :]
        for f in range(chunks):
            sums[1, 2 + f:3 + f, :] = jnp.sum(up_acc[f], 0, keepdims=True)
        for f in (chunks - 2, chunks - 1):
            for copy in put(f, f % 2):
                copy.wait()
        for copy in out:
            copy.wait()

    bf = lambda *s: jax.ShapeDtypeStruct(s, BF)
    f32 = lambda *s: jax.ShapeDtypeStruct(s, F32)
    vm = pltpu.VMEM
    flat = vm((rows, width), BF)
    return pl.pallas_call(
        kernel,
        out_shape=[bf(*w_out.shape), bf(*w_up.shape), bf(*w_down.shape), f32(rows, width), bf(rows, width),
                   f32(2, 8, width)],
        in_specs=[ANY] * 10 + [VMEM, VMEM],
        out_specs=[ANY] * 5 + [VMEM],
        scratch_shapes=[
            flat, vm((rows, width), F32), flat, vm((width, rows), BF), vm((2, rows, width), BF),
            vm((2, rows, width), BF), flat, flat, vm(w_out.shape, BF), vm(w_up.shape, BF), vm(w_down.shape, BF),
            vm((rows, width), F32), flat, vm((2, 2) + w_down.shape[3:], BF), vm((2,) + w_up.shape[2:], BF),
            vm(w_out.shape[1:], BF), vm((4, 8, width), F32), vm((chunks, 8, width), F32),
            pltpu.SemaphoreType.DMA((24,)),
        ],
        compiler_params=pltpu.CompilerParams(vmem_limit_bytes=60 * MIB),
        name="backward_head",
    )(att, m, n2, e, g, dr, dy, w_out, w_up, w_down, vectors, sums_in)


def project_in(x_l, x_s, w_qkv, vectors, merged_bias):
    large, small = x_l.shape[0], x_s.shape[0]
    rows, width = large * LEN_L + small * LEN_S, x_l.shape[3]
    panels, wide = w_qkv.shape[0], w_qkv.shape[-1]

    def kernel(xl_hbm, xs_hbm, w_hbm, vec, bias, out, flat, four, w_v, local):
        copies = Copies(None, None, local)
        loads = load_tokens(copies, xl_hbm, xs_hbm, flat, four) + [copies.here(lambda: (w_hbm, w_v))]
        for copy in loads:
            copy.start()
        for copy in loads[:-1]:
            copy.wait()
        join_small(flat, four, large)

        def normed(start, size):
            at = pl.ds(start, size)
            hat, _ = norm_parts(flat[at, :].astype(F32))
            flat[at, :] = (hat * vec[0:1, :] + vec[4:5, :]).astype(BF)

        row_tiles(rows, 96, normed)
        loads[-1].wait()
        for u in range(panels):
            for c in range(2):
                cols = slice((c * panels + u) * wide, (c * panels + u + 1) * wide)
                got = dot(flat[...], w_v[u, c].reshape(width, wide), NN) + bias[:, cols]
                out[:, cols] = got.astype(BF)

    return pl.pallas_call(
        kernel,
        out_shape=jax.ShapeDtypeStruct((rows, 3 * width), BF),
        in_specs=[ANY] * 3 + [VMEM, VMEM],
        out_specs=VMEM,
        scratch_shapes=[pltpu.VMEM((rows, width), BF), pltpu.VMEM(x_s.shape, BF), pltpu.VMEM(w_qkv.shape, BF),
                        pltpu.SemaphoreType.DMA((4 * large + 2,))],
        compiler_params=pltpu.CompilerParams(vmem_limit_bytes=40 * MIB),
        name="project_in",
    )(x_l, x_s, w_qkv, vectors, merged_bias)


def head_columns(rows, at):
    return pl.BlockSpec((rows, 128), lambda g: (0, g + at))


def attend(qkv, rows_l, rows_s, large, small):
    rows = qkv.shape[0]
    return pl.pallas_call(
        functools.partial(attend_kernel, large, small),
        grid=(H // 2,),
        out_shape=jax.ShapeDtypeStruct((rows, 64 * H), BF),
        in_specs=[head_columns(rows, H // 2 * i) for i in range(3)]
        + [pl.BlockSpec((2, 8, WIDE_L), lambda g: (g, 0, 0)), pl.BlockSpec((2, 8, WIDE_S), lambda g: (g, 0, 0))],
        out_specs=head_columns(rows, 0),
        scratch_shapes=[pltpu.VMEM((2, LEN_L, LEN_L), F32), pltpu.VMEM((2, LEN_S, LEN_S), F32)],
        compiler_params=pltpu.CompilerParams(vmem_limit_bytes=56 * MIB),
        name="attend",
    )(qkv, qkv, qkv, rows_l, rows_s)


def layer_norm(values, gain, shift):
    average = jnp.mean(values, -1, keepdims=True)
    centered = values - average
    variance = jnp.mean(centered * centered, -1, keepdims=True)
    return centered * lax.rsqrt(variance + 1e-06) * gain + shift


def to_images(blocks):
    n = blocks.shape[0] // 4
    got = lax.all_to_all(blocks.reshape((4, n) + blocks.shape[1:]), "rows", 0, 0)
    return jnp.swapaxes(got, 0, 1)


def to_blocks(whole):
    got = lax.all_to_all(jnp.swapaxes(whole, 0, 1), "rows", 0, 0)
    return got.reshape((-1,) + got.shape[2:])


def to_panels(full, panels):
    rows, cols = full.shape
    split = full.reshape(4, 2, 2, rows // 16, 2, panels, cols // 2 // panels)
    return split.transpose(5, 4, 0, 1, 2, 3, 6)


def from_panels(split):
    rows, cols = 16 * split.shape[5], split.shape[0] * 2 * split.shape[6]
    return split.transpose(2, 3, 4, 5, 1, 0, 6).reshape(rows, cols)


CUTS = ((3, 1), (1, 1), (2, 1), (1, 3))


def on_device(img_size, small_images, large_images, w_qkv, w_out, w_up, w_down, gains, biases, up_bias,
              small_table, large_table, small_cotangent, large_cotangent):
    width = small_images.shape[2]
    axes = ("img", "rows")
    shards = [w_qkv, w_out, w_up, w_down]
    own = gains.shape[0]
    own_up = up_bias.shape[0]
    own_len = 10 * own + own_up
    block = jnp.concatenate([gains.T.reshape(-1), biases.T.reshape(-1), up_bias])
    block = jnp.pad(block, (0, 1024 - own_len)).reshape(8, 128)
    arrays = [large_images, small_images, large_cotangent, small_cotangent]
    direct = own % 8 == 0
    if direct:
        got = front(img_size, arrays, block, shards, CUTS)
        full = got[5:]
    else:
        got = [to_images(a) for a in arrays] + [lax.all_gather(block, axes, axis=0)]
        full = [to_panels(lax.all_gather(s.astype(BF), axes, axis=0, tiled=True), c[0]) for s, c in zip(shards, CUTS)]
    large_x, small_x, large_ct, small_ct = got[:4]
    blocks = got[4].reshape(-1, 1024).astype(BF).astype(F32)
    vectors = jnp.swapaxes(blocks[:, :10 * own].reshape(-1, 10, own), 0, 1).reshape(10, width)
    merged_bias = jnp.concatenate([vectors[6:7], jnp.zeros((1, width), F32), vectors[7:8]], 1)
    up_vec = blocks[:, 10 * own:own_len].reshape(-1, width)
    vectors = jnp.pad(vectors, ((0, 6), (0, 0)))
    qkv_w, out_w, up_w, down_w = full

    large, small = large_x.shape[0], small_x.shape[0]
    rows_l = table_rows(large_table, SIDE_L, 47, WIDE_L)
    rows_s = table_rows(small_table, SIDE_S, 29, WIDE_S)

    qkv = project_in(large_x, small_x, qkv_w, vectors, merged_bias)
    attended = attend(qkv, rows_l, rows_s, large, small)
    large_y, small_y, m, n2, e, g, dr, dy, sums = forward_tail(
        attended, large_x, small_x, large_ct, small_ct, out_w, up_w, down_w, vectors, up_vec)
    grad_out, grad_up, grad_down, dm, d_att, sums = backward_head(
        attended, m, n2, e, g, dr, dy, out_w, up_w, down_w, vectors, sums)
    if direct:
        df, large_sums, small_sums, *more = attention_back(
            img_size, qkv, d_att, rows_l, rows_s, [grad_down, grad_out, grad_up], [CUTS[i][1] for i in (3, 1, 2)],
            [large_y, small_y], large, small, 1)
        own_down, own_out, own_up_w, large_out, small_out = more
        large_grad, small_grad, own_qkv, sums, large_sums, small_sums = projection_back(
            img_size, df, dm, large_x, small_x, qkv_w, vectors, sums, [large_sums, small_sums], large, small)
    else:
        df, large_sums, small_sums = attention_back(img_size, qkv, d_att, rows_l, rows_s, [], [], [], large, small, 1)
        split_at = large * LEN_L
        tokens = jnp.concatenate([large_x.reshape(-1, width), small_x.reshape(-1, width)], 0).astype(F32)
        normed, pull = jax.vjp(layer_norm, tokens, vectors[0], vectors[4])
        grad_qkv = jnp.einsum("rd,re->de", normed.astype(BF), df, preferred_element_type=F32)
        d_normed = jnp.einsum("re,de->rd", df, from_panels(qkv_w), preferred_element_type=F32)
        d_tokens, grad_gain, grad_shift = pull(d_normed)
        d_tokens = (dm + d_tokens).astype(BF)
        grad_q = jnp.sum(df[:, :width].astype(F32), 0)
        grad_v = jnp.sum(df[:, 2 * width:].astype(F32), 0)
        for row, value in ((0, grad_gain), (4, grad_shift), (6, grad_q), (7, grad_v)):
            sums = sums.at[0, row].set(value)
        sums, large_sums, small_sums = lax.psum((sums, large_sums, small_sums), axes)
        large_grad = to_blocks(d_tokens[:split_at].reshape(large_x.shape))
        small_grad = to_blocks(d_tokens[split_at:].reshape(small_x.shape))
        large_out, small_out = to_blocks(large_y), to_blocks(small_y)
        grads = [grad_qkv] + [from_panels(g).astype(F32) for g in (grad_out, grad_up, grad_down)]
        own_qkv, own_out, own_up_w, own_down = [
            lax.psum_scatter(g, axes, scatter_dimension=0, tiled=True) for g in grads]

    index = lax.axis_index("img") * 4 + lax.axis_index("rows")
    flat_sums = sums.reshape(16, width)
    own_columns = lax.dynamic_slice(flat_sums, (0, index * own), (10, own)).T
    own_up_sums = lax.dynamic_slice(flat_sums[10:14].reshape(-1), (index * own_up,), (own_up,))
    grad_large_table = table_sums(large_sums[:, :12].reshape(H, 2, WIDE_L), SIDE_L, 47)
    grad_small_table = table_sums(small_sums[:, :12].reshape(H, 2, WIDE_S), SIDE_S, 29)
    return (
        small_out, large_out, small_grad, large_grad, own_qkv, own_out, own_up_w, own_down,
        own_columns[:, :4], own_columns[:, 4:], own_up_sums, grad_small_table, grad_large_table,
    )


def solution(mesh):
    images = P("img", "rows", None)
    matrix = P(("img", "rows"), None)
    vector = P(("img", "rows"))
    in_specs = (images, images) + (matrix,) * 6 + (vector, P(), P(), images, images)
    out_specs = (images,) * 4 + (matrix,) * 6 + (vector, P(), P())
    return jax.shard_map(
        functools.partial(on_device, mesh.shape["img"]),
        mesh=mesh, in_specs=in_specs, out_specs=out_specs, check_vma=False,
    )
```

time: 637 us -> 524 us (0.82)
  matrix products: 163 us -> 0 us
  Pallas kernels: 372 us -> 480 us
  local copies, waits for them, and re-layouts: 67.1 us -> 36.7 us
  other arithmetic: 24.9 us -> 0.98 us
    dot_general x12 -> x0, matrix products: 163 us -> none  [the longest x1 48.5 us: on_device(): hidden = jnp.dot(normed_mid, up_low, preferred_element_type=F32) + up_vec]
    pallas_call x2 -> x5, Pallas kernels: 197 us -> 313 us  [the longest x1 115 us: attention_back(): pl.pallas_call(kernel, out_shape=[jax.ShapeDtypeStruct(qkv.shape, BF), ja...]
    reduce_sum x9 -> x0, other arithmetic: 19.7 us -> none  [the longest x1 7.32 us: on_device(): grad_scale_one = jnp.sum(branch * d_middle, 0)]
    slice x23 -> x8, local copies, waits for them, and re-layouts: 11.9 us -> 1.15 us  [the longest x1 0.74 us: on_device(): flat_sums[10:14].reshape(-1)]
    unnamed x146 -> x70, local copies, waits for them, and re-layouts: 28.9 us -> 20.4 us
    pallas_call x1, Pallas kernels: 144 us -> 137 us  [front(): pl.pallas_call(kernel, out_shape=outs, in_specs=[ANY] * (na + 1 + nw), ou...]
where the time goes in v2:
time: 524 us; the launch traced here: 519 us
  Pallas kernels  480 us (92%)
  local copies, waits for them, and re-layouts  36.7 us (7%)
    pallas_call x1, Pallas kernels, front(): pl.pallas_call(kernel, out_shape=outs, in_specs=[ANY] * (na + 1 + nw), ou...  137 us
    pallas_call x1, Pallas kernels, attention_back(): pl.pallas_call(kernel, out_shape=[jax.ShapeDtypeStruct(qkv.shape, BF), ja...  115 us
    pallas_call x1, Pallas kernels, projection_back(): pl.pallas_call(kernel, out_shape=[jax.ShapeDtypeStruct((4 * a.shape[0],)...  77.8 us
    pallas_call x1, Pallas kernels, backward_head(): pl.pallas_call(kernel, out_shape=[bf(*w_out.shape), bf(*w_up.shape), bf(*...  56.2 us
    pallas_call x1, Pallas kernels, forward_tail(): pl.pallas_call(kernel, out_shape=[bf(*x_l.shape), bf(*x_s.shape), jax.Sha...  51.1 us
    pallas_call x1, Pallas kernels, attend(): pl.pallas_call(functools.partial(attend_kernel, large, small), grid=(H //...  30.3 us
    unnamed x70, local copies, waits for them, and re-layouts  20.4 us
    pallas_call x1, Pallas kernels, project_in(): pl.pallas_call(kernel, out_shape=jax.ShapeDtypeStruct((rows, 3 * width),...  12.9 us

profile of v2, /device:TPU:0, one launch (start us, length us, event | category | flops | bytes accessed | tf_op | source)
XLA Modules:
  0.0 519.1 jit_solution(4537571089052642062)
XLA Ops:
  0.6 1.0 reshape.115
  1.7 0.1 fusion.5
  1.8 0.2 slice.189
  2.2 0.2 reshape.136
  2.5 0.1 fusion.6
  2.6 0.2 slice.185
  2.9 0.2 reshape.135
  3.4 0.2 reshape.134
  3.8 0.2 reshape.133
  4.2 0.9 concatenate.65.rows_s.refs_3_
  5.4 1.5 copy-done.7
  6.9 1.5 copy-done.8
  8.3 0.9 copy-done.15
  9.3 137.1 %front.1 = (bf16[2,4,144,768]{3,2,1,0:T(8,128)(2,1)S(1)}, bf16[1,4,56,768]{3,2,1,0:T(8,128)(2,1)S(1)}, bf16[2,4,144,768]{3,2,1,0:T(8,128)(2,1)S(1)}, bf16[1,4,56...) custom-call(bf16[8,144,768]{2,1,0:T(8,128)(2,1)S(1)} %copy-done.7, ...), custom_call_target="tpu_custom_call" | custom-call | tf_op jit(solution)/shard_map/front/pallas_call | solution.py:513
  146.4 1.8 copy-done.2
  148.2 1.0 copy-done.4
  149.2 1.2 copy-done.6
  150.4 0.7 copy-done.12
  151.8 0.1 reshape.109
  152.0 2.0 copy-done.3
  154.0 12.9 %project_in.1.q_ref.k_ref.v_ref.refs_0_ = bf16[1376,2304]{1,0:T(8,128)(2,1)S(1)} custom-call(bf16[2,4,144,768]{3,2,1,0:T(8,128)(2,1)S(1)} %get-tuple-element.51.xl_hbm.refs_2_, bf16[1,4,56,768]{3,2,1,0:T(8,128)(2,1)S(1)} %get-tuple-element.52.xs_hbm.refs_3_, bf16[3,2,4,2,2,48,384]{6,5,4,3,2,1,0:T(8,128)(2,1)S(1)} %copy-done.3, ...), custom_call_target="tpu_custom_call" | custom-call | tf_op jit(solution)/shard_map/project_in/pallas_call | solution.py:1280
  166.9 2.7 copy-done
  169.6 0.2 reshape.110
  169.8 0.1 fusion.4
  169.9 0.3 slice.170
  170.3 0.2 reshape.131
  170.5 0.2 slice.215
  170.7 0.1 fusion.3
  170.8 0.3 slice.174
  171.2 0.2 reshape.132
  171.4 0.2 slice.218
  171.6 0.1 pad_maximum_fusion.5
  171.8 0.2 reshape.129
  172.0 0.2 slice.209
  172.2 0.2 reshape.130
  172.4 0.2 slice.212
  172.7 0.1 pad_maximum_fusion.3
  172.8 1.1 concatenate.59.rows_l.refs_2_
  174.0 30.3 %attend.1.att_hbm = bf16[1376,768]{1,0:T(8,128)(2,1)} custom-call(bf16[1376,2304]{1,0:T(8,128)(2,1)} %copy-done, bf16[1376,2304]{1,0:T(8,128)(2,1)} %copy-done, bf16[1376,2304]{1,0:T(8,128)(2,1)} %copy-done, f32[12,8,1152]{2,1,0:T(8,128)} %concatenate.59.rows_l.refs_2_, f32[12,8,512]{2,1,0:T(8,128)} %concatenate.65.rows_s.refs_3_), custom_call_target="tpu_custom_call" | custom-call | tf_op jit(solution)/shard_map/attend/pallas_call | solution.py:1298
  204.3 0.7 reshape.120.upv
  205.0 51.1 %forward_tail.1 = (bf16[2,4,144,768]{3,2,1,0:T(8,128)(2,1)}, bf16[1,4,56,768]{3,2,1,0:T(8,128)(2,1)}, f32[1376,768]{1,0:T(8,128)}, bf16[1376,768]{1,0:T(8,128)(2...) custom-call(bf16[1376,768]{1,0:T(8,128)(2,1)} %attend.1.att_hbm, ...), custom_call_target="tpu_custom_call" | custom-call | tf_op jit(solution)/shard_map/forward_tail/pallas_call | solution.py:1089
  256.1 56.2 %backward_head.1 = (bf16[1,2,4,2,2,48,384]{6,5,4,3,2,1,0:T(8,128)(2,1)}, bf16[2,2,4,2,2,48,768]{6,5,4,3,2,1,0:T(8,128)(2,1)}, bf16[1,2,4,2,2,192,384]{6,5,4,3,2,...) custom-call(bf16[1376,768]{1,0:T(8,128)(2,1)} %attend.1.att_hbm, ...), custom_call_target="tpu_custom_call" | custom-call | tf_op jit(solution)/shard_map/backward_head/pallas_call | solution.py:1235
  312.3 114.6 %attention_back.1 = (bf16[1376,2304]{1,0:T(8,128)(2,1)}, f32[2,16,1152]{2,1,0:T(8,128)}, f32[2,16,512]{2,1,0:T(8,128)}, f32[96,768]{1,0:T(8,128)}, f32[24,768]{1...) custom-call(bf16[1376,2304]{1,0:T(8,128)(2,1)} %copy-done, ...), custom_call_target="tpu_custom_call" | custom-call | tf_op jit(solution)/shard_map/attention_back/pallas_call | solution.py:740
  426.9 77.8 %projection_back.1 = (bf16[8,144,768]{2,1,0:T(8,128)(2,1)}, bf16[4,56,768]{2,1,0:T(8,128)(2,1)}, f32[24,2304]{1,0:T(8,128)}, f32[2,8,768]{2,1,0:T(8,128)}, f32[2...) custom-call(bf16[1376,2304]{1,0:T(8,128)(2,1)} %get-tuple-element.75.refs_0_, f32[1376,768]{1,0:T(8,128)} %get-tuple-element.76.refs_1_, ...), custom_call_target="tpu_custom_call" | custom-call | tf_op jit(solution)/shard_map/projection_back/pallas_call | solution.py:935
  504.7 1.3 reshape.126
  506.1 0.1 pad_maximum_fusion
  506.2 0.8 reshape.127
  507.2 0.4 reshape.124
  507.7 0.1 slice_maximum_fusion
  508.0 0.8 reshape.125
  508.7 0.7 slice.232
  509.5 0.6 dynamic_slice.7
  510.1 0.8 dynamic-slice_bitcast_fusion
  510.8 0.6 slice.231
  511.4 0.6 slice.230
  512.0 0.7 copy.60
  512.8 1.2 copy.61
  514.0 0.7 copy.62
  514.7 0.2 copy-done.18
  514.9 1.2 copy.63
  516.1 0.7 copy.64
  516.8 0.6 copy.65
  517.4 0.7 copy.66
  518.2 0.7 copy.67
  (104 shorter events, 2.4 us)
Async XLA Ops:
  2.1 3.0 copy-start.27
  2.1 3.1 copy-start.28
  2.1 3.2 copy-start.29
  2.1 3.2 copy-start.10
  2.1 3.2 copy-start.11
  2.1 3.2 copy-start.13
  2.1 3.2 copy-start.14
  2.2 3.2 copy-start.16
  5.4 1.5 copy-start.7
  6.9 1.5 copy-start.8
  8.3 0.9 copy-start.15
  146.3 1.8 copy-start.2
  148.2 1.0 copy-start.4
  149.2 1.2 copy-start.6
  150.4 0.7 copy-start.12
  151.1 15.7 %copy-start.1 = (bf16[2,4,144,768]{3,2,1,0:T(8,128)(2,1)}, bf16[2,4,144,768]{3,2,1,0:T(8,128)(2,1)S(1)}, u32[]{:S(2)}) copy-start(bf16[2,4,144,768]{3,2,1,0:T(8,128)(2,1)S(1)} %get-tuple-element.51.xl_hbm.refs_2_) | copy-start | bytes 5308420
  151.1 15.7 %copy-start.5 = (bf16[1,4,56,768]{3,2,1,0:T(8,128)(2,1)}, bf16[1,4,56,768]{3,2,1,0:T(8,128)(2,1)S(1)}, u32[]{:S(2)}) copy-start(bf16[1,4,56,768]{3,2,1,0:T(8,128)(2,1)S(1)} %get-tuple-element.52.xs_hbm.refs_3_) | copy-start | bytes 1032196
  152.0 14.9 %copy-start.9 = (f32[16,768]{1,0:T(8,128)}, f32[16,768]{1,0:T(8,128)S(1)}, u32[]{:S(2)}) copy-start(f32[16,768]{1,0:T(8,128)S(1)} %pad.50.vec.refs_5_) | copy-start | bytes 147460
  152.0 2.0 copy-start.3
  154.0 15.6 %copy-start.24 = (f32[12,2209]{1,0:T(8,128)S(1)}, f32[12,2209]{1,0:T(8,128)}, u32[]{:S(2)}) copy-start(f32[12,2209]{1,0:T(8,128)} %param.23) | copy-start | bytes 318100
  166.9 2.7 copy-start
  504.7 2.4 copy-start.26
  506.1 6.0 %copy-start.19 = (bf16[4,56,768]{2,1,0:T(8,128)(2,1)S(1)}, bf16[4,56,768]{2,1,0:T(8,128)(2,1)}, u32[]{:S(2)}) copy-start(bf16[4,56,768]{2,1,0:T(8,128)(2,1)} %get-tuple-element.120) | copy-start | bytes 1032196
  506.2 6.5 %copy-start.17 = (bf16[8,144,768]{2,1,0:T(8,128)(2,1)S(1)}, bf16[8,144,768]{2,1,0:T(8,128)(2,1)}, u32[]{:S(2)}) copy-start(bf16[8,144,768]{2,1,0:T(8,128)(2,1)} %get-tuple-element.121) | copy-start | bytes 5308420
  512.0 1.9 copy-start.20
  512.8 2.1 copy-start.18
  514.0 2.1 copy-start.23
  514.9 1.9 copy-start.25
  514.9 2.5 copy-start.22
  514.9 3.3 copy-start.21

commit v3 on v2

--- a/solution.py
+++ b/solution.py
@@ -134,9 +134,8 @@
     def __init__(self, place, copies, shard, full, both, low, pieces):
         self.p, self.copies = place, copies
         self.full, self.both, self.low = full, both, low
-        self.k, self.cols = shard.shape
-        self.half = self.cols // 2
         self.panels, self.wide = full.shape[0], full.shape[-1]
+        self.k, self.half = full.shape[5] // 2, self.panels * self.wide
         self.tall = 2 * self.k // pieces
         self.pieces = pieces
         p = place
@@ -144,9 +143,10 @@
         def mine():
             return both.at[pl.ds(pl.multiple_of(p.c * self.k, 8), self.k)]
 
-        self.kept = copies.here(lambda: (shard.at[:, columns(p.c * self.half, self.half)], mine()))
-        self.swapped = copies.remote(
-            lambda: (shard.at[:, columns((1 - p.c) * self.half, self.half)], mine(), p.at(c=1 - p.c)))
+        if shard is not None:
+            self.kept = copies.here(lambda: (shard.at[:, columns(p.c * self.half, self.half)], mine()))
+            self.swapped = copies.remote(
+                lambda: (shard.at[:, columns((1 - p.c) * self.half, self.half)], mine(), p.at(c=1 - p.c)))
 
     def exchange(self):
         self.kept.start()
@@ -157,56 +157,76 @@
         self.swapped.wait_recv()
         self.low[...] = self.both[...].astype(BF)
 
-    def unit(self, u, r):
-        p, full = self.p, self.full
+    def over_z(self, u, r):
+        p = self.p
         rows = pl.ds(r * self.tall, self.tall)
         src = self.low.at[rows, pl.ds(u * self.wide, self.wide)]
 
         def dst():
-            return full.at[u, p.c, p.z, p.x, p.y, rows]
-
-        def twice(part, device):
-            return self.copies.remote(lambda: (part(), part(), device()))
+            return self.full.at[u, p.c, p.z, p.x, p.y, rows]
 
         own = self.copies.here(lambda: (src, dst()))
-        over_z = [
-            self.copies.remote(lambda s=s: (src, dst(), p.at(z=p.z_other(s)))) for s in range(1, p.zs)
-        ]
-        over_y = twice(lambda: full.at[u, p.c, :, p.x, p.y, rows], lambda: p.at(y=1 - p.y))
-        over_x = twice(lambda: full.at[u, p.c, :, p.x, :, rows], lambda: p.at(x=1 - p.x))
-        over_c = twice(lambda: full.at[u, p.c, :, :, :, rows], lambda: p.at(c=1 - p.c))
-
-        def along_z():
+        sent = [self.copies.remote(lambda s=s: (src, dst(), p.at(z=p.z_other(s)))) for s in range(1, p.zs)]
+
+        def start():
             if u == 0 and r == 0:
                 self.convert()
-            for copy in [own] + over_z:
+            for copy in [own] + sent:
                 copy.start()
 
-        def along_y():
+        def wait():
             own.wait()
-            for copy in over_z:
+            for copy in sent:
                 copy.wait_recv()
-            over_y.start()
-
-        def along_x():
-            over_y.wait_recv()
-            over_x.start()
-
-        def along_c():
-            over_x.wait_recv()
-            over_c.start()
-
-        def finish():
-            over_c.wait_recv()
-            for copy in over_z + [over_y, over_x, over_c]:
+            for copy in sent:
                 copy.wait_send()
             if u == 0 and r == 0:
                 self.swapped.wait_send()
 
-        return [along_z, along_y, along_x, along_c, finish]
-
-    def units(self):
-        return [self.unit(u, r) for u in range(self.panels) for r in range(self.pieces)]
+        return [start, wait]
+
+    def over_yx(self, u, r, x_first=False):
+        p, full = self.p, self.full
+        rows = pl.ds(r * self.tall, self.tall)
+        one = lambda: full.at[u, p.c, :, p.x, p.y, rows]
+        if x_first:
+            first = self.twice(one, lambda: p.at(x=1 - p.x))
+            second = self.twice(lambda: full.at[u, p.c, :, :, p.y, rows], lambda: p.at(y=1 - p.y))
+        else:
+            first = self.twice(one, lambda: p.at(y=1 - p.y))
+            second = self.twice(lambda: full.at[u, p.c, :, p.x, :, rows], lambda: p.at(x=1 - p.x))
+        third = self.twice(lambda: full.at[u, p.c, :, :, :, rows], lambda: p.at(c=1 - p.c))
+
+        def next_(before, after):
+            before.wait_recv()
+            after.start()
+
+        def finish():
+            third.wait_recv()
+            for copy in (first, second, third):
+                copy.wait_send()
+
+        return [first.start, functools.partial(next_, first, second), functools.partial(next_, second, third), finish]
+
+    def unit(self, u, r, x_first=False):
+        start, wait = self.over_z(u, r)
+        after = self.over_yx(u, r, x_first)
+
+        def second():
+            wait()
+            after[0]()
+
+        return [start, second] + after[1:]
+
+    def twice(self, part, device):
+        return self.copies.remote(lambda: (part(), part(), device()))
+
+    def units(self, kind=None, x_first=()):
+        if kind is not None:
+            return [kind(u, r) for u in range(self.panels) for r in range(self.pieces)]
+        return [
+            self.unit(u, r, u * self.pieces + r in x_first) for u in range(self.panels) for r in range(self.pieces)
+        ]
 
     @staticmethod
     def scratch(shape):
@@ -481,45 +501,6 @@
 def full_shape(img_size, shard, panels):
     k, cols = shard.shape
     return (panels, 2, img_size // 2, 2, 2, 2 * k, cols // 2 // panels)
-
-
-def front(img_size, arrays, block, shards, cuts):
-    na, nw = len(arrays), len(shards)
-    zs = img_size // 2
-    outs = [jax.ShapeDtypeStruct((a.shape[0] // 4, 4) + a.shape[1:], a.dtype) for a in arrays]
-    outs += [jax.ShapeDtypeStruct((zs, 2, 2, 2, 8, 128), F32)]
-    outs += [jax.ShapeDtypeStruct(full_shape(img_size, s, c[0]), BF) for s, c in zip(shards, cuts)]
-
-    def kernel(*refs):
-        ins, blk, sh, whole, small, full, scr = split_refs(refs, na, 1, nw, na, 1, nw)
-        p = Place(img_size)
-        greet(p.partners())
-        copies = Copies(*scr[-3:])
-        gathers = [Gather(p, copies, sh[i], full[i], scr[2 * i], scr[2 * i + 1], cuts[i][1]) for i in range(nw)]
-        moves = [Move(p, copies, a, b, True) for a, b in zip(ins, whole)]
-        for g in gathers:
-            g.exchange()
-        for m in moves:
-            m.start()
-        units = Spread(p, copies, blk[0], small[0]).units()
-        for g in gathers:
-            units += g.units()
-        for step in pipelined(units):
-            step()
-        for m in moves:
-            m.finish()
-
-    count = sum(a * b for a, b in cuts)
-    return pl.pallas_call(
-        kernel,
-        out_shape=outs,
-        in_specs=[ANY] * (na + 1 + nw),
-        out_specs=[ANY] * len(outs),
-        scratch_shapes=[s for w in shards for s in Gather.scratch(w.shape)]
-        + semaphores(3 * na + (zs + 2) * (1 + count) + nw, na + 1 + nw + count),
-        compiler_params=pltpu.CompilerParams(collective_id=0, has_side_effects=True, vmem_limit_bytes=40 * MIB),
-        name="front",
-    )(*arrays, block, *shards)
 
 
 def table_rows(table, side, blocks, wide):
@@ -799,7 +780,7 @@
         flat[at:at + LEN_S, :] = rows.astype(flat.dtype)
 
 
-def projection_back(img_size, df, dm, x_l, x_s, w_qkv, vectors, sums, tables, large, small):
+def projection_back(img_size, df, dm, n1, x_l, x_s, w_qkv, vectors, sums, tables, large, small):
     zs = img_size // 2
     rows, width = dm.shape
     panels, _, _, _, _, k2, wide = w_qkv.shape
@@ -807,17 +788,17 @@
     nt = len(tables)
 
     def kernel(*refs):
-        ins, tabs, outs, tab_outs, scr = split_refs(refs, 7, nt, 4, nt)
-        df_hbm, dm_hbm, xl_hbm, xs_hbm, w_hbm, vec, sums_in = ins
+        ins, tabs, outs, tab_outs, scr = split_refs(refs, 8, nt, 4, nt)
+        df_hbm, dm_hbm, n1_hbm, xl_hbm, xs_hbm, w_hbm, vec, sums_in = ins
         gl_out, gs_out, shard, sums_out = outs
-        df_v, dm_v, flat, four, w_v, nt_v, dn, acc, own_sums, dl, ds = scr[:11]
-        at = 11
+        df_v, dm_v, flat, four, w_v, n1_v, nt_v, dn, acc, own_sums, dl, ds, grad = scr[:13]
+        at = 13
         p = Place(img_size)
         copies = Copies(*scr[-3:])
-        x_loads = load_tokens(copies, xl_hbm, xs_hbm, flat, four)
-        df_load = copies.here(lambda: (df_hbm, df_v))
-        later = [copies.here(lambda: (w_hbm, w_v)), copies.here(lambda: (dm_hbm, dm_v))]
-        for copy in x_loads + [df_load] + later:
+        first = [copies.here(lambda: (n1_hbm, n1_v)), copies.here(lambda: (df_hbm, df_v))]
+        w_load = copies.here(lambda: (w_hbm, w_v))
+        later = load_tokens(copies, xl_hbm, xs_hbm, flat, four) + [copies.here(lambda: (dm_hbm, dm_v))]
+        for copy in first + [w_load] + later:
             copy.start()
         greet(p.partners())
         scatter = Scatter(p, copies, None, shard, scr[at:at + 7], 1)
@@ -828,54 +809,41 @@
             at += 3
         last = Total(p, copies, own_sums, sums_out, *scr[at:at + 3])
         moves = [Move(p, copies, dl, gl_out, False), Move(p, copies, ds, gs_out, False)]
-        for t in totals:
-            t.along_c()
-        for copy in x_loads:
+        units = scatter.units()
+        first[0].wait()
+        nt_v[...] = n1_v[...].T
+        first[1].wait()
+
+        def pair(ref, u):
+            return jnp.concatenate(
+                [ref[:, c * (cols // 2) + u * wide:c * (cols // 2) + (u + 1) * wide] for c in range(2)], 1)
+
+        def gradient(u):
+            grad[...] = dot(nt_v[...], pair(df_v, u), NN).astype(BF)
+            for to, c in ((scatter.stage, 1 - p.c), (scatter.own, p.c)):
+                to[u] = grad[:, columns(c * wide, wide)].reshape(zs, 2, 2, k2, wide)
+            units[u][0]()
+
+        def all_totals(phase):
+            for t in totals:
+                phase(t)
+
+        gradient(0)
+        all_totals(Total.along_c)
+        w_load.wait()
+        for u in range(panels):
+            w = jnp.concatenate([w_v[u, c].reshape(width, wide) for c in range(2)], 1)
+            got = dot(pair(df_v, u), w, NT)
+            dn[...] = got if u == 0 else dn[...] + got
+            if u == 0:
+                units[0][1]()
+                all_totals(Total.along_x)
+        for copy in later:
             copy.wait()
         join_small(flat, four, large)
-        gain, shift = vec[0:1, :], vec[4:5, :]
-
-        def normed(start, size):
-            hat, _ = norm_parts(flat[pl.ds(start, size), :].astype(F32))
-            n1_v[pl.ds(start, size), :] = (hat * gain + shift).astype(BF)
-
-        n1_v = scr[-4]
-        row_tiles(rows, 96, normed)
-        nt_v[...] = n1_v[...].T
-        df_load.wait()
-        units = scatter.units()
-        for t in totals:
-            t.along_x()
-        for u in range(panels):
-            def part(c):
-                cols_ = columns(c * (cols // 2) + u * wide, wide)
-                got = dot(nt_v[...], df_v[:, cols_], NN).astype(BF)
-                return got.reshape(zs, 2, 2, k2, wide)
-            scatter.stage[u] = part(1 - p.c)
-            units[u][0]()
-            scatter.own[u] = part(p.c)
-            if u >= 1:
-                units[u - 1][1]()
-            if u >= 2:
-                units[u - 2][2]()
-            if u == 1:
-                for t in totals:
-                    t.along_y()
-            if u == 2:
-                for t in totals:
-                    t.along_z()
-        for copy in later:
-            copy.wait()
-        for u in range(panels):
-            for c in range(2):
-                cols_ = slice(c * (cols // 2) + u * wide, c * (cols // 2) + (u + 1) * wide)
-                w = w_v[u, c].reshape(width, wide)
-                got = dot(df_v[:, cols_], w, NT)
-                dn[...] = got if u == 0 and c == 0 else dn[...] + got
-            if u == 0:
-                units[panels - 1][1]()
-                units[panels - 2][2]()
         acc[...] = jnp.zeros_like(acc)
+        gain = vec[0:1, :]
+        units[0][2]()
 
         def back(start, size):
             at_rows = pl.ds(start, size)
@@ -885,16 +853,16 @@
             acc[1] += fold8(d)
             acc[2] += fold8(df_v[at_rows, :width].astype(F32))
             acc[3] += fold8(df_v[at_rows, 2 * width:].astype(F32))
-            dm_v[at_rows, :] = dm_v[at_rows, :] + norm_back(d, hat, scale, gain)
+            flat[at_rows, :] = (dm_v[at_rows, :] + norm_back(d, hat, scale, gain)).astype(BF)
 
         row_tiles(rows, 96, back)
         for i in range(large):
             for j in range(4):
                 start = (i * 4 + j) * (LEN_L // 4)
-                dl[i, j] = dm_v[start:start + LEN_L // 4, :].astype(BF)
+                dl[i, j] = flat[start:start + LEN_L // 4, :]
         for n in range(small):
             start = large * LEN_L + n * LEN_S
-            place_small(ds, dm_v[start:start + LEN_S, :], n)
+            place_small(ds, flat[start:start + LEN_S, :].astype(F32), n)
         for m in moves:
             m.start()
         for i, row in ((0, 0), (1, 4), (2, 6), (3, 7)):
@@ -903,45 +871,228 @@
             own_sums[0, row:row + 1, :] = sums_in[0, row:row + 1, :]
         own_sums[1] = sums_in[1]
         last.along_c()
-        units[panels - 1][2]()
-        for f in (3, 4):
-            for u in range(panels):
-                units[u][f]()
-            if f == 3:
-                last.along_x()
-                for t in totals:
-                    t.finish()
+        for u in range(1, panels):
+            gradient(u)
+        all_totals(Total.along_y)
+        units[1][1]()
+        units[2][1]()
+        units[0][3]()
+        last.along_x()
+        all_totals(Total.along_z)
+        units[1][2]()
         last.along_y()
+        units[0][4]()
+        units[2][2]()
+        units[1][3]()
         last.along_z()
+        all_totals(Total.finish)
+        units[2][3]()
+        units[1][4]()
         last.finish()
+        units[2][4]()
         scatter.end()
         for t in totals + [last]:
             t.end()
         for m in moves:
             m.finish()
 
+    flat = pltpu.VMEM((rows, width), BF)
     scratch = [
-        pltpu.VMEM(df.shape, BF), pltpu.VMEM(dm.shape, F32), pltpu.VMEM((rows, width), BF),
-        pltpu.VMEM(x_s.shape, BF), pltpu.VMEM(w_qkv.shape, BF), pltpu.VMEM((width, rows), BF),
-        pltpu.VMEM((rows, width), F32), pltpu.VMEM((4, 8, width), F32), pltpu.VMEM((2, 8, width), F32),
-        pltpu.VMEM(x_l.shape, BF), pltpu.VMEM(x_s.shape, BF),
+        pltpu.VMEM(df.shape, BF), pltpu.VMEM(dm.shape, F32), flat, pltpu.VMEM(x_s.shape, BF),
+        pltpu.VMEM(w_qkv.shape, BF), flat, pltpu.VMEM((width, rows), BF), pltpu.VMEM((rows, width), F32),
+        pltpu.VMEM((4, 8, width), F32), pltpu.VMEM((2, 8, width), F32),
+        pltpu.VMEM(x_l.shape, BF), pltpu.VMEM(x_s.shape, BF), pltpu.VMEM((width, 2 * wide), BF),
     ] + Scatter.scratch(zs, k, cols, panels, 1, True)
     for t in list(tables) + [sums]:
         scratch += Total.scratch(zs, t.shape[1], t.shape[2])
-    scratch += [pltpu.VMEM((rows, width), BF)]
     remotes = 6 + Scatter.remotes(zs, panels, 1) + Total.remotes(zs) * (nt + 1)
-    locals_ = 4 * x_l.shape[0] + 1 + 3 + 2 + 1 + 2 * (nt + 1)
+    locals_ = 4 * x_l.shape[0] + 1 + 4 + 2 + 1 + 2 * (nt + 1)
     f32 = lambda s: jax.ShapeDtypeStruct(s, F32)
     return pl.pallas_call(
         kernel,
         out_shape=[jax.ShapeDtypeStruct((4 * a.shape[0],) + a.shape[2:], BF) for a in (x_l, x_s)]
         + [f32((k, cols)), f32(sums.shape)] + [f32(t.shape) for t in tables],
-        in_specs=[ANY] * 5 + [VMEM, VMEM] + [ANY] * nt,
+        in_specs=[ANY] * 6 + [VMEM, VMEM] + [ANY] * nt,
         out_specs=[ANY] * (4 + nt),
         scratch_shapes=scratch + semaphores(remotes, locals_),
         compiler_params=pltpu.CompilerParams(collective_id=2, has_side_effects=True, vmem_limit_bytes=60 * MIB),
         name="projection_back",
-    )(df, dm, x_l, x_s, w_qkv, vectors, sums, *tables)
+    )(df, dm, n1, x_l, x_s, w_qkv, vectors, sums, *tables)
+
+
+def attend_pair(hp, qkv, bias_l, bias_s, out, large, small, between):
+    mask = lax.broadcasted_iota(jnp.int32, (1, 128), 1) < 64
+    keep = lax.broadcasted_iota(jnp.int32, (1, LEN_S), 1) < SIDE_S * SIDE_S
+    images = [(n * LEN_L, LEN_L, bias_l) for n in range(large)]
+    images += [(large * LEN_L + n * LEN_S, LEN_S, bias_s) for n in range(small)]
+    cols = [columns(i * 64 * H + hp * 128, 128) for i in range(3)]
+    between(0)
+    for at, size, bias in images:
+        rows = slice(at, at + size)
+        q, k, v = (qkv[rows, c] for c in cols)
+        outs = []
+        for h in range(2):
+            s = dot(head_part(q, mask, h) * BF(0.125), k, NT) + bias[2 * hp + h]
+            if size == LEN_S:
+                s = jnp.where(keep, s, -1e30)
+            e = jnp.exp(s - jnp.max(s, 1, keepdims=True))
+            outs.append(dot(e.astype(BF), v, NN) * (1.0 / jnp.sum(e, 1, keepdims=True)))
+        out[rows, cols[0]] = jnp.where(mask, outs[0], outs[1]).astype(BF)
+
+
+def fill_heads(start, stop, rows_l, rows_s, bias_l, bias_s):
+    lower_l = lower_offsets(SIDE_L, SIDE_L, WIDE_L)
+    lower_s = lower_offsets(SIDE_S, 16, WIDE_S)
+
+    def body(h, carry):
+        fill_bias(bias_l, h, spread_rows(rows_l, h, 2, SIDE_L, SIDE_L, WIDE_L, lower_l), SIDE_L, 24, 23)
+        fill_bias(bias_s, h, spread_rows(rows_s, h, 2, SIDE_S, 16, WIDE_S, lower_s), SIDE_S, 16, 15)
+        return carry
+
+    lax.fori_loop(start, stop, body, 0)
+
+
+def assemble(blocks, count, vectors, up_vec):
+    row = lax.broadcasted_iota(jnp.int32, (16, 128), 0)
+    vectors[...] = jnp.zeros_like(vectors)
+    up_vec[...] = jnp.zeros_like(up_vec)
+    width = vectors.shape[1] - 128
+    own, own_up = width // count, 4 * width // count
+
+    def shifted(part, offset):
+        part = jnp.concatenate([part, jnp.zeros_like(part)], 1)
+        return pltpu.roll(part, offset % 128, 1) if offset % 128 else part
+
+    for d in range(count):
+        block = blocks[d].astype(BF).astype(F32)
+        offset = d * own
+        base = offset // 128 * 128
+        vectors[:, base:base + 256] += shifted(jnp.where(row < 10, block, 0.0), offset)
+        at, offset = d * own_up // width, d * own_up % width
+        base = offset // 128 * 128
+        up_vec[at:at + 1, base:base + 256] += shifted(block[10:11], offset)
+
+
+def front(img_size, arrays, block, shards, cuts, firsts, rows_l, rows_s):
+    na, nw = len(arrays), len(shards)
+    zs = img_size // 2
+    large, small = arrays[0].shape[0] // 4, arrays[1].shape[0] // 4
+    width = arrays[0].shape[2]
+    rows = large * LEN_L + small * LEN_S
+    count = 4 * img_size
+    whole_shapes = [(a.shape[0] // 4, 4) + a.shape[1:] for a in arrays]
+    full_shapes = [full_shape(img_size, s, c[0]) for s, c in zip(shards, cuts)]
+    panels, wide = cuts[0][0], full_shapes[0][-1]
+
+    def kernel(*refs):
+        ins, blk, sh, tabs, whole, full, outs, scr = split_refs(refs, na, 1, nw, 2, na, nw, 5)
+        qkv_hbm, n1_hbm, att, vec_out, up_out = outs
+        flat, four, w_v, qkv, bias_l, bias_s, small_v, vectors, up_vec = scr[:9]
+        gather_scr = scr[9:9 + 2 * nw]
+        p = Place(img_size)
+        greet(p.partners())
+        copies = Copies(*scr[-3:])
+        gathers = [
+            Gather(p, copies, sh[i], full[i], gather_scr[2 * i], gather_scr[2 * i + 1], cuts[i][1]) for i in range(nw)
+        ]
+        moves = [Move(p, copies, a, b, True) for a, b in zip(ins, whole)]
+        gathers[0].exchange()
+        first = Spread(p, copies, blk[0], small_v).units() + gathers[0].units()
+        rest = []
+        for g, x_first in zip(gathers[1:-1], firsts):
+            rest += g.units(None, x_first)
+        last = gathers[-1].units(gathers[-1].over_z)
+        steps = pipelined(rest + last)
+        fill = functools.partial(fill_heads, rows_l=tabs[0], rows_s=tabs[1], bias_l=bias_l, bias_s=bias_s)
+        for unit in first:
+            unit[0]()
+        for g in gathers[1:]:
+            g.exchange()
+        fill(0, 4)
+        for unit in first:
+            unit[1]()
+        for m in moves:
+            m.start()
+        steps[0]()
+        fill(4, 8)
+        for unit in first:
+            unit[2]()
+        steps[1]()
+        fill(8, 12)
+        done = 2
+        for unit in first:
+            unit[3]()
+            steps[done]()
+            done += 1
+        first[0][4]()
+        assemble(small_v.reshape(count, 16, 128), count, vectors, up_vec)
+        vec_out[...] = vectors[:, :width]
+        up_out[...] = up_vec[:4, :width]
+        for m in moves:
+            m.finish()
+        loads = load_tokens(copies, whole[0], whole[1], flat, four)
+        for copy in loads:
+            copy.start()
+        for copy in loads:
+            copy.wait()
+        join_small(flat, four, large)
+        gain, shift = vectors[0:1, :width], vectors[4:5, :width]
+
+        def normed(start, size):
+            at = pl.ds(start, size)
+            hat, _ = norm_parts(flat[at, :].astype(F32))
+            flat[at, :] = (hat * gain + shift).astype(BF)
+
+        row_tiles(rows, 96, normed)
+        for unit in first[1:]:
+            unit[4]()
+        w_loads = [copies.here(lambda u=u: (full[0].at[u], w_v.at[u])) for u in range(panels)]
+        for copy in w_loads:
+            copy.start()
+        for u in range(panels):
+            w_loads[u].wait()
+            w = jnp.concatenate([w_v[u, c].reshape(width, wide) for c in range(2)], 1)
+            got = dot(flat[...], w, NN)
+            for c in range(2):
+                at = (c * panels + u) * wide
+                part = got[:, c * wide:(c + 1) * wide]
+                if at + wide <= width:
+                    part += vectors[6:7, at:at + wide]
+                elif at >= 2 * width:
+                    part += vectors[7:8, at - 2 * width:at - 2 * width + wide]
+                qkv[:, at:at + wide] = part.astype(BF)
+        out = [copies.here(lambda: (qkv, qkv_hbm)), copies.here(lambda: (flat, n1_hbm))]
+        for copy in out:
+            copy.start()
+        points = loop_points(steps[done:], 1)
+
+        def body(hp, carry):
+            attend_pair(hp, qkv, bias_l, bias_s, att, large, small,
+                        lambda index: run_point(points, hp, index, 1, H // 2))
+            return carry
+
+        lax.fori_loop(0, H // 2, body, 0)
+        run_rest(points, H // 2)
+        for copy in out:
+            copy.wait()
+
+    units = 1 + sum(a * b for a, b in cuts)
+    vm = pltpu.VMEM
+    return pl.pallas_call(
+        kernel,
+        out_shape=[jax.ShapeDtypeStruct(s, BF) for s in whole_shapes + full_shapes + [(rows, 3 * width), (rows, width), (rows, width)]]
+        + [jax.ShapeDtypeStruct((16, width), F32), jax.ShapeDtypeStruct((4, width), F32)],
+        in_specs=[ANY] * (na + 1 + nw) + [VMEM, VMEM],
+        out_specs=[ANY] * (na + nw + 2) + [VMEM] * 3,
+        scratch_shapes=[
+            vm((rows, width), BF), vm(whole_shapes[1], BF), vm(full_shapes[0], BF), vm((rows, 3 * width), BF),
+            vm((H, LEN_L, LEN_L), F32), vm((H, LEN_S, LEN_S), F32), vm((zs, 2, 2, 2, 16, 128), F32),
+            vm((16, width + 128), F32), vm((8, width + 128), F32),
+        ] + [s for w in shards for s in Gather.scratch(w.shape)]
+        + semaphores(3 * na + (zs + 2) * units + nw, na + nw + units + 4 * large + 1 + panels + 2),
+        compiler_params=pltpu.CompilerParams(collective_id=0, has_side_effects=True, vmem_limit_bytes=56 * MIB),
+        name="front",
+    )(*arrays, block, *shards, rows_l, rows_s)
 
 
 def gelu_parts(u):
@@ -963,33 +1114,51 @@
     return parts, [(n, large * LEN_L + n * LEN_S) for n in range(small)]
 
 
-def forward_tail(att, x_l, x_s, ct_l, ct_s, w_out, w_up, w_down, vectors, up_vec):
+def forward_tail(img_size, att, x_l, x_s, ct_l, ct_s, w_out, w_up, w_down, cut, vectors, up_vec):
     large, small = x_l.shape[0], x_s.shape[0]
     rows, width = att.shape
     chunks = up_vec.shape[0]
     half = rows // 2
-
-    def kernel(att_hbm, xl_hbm, xs_hbm, cl_hbm, cs_hbm, wo_hbm, wu_hbm, wd_hbm, vec, upv,
-               yl, ys, m_hbm, n2_hbm, e_hbm, g_hbm, dr_hbm, dy_hbm, sums,
-               att_v, flat, four, ct_four, wo, wu, wd, m_v, n2_v, r_v, e_v, g_v, acc, local):
-        copies = Copies(None, None, local)
+    direct = img_size is not None
+    down_shape = w_down.shape
+    bf = lambda *s: jax.ShapeDtypeStruct(s, BF)
+    more = [bf(*down_shape), bf(*x_l.shape), bf(*x_s.shape)] if direct else []
+
+    def kernel(att_hbm, xl_hbm, xs_hbm, cl_hbm, cs_hbm, wo_hbm, wu_hbm, wd_in, vec, upv, *refs):
+        outs, extra, scr = split_refs(refs, 9, len(more))
+        yl, ys, m_hbm, n2_hbm, e_hbm, g_hbm, dr_hbm, dy_hbm, sums = outs
+        att_v, flat, four, ct_four, wo, wu, wd, m_v, n2_v, e_v, g_v, acc = scr[:12]
+        copies = Copies(*scr[-3:])
         first = [copies.here(lambda: (att_hbm, att_v)), copies.here(lambda: (wo_hbm, wo))]
         first += load_tokens(copies, xl_hbm, xs_hbm, flat, four)
-        second = [copies.here(lambda: (wu_hbm, wu))]
-        third = [copies.here(lambda: (wd_hbm, wd))]
-        for copy in first + second + third:
+        second = copies.here(lambda: (wu_hbm, wu))
+        for copy in first + [second]:
             copy.start()
+        steps, moves = [], []
+        wd_hbm, ct = wd_in, (cl_hbm, cs_hbm)
+        if direct:
+            p = Place(img_size)
+            greet(p.partners())
+            wd_hbm, ct = extra[0], extra[1:]
+            gather = Gather(p, copies, None, wd_hbm, None, None, cut[1])
+            moves = [Move(p, copies, a, b, True) for a, b in zip((cl_hbm, cs_hbm), ct)]
+            units = gather.units(gather.over_yx)
+            for unit in units:
+                unit[0]()
+            for m in moves:
+                m.start()
+            steps = [unit[f] for f in range(1, 4) for unit in units]
         for copy in first:
             copy.wait()
         join_small(flat, four, large)
         g2, s1, s2, b2, bo, bd = (vec[i:i + 1, :] for i in (1, 2, 3, 5, 8, 9))
-
-        def project(i, carry):
-            at = pl.ds(pl.multiple_of(i * half, 16), half)
-            m_v[at, :] = dot(att_v[at, :], joined(wo, 0), NN)
-            return carry
-
-        lax.fori_loop(0, 2, project, 0)
+        points = {t + 1: step for t, step in enumerate(steps[3:])}
+        w = joined(wo, 0)
+        for i in range(2):
+            at = slice(i * half, (i + 1) * half)
+            m_v[at, :] = dot(att_v[at, :], w, NN)
+        for step in steps[:1]:
+            step()
 
         def middle(start, size):
             at = pl.ds(start, size)
@@ -999,77 +1168,69 @@
             n2_v[at, :] = (hat * g2 + b2).astype(BF)
 
         row_tiles(rows, 96, middle)
+        for step in steps[1:3]:
+            step()
         m_out = [copies.here(lambda: (m_v, m_hbm)), copies.here(lambda: (n2_v, n2_hbm))]
         for copy in m_out:
             copy.start()
-        ct = load_tokens(copies, cl_hbm, cs_hbm, flat, ct_four)
-        for copy in ct:
-            copy.start()
-        for copy in second + third:
-            copy.wait()
-
+        second.wait()
         out_at = copies.locals
-        copies.locals += 4
-
-        def out(f, slot):
-            return [
-                pltpu.make_async_copy(v.at[slot], hbm.at[f], local.at[out_at + 2 * slot + i])
-                for i, (v, hbm) in enumerate(((e_v, e_hbm), (g_v, g_hbm)))
-            ]
+        copies.locals += chunks
+
+        def out(f):
+            return pltpu.make_async_copy(
+                g_v.at[lax.rem(f, 2)], g_hbm.at[f], copies.local.at[out_at + f])
 
         def chunk(f, carry):
-            slot = lax.rem(f, 2)
+            run_point(points, f, 0, 1, chunks)
 
             @pl.when(f >= 2)
             def _():
-                for copy in out(f - 2, slot):
-                    copy.wait()
+                out(f - 2).wait()
 
             w1 = wu[lax.rem(f, 2), f // 2].reshape(width, width)
-            w2 = jnp.concatenate([wd[0, c, f].reshape(width, width // 2) for c in range(2)], 1)
             for i in range(2):
                 at = slice(i * half, (i + 1) * half)
                 u = dot(n2_v[at, :], w1, NN) + upv[pl.ds(f, 1), :]
                 e, g = gelu_parts(u)
-                e = e.astype(BF)
-                e_v[slot, at, :] = e
-                g_v[slot, at, :] = g.astype(BF)
-                r = dot(e, w2, NN)
-
-                @pl.when(f == 0)
-                def _():
-                    r_v[at, :] = r
-
-                @pl.when(f > 0)
-                def _():
-                    r_v[at, :] += r
-            for copy in out(f, slot):
-                copy.start()
+                e_v[at, columns(f * width, width)] = e.astype(BF)
+                g_v[lax.rem(f, 2), at, :] = g.astype(BF)
+            out(f).start()
             return carry
 
         lax.fori_loop(0, chunks, chunk, 0)
-        for copy in ct:
+        run_rest(points, chunks)
+        e_out = copies.here(lambda: (e_v, e_hbm))
+        e_out.start()
+        third = copies.here(lambda: (wd_hbm, wd))
+        third.start()
+        for m in moves:
+            m.finish()
+        loads = load_tokens(copies, *ct, flat, ct_four)
+        for copy in loads:
+            copy.start()
+        third.wait()
+        for copy in m_out:
+            copy.wait()
+        for copy in loads:
             copy.wait()
         join_small(flat, ct_four, large)
         for n in range(small):
             at = large * LEN_L + n * LEN_S + SIDE_S * SIDE_S // 16 * 16
             keep = lax.broadcasted_iota(jnp.int32, (32, 1), 0) < SIDE_S * SIDE_S % 16
             flat[at:at + 32, :] = jnp.where(keep, flat[at:at + 32, :].astype(F32), 0.0).astype(BF)
-        for copy in m_out:
-            copy.wait()
         acc[...] = jnp.zeros_like(acc)
-
-        def result(start, size):
-            at = pl.ds(start, size)
-            r = r_v[at, :] + bd
+        w2 = joined(wd, 0)
+        part = rows // 2
+        for i in range(2):
+            at = slice(i * part, (i + 1) * part)
+            r = dot(e_v[at, :], w2, NN) + bd
             dy = flat[at, :].astype(F32)
             dr = (s2 * dy).astype(BF)
             acc[0] += fold8(r * dy)
             acc[1] += fold8(dr.astype(F32))
             m_v[at, :] = m_v[at, :] + s2 * r
             n2_v[at, :] = dr
-
-        row_tiles(rows, 96, result)
         last = [copies.here(lambda: (n2_v, dr_hbm)), copies.here(lambda: (flat, dy_hbm))]
         for copy in last:
             copy.start()
@@ -1080,86 +1241,133 @@
         for i in range(2):
             sums[i:i + 1, :] = jnp.sum(acc[i], 0, keepdims=True)
         for f in (chunks - 2, chunks - 1):
-            for copy in out(f, f % 2):
-                copy.wait()
-        for copy in last:
+            out(f).wait()
+        for copy in last + [e_out]:
             copy.wait()
 
-    bf = lambda *s: jax.ShapeDtypeStruct(s, BF)
+    vm = pltpu.VMEM
+    flat = vm((rows, width), BF)
+    scratch = [
+        flat, flat, vm(x_s.shape, BF), vm(x_s.shape, BF), vm(w_out.shape, BF), vm(w_up.shape, BF),
+        vm(down_shape, BF), vm((rows, width), F32), flat, vm((rows, chunks * width), BF),
+        vm((2, rows, width), BF), vm((2, 8, width), F32),
+    ]
+    units = cut[0] * cut[1]
+    scratch += semaphores(6 + 3 * units, 12 + 8 * large + 2 + chunks + units + 3)
+    remote = dict(collective_id=3, has_side_effects=True) if direct else {}
     return pl.pallas_call(
         kernel,
         out_shape=[bf(*x_l.shape), bf(*x_s.shape), jax.ShapeDtypeStruct((rows, width), F32), bf(rows, width),
-                   bf(chunks, rows, width), bf(chunks, rows, width), bf(rows, width), bf(rows, width),
-                   jax.ShapeDtypeStruct((8, width), F32)],
+                   bf(rows, chunks * width), bf(chunks, rows, width), bf(rows, width), bf(rows, width),
+                   jax.ShapeDtypeStruct((8, width), F32)] + more,
         in_specs=[ANY] * 8 + [VMEM, VMEM],
-        out_specs=[VMEM, VMEM] + [ANY] * 6 + [VMEM],
-        scratch_shapes=[
-            pltpu.VMEM((rows, width), BF), pltpu.VMEM((rows, width), BF), pltpu.VMEM(x_s.shape, BF),
-            pltpu.VMEM(x_s.shape, BF), pltpu.VMEM(w_out.shape, BF), pltpu.VMEM(w_up.shape, BF),
-            pltpu.VMEM(w_down.shape, BF), pltpu.VMEM((rows, width), F32), pltpu.VMEM((rows, width), BF),
-            pltpu.VMEM((rows, width), F32), pltpu.VMEM((2, rows, width), BF), pltpu.VMEM((2, rows, width), BF),
-            pltpu.VMEM((2, 8, width), F32), pltpu.SemaphoreType.DMA((16 + 8 * large + 4,)),
-        ],
-        compiler_params=pltpu.CompilerParams(vmem_limit_bytes=60 * MIB),
+        out_specs=[VMEM, VMEM] + [ANY] * 6 + [VMEM] + [ANY] * len(more),
+        scratch_shapes=scratch,
+        input_output_aliases={7: 9} if direct else {},
+        compiler_params=pltpu.CompilerParams(vmem_limit_bytes=60 * MIB, **remote),
         name="forward_tail",
     )(att, x_l, x_s, ct_l, ct_s, w_out, w_up, w_down, vectors, up_vec)
 
 
-def backward_head(att, m, n2, e, g, dr, dy, w_out, w_up, w_down, vectors, sums_in):
+def backward_head(img_size, att, m, n2, e, g, dr, dy, w_out, w_up, w_down, cut, vectors, sums_in, wholes):
     rows, width = att.shape
-    chunks = e.shape[0]
+    chunks = g.shape[0]
     half = rows // 2
-
-    def kernel(att_hbm, m_hbm, n2_hbm, e_hbm, g_hbm, dr_hbm, dy_hbm, wo_hbm, wu_hbm, wd_hbm, vec, s_in,
-               go, gu, gd, dm_hbm, da_hbm, sums,
-               att_v, m_v, n2_v, nt_v, e_v, g_v, dr_v, dy_v, wo, wu, wd, dn, du_v, gd_v, gu_v, go_v, acc, up_acc, local):
-        copies = Copies(None, None, local)
-        pairs = [(dr_hbm, dr_v), (n2_hbm, n2_v), (wd_hbm, wd), (wu_hbm, wu),
-                 (m_hbm, m_v), (dy_hbm, dy_v), (att_hbm, att_v), (wo_hbm, wo)]
+    direct = img_size is not None
+    zs = img_size // 2 if direct else 0
+    nw = len(wholes)
+    k2, wide = w_down.shape[5:]
+    cols = w_down.shape[0] * 2 * wide
+    tall = k2 // cut
+
+    def kernel(*refs):
+        ins, wh, outs, blocks, scr = split_refs(refs, 12, nw, 6, nw)
+        att_hbm, m_hbm, n2_hbm, e_hbm, g_hbm, dr_hbm, dy_hbm, wo_hbm, wu_hbm, wd_hbm, vec, s_in = ins
+        go, gu, gd, dm_hbm, da_hbm, sums = outs
+        m_v, n2_v, nt_v, e_v, g_v, dr_v, wo, wu, wd, dn, du_v, gd_v, gu_v, go_v, acc, up_acc = scr[:16]
+        copies = Copies(*scr[-3:])
+        pairs = [(dr_hbm, dr_v), (n2_hbm, n2_v), (wd_hbm, wd), (wu_hbm, wu), (m_hbm, m_v), (wo_hbm, wo)]
         loads = [copies.here(lambda a=a, b=b: (a, b)) for a, b in pairs]
-        base = copies.locals
-        copies.locals += 8
-
-        def fetch(f, slot):
-            return [pltpu.make_async_copy(h.at[f], v.at[slot], local.at[base + 2 * slot + i])
-                    for i, (h, v) in enumerate(((e_hbm, e_v), (g_hbm, g_v)))]
-
-        def put(f, slot):
-            return [
-                pltpu.make_async_copy(gd_v.at[slot], gd.at[0, :, f], local.at[base + 4 + 2 * slot]),
-                pltpu.make_async_copy(gu_v.at[slot], gu.at[lax.rem(f, 2), f // 2], local.at[base + 5 + 2 * slot]),
-            ]
-
-        for copy in fetch(0, 0):
+        at_e = copies.locals
+        at_g = at_e + chunks
+        at_gu = at_g + chunks
+        copies.locals += 3 * chunks
+
+        def fetch_e(f):
+            return pltpu.make_async_copy(
+                e_hbm.at[:, columns(f * width, width)], e_v.at[lax.rem(f, 2)], copies.local.at[at_e + f])
+
+        def fetch_g(f):
+            return pltpu.make_async_copy(g_hbm.at[f], g_v.at[lax.rem(f, 2)], copies.local.at[at_g + f])
+
+        def put(f):
+            return pltpu.make_async_copy(
+                gu_v.at[lax.rem(f, 2)], gu.at[lax.rem(f, 2), f // 2], copies.local.at[at_gu + f])
+
+        loads[0].start()
+        fetch_e(0).start()
+        fetch_e(1).start()
+        for copy in loads[1:]:
             copy.start()
-        for copy in loads:
+        fetch_g(0).start()
+        moves, steps = [], []
+        if direct:
+            p = Place(img_size)
+            greet(p.partners())
+            moves = [Move(p, copies, a, b, False) for a, b in zip(wh, blocks)]
+            scatter = Scatter(p, copies, None, gd, scr[16:23], cut)
+            units = scatter.units()
+            steps = pipelined(units)
+        for m in moves:
+            m.start()
+        loads[0].wait()
+
+        def down(f, carry):
+            fetch_e(f).wait()
+            gd_v[...] = dot(e_v[lax.rem(f, 2)], dr_v[...], TN).astype(BF)
+            if direct:
+                for to, c in ((scatter.own, p.c), (scatter.stage, 1 - p.c)):
+                    got = gd_v[:, columns(c * wide, wide)].reshape(2, 2, cut, tall, wide)
+                    for r in range(cut):
+                        to[r, f] = got[:, :, r]
+            else:
+                for c in range(2):
+                    gd[0, c, f] = gd_v[:, c * wide:(c + 1) * wide].reshape(2, 2, k2, wide)
+
+            @pl.when(f + 2 < chunks)
+            def _():
+                fetch_e(f + 2).start()
+
+            return carry
+
+        lax.fori_loop(0, chunks, down, 0)
+        for step in steps[:1]:
+            step()
+        late = [copies.here(lambda: (att_hbm, e_v.at[0])), copies.here(lambda: (dy_hbm, e_v.at[1]))]
+        for copy in late:
             copy.start()
-        for copy in loads[:4]:
+        for copy in loads[1:4]:
             copy.wait()
         nt_v[...] = n2_v[...].T
+        dn[...] = jnp.zeros_like(dn)
         g2, s1, b2, bo = (vec[i:i + 1, :] for i in (1, 2, 5, 8))
+        points = loop_points(steps[1:], 1)
 
         def chunk(f, carry):
+            run_point(points, f, 0, 1, chunks)
             slot = lax.rem(f, 2)
-            for copy in fetch(f, slot):
-                copy.wait()
+            fetch_g(f).wait()
 
             @pl.when(f + 1 < chunks)
             def _():
-                for copy in fetch(f + 1, 1 - slot):
-                    copy.start()
+                fetch_g(f + 1).start()
 
             @pl.when(f >= 2)
             def _():
-                for copy in put(f - 2, slot):
-                    copy.wait()
-
-            w1 = wu[lax.rem(f, 2), f // 2].reshape(width, width)
-            w2 = jnp.concatenate([wd[0, c, f].reshape(width, width // 2) for c in range(2)], 1)
-            got = dot(e_v[slot], dr_v[...], TN).astype(BF)
-            for c in range(2):
-                part = got[:, c * (width // 2):(c + 1) * (width // 2)]
-                gd_v[slot, c] = part.reshape(gd_v.shape[2:])
+                put(f - 2).wait()
+
+            w1 = wu[slot, f // 2].reshape(width, width)
+            w2 = jnp.concatenate([wd[0, c, f].reshape(width, wide) for c in range(2)], 1)
             total = jnp.zeros((8, width), F32)
             for i in range(2):
                 at = slice(i * half, (i + 1) * half)
@@ -1167,25 +1375,19 @@
                 du = (de * g_v[slot, at, :].astype(F32)).astype(BF)
                 du_v[at, :] = du
                 total += fold8(du.astype(F32))
-                d = dot(du, w1, NT)
-
-                @pl.when(f == 0)
-                def _():
-                    dn[at, :] = d
-
-                @pl.when(f > 0)
-                def _():
-                    dn[at, :] += d
             up_acc[f] = total
+            dn[...] += dot(du_v[...], w1, NT)
             gu_v[slot] = dot(nt_v[...], du_v[...], NN).astype(BF).reshape(gu_v.shape[1:])
-            for copy in put(f, slot):
-                copy.start()
+            put(f).start()
             return carry
 
         lax.fori_loop(0, chunks, chunk, 0)
-        for copy in loads[4:]:
+        for copy in loads[4:] + late:
             copy.wait()
         acc[...] = jnp.zeros_like(acc)
+        run_some = [points[t] for t in sorted(points) if t >= chunks]
+        for step in run_some[:1]:
+            step()
 
         def norm(start, size):
             at = pl.ds(start, size)
@@ -1193,7 +1395,7 @@
             d = dn[at, :]
             acc[0] += fold8(d * hat)
             acc[1] += fold8(d)
-            dm = dy_v[at, :].astype(F32) + norm_back(d, hat, scale, g2)
+            dm = e_v[1, at, :].astype(F32) + norm_back(d, hat, scale, g2)
             da = (s1 * dm).astype(BF)
             acc[2] += fold8(da.astype(F32))
             m_v[at, :] = dm
@@ -1202,8 +1404,10 @@
         row_tiles(rows, 96, norm)
         out = [copies.here(lambda: (m_v, dm_hbm))]
         out[0].start()
+        for step in run_some[1:]:
+            step()
         w = joined(wo, 0)
-        got = dot(att_v[...], du_v[...], TN).astype(BF)
+        got = dot(e_v[0], du_v[...], TN).astype(BF)
         for c in range(2):
             go_v[c] = got[:, c * (width // 2):(c + 1) * (width // 2)].reshape(go_v.shape[1:])
         out.append(copies.here(lambda: (go_v, go.at[0])))
@@ -1211,7 +1415,7 @@
         for i in range(2):
             at = slice(i * half, (i + 1) * half)
             n2_v[at, :] = dot(du_v[at, :], w, NT).astype(BF)
-            a = dot(att_v[at, :], w, NN) + bo
+            a = dot(e_v[0, at, :], w, NN) + bo
             acc[3] += fold8(a * m_v[at, :])
         out.append(copies.here(lambda: (n2_v, da_hbm)))
         out[2].start()
@@ -1223,8 +1427,11 @@
         for f in range(chunks):
             sums[1, 2 + f:3 + f, :] = jnp.sum(up_acc[f], 0, keepdims=True)
         for f in (chunks - 2, chunks - 1):
-            for copy in put(f, f % 2):
-                copy.wait()
+            put(f).wait()
+        if direct:
+            scatter.end()
+        for copy in moves:
+            copy.finish()
         for copy in out:
             copy.wait()
 
@@ -1232,22 +1439,27 @@
     f32 = lambda *s: jax.ShapeDtypeStruct(s, F32)
     vm = pltpu.VMEM
     flat = vm((rows, width), BF)
+    scratch = [
+        vm((rows, width), F32), flat, vm((width, rows), BF), vm((2, rows, width), BF),
+        vm((2, rows, width), BF), flat, vm(w_out.shape, BF), vm(w_up.shape, BF), vm(w_down.shape, BF),
+        vm((rows, width), F32), flat, vm((width, width), BF), vm((2,) + w_up.shape[2:], BF),
+        vm(w_out.shape[1:], BF), vm((4, 8, width), F32), vm((chunks, 8, width), F32),
+    ]
+    if direct:
+        scratch += Scatter.scratch(zs, k2 // 2, cols, 1, cut, True)
+    scratch += semaphores(max(1, 3 * nw + Scatter.remotes(zs, 1, cut)), 6 + 3 * chunks + 2 + 3 + nw + 1)
+    remote = dict(collective_id=4, has_side_effects=True) if direct else {}
     return pl.pallas_call(
         kernel,
-        out_shape=[bf(*w_out.shape), bf(*w_up.shape), bf(*w_down.shape), f32(rows, width), bf(rows, width),
-                   f32(2, 8, width)],
-        in_specs=[ANY] * 10 + [VMEM, VMEM],
-        out_specs=[ANY] * 5 + [VMEM],
-        scratch_shapes=[
-            flat, vm((rows, width), F32), flat, vm((width, rows), BF), vm((2, rows, width), BF),
-            vm((2, rows, width), BF), flat, flat, vm(w_out.shape, BF), vm(w_up.shape, BF), vm(w_down.shape, BF),
-            vm((rows, width), F32), flat, vm((2, 2) + w_down.shape[3:], BF), vm((2,) + w_up.shape[2:], BF),
-            vm(w_out.shape[1:], BF), vm((4, 8, width), F32), vm((chunks, 8, width), F32),
-            pltpu.SemaphoreType.DMA((24,)),
-        ],
-        compiler_params=pltpu.CompilerParams(vmem_limit_bytes=60 * MIB),
+        out_shape=[bf(*w_out.shape), bf(*w_up.shape), f32(k2 // 2, cols) if direct else bf(*w_down.shape),
+                   f32(rows, width), bf(rows, width), f32(2, 8, width)]
+        + [bf(w.shape[0] * 4, *w.shape[2:]) for w in wholes],
+        in_specs=[ANY] * 10 + [VMEM, VMEM] + [ANY] * nw,
+        out_specs=[ANY, ANY, ANY if direct else VMEM, ANY, ANY, VMEM] + [ANY] * nw,
+        scratch_shapes=scratch,
+        compiler_params=pltpu.CompilerParams(vmem_limit_bytes=61 * MIB, **remote),
         name="backward_head",
-    )(att, m, n2, e, g, dr, dy, w_out, w_up, w_down, vectors, sums_in)
+    )(att, m, n2, e, g, dr, dy, w_out, w_up, w_down, vectors, sums_in, *wholes)
 
 
 def project_in(x_l, x_s, w_qkv, vectors, merged_bias):
@@ -1337,54 +1549,55 @@
     return split.transpose(2, 3, 4, 5, 1, 0, 6).reshape(rows, cols)
 
 
-CUTS = ((3, 1), (1, 1), (2, 1), (1, 3))
+CUTS = ((3, 1), (1, 1), (2, 3), (1, 3))
 
 
 def on_device(img_size, small_images, large_images, w_qkv, w_out, w_up, w_down, gains, biases, up_bias,
               small_table, large_table, small_cotangent, large_cotangent):
     width = small_images.shape[2]
     axes = ("img", "rows")
-    shards = [w_qkv, w_out, w_up, w_down]
     own = gains.shape[0]
     own_up = up_bias.shape[0]
-    own_len = 10 * own + own_up
-    block = jnp.concatenate([gains.T.reshape(-1), biases.T.reshape(-1), up_bias])
-    block = jnp.pad(block, (0, 1024 - own_len)).reshape(8, 128)
-    arrays = [large_images, small_images, large_cotangent, small_cotangent]
+    rows_l = table_rows(large_table, SIDE_L, 47, WIDE_L)
+    rows_s = table_rows(small_table, SIDE_S, 29, WIDE_S)
     direct = own % 8 == 0
     if direct:
-        got = front(img_size, arrays, block, shards, CUTS)
-        full = got[5:]
+        block = jnp.concatenate([gains.T, biases.T], 0)
+        block = jnp.pad(block, ((0, 0), (0, own_up - own)))
+        block = jnp.pad(jnp.concatenate([block, up_bias[None]], 0), ((0, 5), (0, 128 - own_up)))
+        large_x, small_x, qkv_w, up_w, out_w, down_w, qkv, n1, attended, vectors, up_vec = front(
+            img_size, [large_images, small_images], block, [w_qkv, w_up, w_out, w_down],
+            [CUTS[i] for i in (0, 2, 1, 3)], [(0, 3), (0,)], rows_l, rows_s)
+        large, small = large_x.shape[0], small_x.shape[0]
+        large_y, small_y, m, n2, e, g, dr, dy, sums, down_w, _, _ = forward_tail(
+            img_size, attended, large_x, small_x, large_cotangent, small_cotangent, out_w, up_w, down_w, CUTS[3],
+            vectors, up_vec)
+        grad_out, grad_up, own_down, dm, d_att, sums, large_out, small_out = backward_head(
+            img_size, attended, m, n2, e, g, dr, dy, out_w, up_w, down_w, CUTS[3][1], vectors, sums,
+            [large_y, small_y])
+        df, large_sums, small_sums, own_out, own_up_w = attention_back(
+            img_size, qkv, d_att, rows_l, rows_s, [grad_out, grad_up], [1, 1], [], large, small, 3)
+        large_grad, small_grad, own_qkv, sums, large_sums, small_sums = projection_back(
+            img_size, df, dm, n1, large_x, small_x, qkv_w, vectors, sums, [large_sums, small_sums], large, small)
     else:
-        got = [to_images(a) for a in arrays] + [lax.all_gather(block, axes, axis=0)]
-        full = [to_panels(lax.all_gather(s.astype(BF), axes, axis=0, tiled=True), c[0]) for s, c in zip(shards, CUTS)]
-    large_x, small_x, large_ct, small_ct = got[:4]
-    blocks = got[4].reshape(-1, 1024).astype(BF).astype(F32)
-    vectors = jnp.swapaxes(blocks[:, :10 * own].reshape(-1, 10, own), 0, 1).reshape(10, width)
-    merged_bias = jnp.concatenate([vectors[6:7], jnp.zeros((1, width), F32), vectors[7:8]], 1)
-    up_vec = blocks[:, 10 * own:own_len].reshape(-1, width)
-    vectors = jnp.pad(vectors, ((0, 6), (0, 0)))
-    qkv_w, out_w, up_w, down_w = full
-
-    large, small = large_x.shape[0], small_x.shape[0]
-    rows_l = table_rows(large_table, SIDE_L, 47, WIDE_L)
-    rows_s = table_rows(small_table, SIDE_S, 29, WIDE_S)
-
-    qkv = project_in(large_x, small_x, qkv_w, vectors, merged_bias)
-    attended = attend(qkv, rows_l, rows_s, large, small)
-    large_y, small_y, m, n2, e, g, dr, dy, sums = forward_tail(
-        attended, large_x, small_x, large_ct, small_ct, out_w, up_w, down_w, vectors, up_vec)
-    grad_out, grad_up, grad_down, dm, d_att, sums = backward_head(
-        attended, m, n2, e, g, dr, dy, out_w, up_w, down_w, vectors, sums)
-    if direct:
-        df, large_sums, small_sums, *more = attention_back(
-            img_size, qkv, d_att, rows_l, rows_s, [grad_down, grad_out, grad_up], [CUTS[i][1] for i in (3, 1, 2)],
-            [large_y, small_y], large, small, 1)
-        own_down, own_out, own_up_w, large_out, small_out = more
-        large_grad, small_grad, own_qkv, sums, large_sums, small_sums = projection_back(
-            img_size, df, dm, large_x, small_x, qkv_w, vectors, sums, [large_sums, small_sums], large, small)
-    else:
-        df, large_sums, small_sums = attention_back(img_size, qkv, d_att, rows_l, rows_s, [], [], [], large, small, 1)
+        large_x, small_x, large_ct, small_ct = [
+            to_images(a) for a in (large_images, small_images, large_cotangent, small_cotangent)]
+        large, small = large_x.shape[0], small_x.shape[0]
+        qkv_w, out_w, up_w, down_w = [
+            to_panels(lax.all_gather(s.astype(BF), axes, axis=0, tiled=True), c[0])
+            for s, c in zip((w_qkv, w_out, w_up, w_down), CUTS)]
+        vectors = lax.all_gather(jnp.concatenate([gains, biases], 1).astype(BF), axes, axis=0, tiled=True)
+        vectors = jnp.pad(vectors.astype(F32).T, ((0, 6), (0, 0)))
+        up_vec = lax.all_gather(up_bias.astype(BF), axes, axis=0, tiled=True).astype(F32).reshape(-1, width)
+        merged_bias = jnp.concatenate([vectors[6:7], jnp.zeros((1, width), F32), vectors[7:8]], 1)
+        qkv = project_in(large_x, small_x, qkv_w, vectors, merged_bias)
+        attended = attend(qkv, rows_l, rows_s, large, small)
+        large_y, small_y, m, n2, e, g, dr, dy, sums = forward_tail(
+            None, attended, large_x, small_x, large_ct, small_ct, out_w, up_w, down_w, (1, 1), vectors, up_vec)
+        grad_out, grad_up, grad_down, dm, d_att, sums = backward_head(
+            None, attended, m, n2, e, g, dr, dy, out_w, up_w, down_w, 1, vectors, sums, [])
+        df, large_sums, small_sums = attention_back(
+            img_size, qkv, d_att, rows_l, rows_s, [], [], [], large, small, 1)
         split_at = large * LEN_L
         tokens = jnp.concatenate([large_x.reshape(-1, width), small_x.reshape(-1, width)], 0).astype(F32)
         normed, pull = jax.vjp(layer_norm, tokens, vectors[0], vectors[4])

time: 524 us -> 399 us (0.76)
  Pallas kernels: 480 us -> 369 us
  local copies, waits for them, and re-layouts: 36.7 us -> 21.9 us
    pallas_call x4 -> x2, Pallas kernels: 236 us -> 170 us  [the longest x1 107 us: front(): pl.pallas_call(kernel, out_shape=[jax.ShapeDtypeStruct(s, BF) for s in wh...]
    pallas_call x1, Pallas kernels: 115 us -> 74.1 us  [attention_back(): pl.pallas_call(kernel, out_shape=[jax.ShapeDtypeStruct(qkv.shape, BF), ja...]
    unnamed x70 -> x34, local copies, waits for them, and re-layouts: 20.4 us -> 6.87 us
    pallas_call x1, Pallas kernels: 77.8 us -> 67.2 us  [projection_back(): pl.pallas_call(kernel, out_shape=[jax.ShapeDtypeStruct((4 * a.shape[0],)...]
    pallas_call x1, Pallas kernels: 51.1 us -> 57.4 us  [forward_tail(): pl.pallas_call(kernel, out_shape=[bf(*x_l.shape), bf(*x_s.shape), jax.Sha...]
where the time goes in v3:
time: 399 us; the launch traced here: 394 us
  Pallas kernels  369 us (92%)
  local copies, waits for them, and re-layouts  21.9 us (5%)
    pallas_call x1, Pallas kernels, front(): pl.pallas_call(kernel, out_shape=[jax.ShapeDtypeStruct(s, BF) for s in wh...  107 us
    pallas_call x1, Pallas kernels, attention_back(): pl.pallas_call(kernel, out_shape=[jax.ShapeDtypeStruct(qkv.shape, BF), ja...  74.1 us
    pallas_call x1, Pallas kernels, projection_back(): pl.pallas_call(kernel, out_shape=[jax.ShapeDtypeStruct((4 * a.shape[0],)...  67.2 us
    pallas_call x1, Pallas kernels, backward_head(): pl.pallas_call(kernel, out_shape=[bf(*w_out.shape), bf(*w_up.shape), f32(...  63.5 us
    pallas_call x1, Pallas kernels, forward_tail(): pl.pallas_call(kernel, out_shape=[bf(*x_l.shape), bf(*x_s.shape), jax.Sha...  57.4 us

profile of v3, /device:TPU:0, one launch (start us, length us, event | category | flops | bytes accessed | tf_op | source)
XLA Modules:
  0.0 394.2 jit_solution(1963377078439884711)
XLA Ops:
  0.6 1.0 reshape.86
  1.7 0.1 fusion.3
  1.8 0.2 slice.166
  2.1 0.0 copy-start.7
  2.1 0.2 reshape.105
  2.3 0.1 pad_slice_fusion
  2.4 0.1 fusion.4
  2.5 0.2 slice.162
  2.8 0.2 reshape.104
  3.0 0.1 pad_slice_fusion.1
  3.2 0.1 pad_maximum_fusion.10
  3.3 0.2 reshape.103
  3.5 0.1 pad_slice_fusion.2
  3.7 0.2 reshape.102
  3.9 0.1 pad_slice_fusion.3
  4.0 0.1 pad_maximum_fusion.8
  4.2 0.9 concatenate.65.refs_8_.refs_3_
  5.0 0.2 reshape.81
  5.2 0.1 fusion.2
  5.4 0.3 slice.147
  5.7 0.2 reshape.100
  5.9 0.2 slice.188
  6.1 0.1 fusion.1
  6.3 0.3 slice.151
  6.6 0.0 copy-start.10
  6.6 0.0 copy-start.11
  6.6 0.0 copy-start.12
  6.6 0.2 reshape.101
  6.9 0.2 slice.191
  7.1 0.1 pad_maximum_fusion.5
  7.2 0.2 reshape.98
  7.5 0.2 slice.182
  7.7 0.2 reshape.99
  7.9 0.2 slice.185
  8.1 0.1 pad_maximum_fusion.3
  8.3 1.4 concatenate.59.refs_7_.refs_2_
  9.7 0.6 select_maximum_fusion.refs_2_
  10.3 106.9 %front.1 = (bf16[2,4,144,768]{3,2,1,0:T(8,128)(2,1)}, bf16[1,4,56,768]{3,2,1,0:T(8,128)(2,1)}, bf16[3,2,4,2,2,48,384]{6,5,4,3,2,1,0:T(8,128)(2,1)}, bf16[2,2,4,2...) custom-call(bf16[8,144,768]{2,1,0:T(8,128)(2,1)} %refs_0_.1, ...), custom_call_target="tpu_custom_call" | custom-call | tf_op jit(solution)/shard_map/front/pallas_call | solution.py:1081
  117.2 57.4 %forward_tail.1 = (bf16[2,4,144,768]{3,2,1,0:T(8,128)(2,1)}, bf16[1,4,56,768]{3,2,1,0:T(8,128)(2,1)}, f32[1376,768]{1,0:T(8,128)}, bf16[1376,768]{1,0:T(8,128)(2...) custom-call(bf16[1376,768]{1,0:T(8,128)(2,1)} %get-tuple-element.53., ...), custom_call_target="tpu_custom_call", output_to_operand_aliasing={{9}: (7, {})} | custom-call | tf_op jit(solution)/shard_map/forward_tail/pallas_call | solution.py:1258
  174.6 63.5 %backward_head.1 = (bf16[1,2,4,2,2,48,384]{6,5,4,3,2,1,0:T(8,128)(2,1)}, bf16[2,2,4,2,2,48,768]{6,5,4,3,2,1,0:T(8,128)(2,1)}, f32[96,768]{1,0:T(8,128)}, f32[137...) custom-call(bf16[1376,768]{1,0:T(8,128)(2,1)} %get-tuple-element.53., ...), custom_call_target="tpu_custom_call" | custom-call | tf_op jit(solution)/shard_map/backward_head/pallas_call | solution.py:1452
  238.1 74.1 %attention_back.1 = (bf16[1376,2304]{1,0:T(8,128)(2,1)}, f32[2,16,1152]{2,1,0:T(8,128)}, f32[2,16,512]{2,1,0:T(8,128)}, f32[24,768]{1,0:T(8,128)}, f32[24,3072]{1,0:T(8,128)}) custom-call(bf16[1376,2304]{1,0:T(8,128)(2,1)} %get-tuple-element.73.refs_0_, bf16[1376,768]{1,0:T(8,128)(2,1)} %get-tuple-element.74.refs_1_, ...), custom_call_target="tpu_custom_call" | custom-call | tf_op jit(solution)/shard_map/attention_back/pallas_call | solution.py:721
  312.3 67.2 %projection_back.1 = (bf16[8,144,768]{2,1,0:T(8,128)(2,1)}, bf16[4,56,768]{2,1,0:T(8,128)(2,1)}, f32[24,2304]{1,0:T(8,128)}, f32[2,8,768]{2,1,0:T(8,128)}, f32[2...) custom-call(bf16[1376,2304]{1,0:T(8,128)(2,1)} %get-tuple-element.77.refs_0_, f32[1376,768]{1,0:T(8,128)} %get-tuple-element.78.refs_1_, ...), custom_call_target="tpu_custom_call" | custom-call | tf_op jit(solution)/shard_map/projection_back/pallas_call | solution.py:911
  379.5 1.3 reshape.96
  380.9 0.1 pad_maximum_fusion
  381.1 0.8 reshape.97
  382.0 0.1 slice.205
  382.1 0.4 reshape.94
  382.5 0.1 slice_maximum_fusion
  382.7 0.1 fusion
  382.8 0.8 reshape.95
  383.6 0.7 slice.204
  384.3 0.6 dynamic_slice.7
  384.9 0.8 dynamic-slice_bitcast_fusion
  385.7 0.6 slice.203
  386.3 0.6 slice.202
  386.9 0.7 copy.54
  387.6 1.2 copy.55
  388.8 0.7 copy.56
  389.6 0.2 copy-done.1
  389.8 1.2 copy.57
  391.0 0.7 copy.58
  391.7 0.6 copy.59
  392.3 0.7 copy.60
  393.0 0.7 copy.61
  (50 shorter events, 0.6 us)
Async XLA Ops:
  2.1 3.0 copy-start.7
  6.6 3.1 copy-start.10
  6.6 3.0 copy-start.11
  6.6 3.0 copy-start.12
  379.5 2.4 copy-start.9
  380.9 6.0 %copy-start.2 = (bf16[4,56,768]{2,1,0:T(8,128)(2,1)S(1)}, bf16[4,56,768]{2,1,0:T(8,128)(2,1)}, u32[]{:S(2)}) copy-start(bf16[4,56,768]{2,1,0:T(8,128)(2,1)} %get-tuple-element.122) | copy-start | bytes 1032196
  381.1 6.5 %copy-start = (bf16[8,144,768]{2,1,0:T(8,128)(2,1)S(1)}, bf16[8,144,768]{2,1,0:T(8,128)(2,1)}, u32[]{:S(2)}) copy-start(bf16[8,144,768]{2,1,0:T(8,128)(2,1)} %get-tuple-element.123) | copy-start | bytes 5308420
  386.9 1.9 copy-start.3
  387.6 2.1 copy-start.1
  388.8 2.1 copy-start.6
  389.8 1.9 copy-start.8
  389.8 2.5 copy-start.5
  389.8 3.3 copy-start.4
